TPU v7x, 512 devices: a whole 4x8x8 slice. The times are simulated.
512 devices in a mesh: row: 16 (over y, x_lo), col: 32 (over x_hi, z, core).
Axes of the slice: x: 4 (x_hi: 2, x_lo: 2; x = x_hi * 2 + x_lo), y: 8, z: 8, core: 2. Of those that a mesh axis runs over, the one named last changes fastest.
Arguments:
- tokens: float32 [128, 512, 128], P('row', 'col'), may hold values from -6 to 6
- cotangent: float32 [128, 512, 128], P('row', 'col'), may hold values from -6 to 6
- conv_weight: float32 [3, 3, 128], replicated, may hold values from -1 to 1
- w_query: float32 [128, 128], replicated, may hold values from -8 to 8, as said below
- w_key: float32 [128, 128], replicated, may hold values from -0.5 to 0.5
- w_value: float32 [128, 128], replicated, may hold values from -0.5 to 0.5
- w_out: float32 [128, 128], replicated, may hold values from -0.5 to 0.5
Outputs:
- output: float32 [128, 512, 128], P('row', 'col')
- d_tokens: float32 [128, 512, 128], P('row', 'col')
- g_conv: float32 [3, 3, 128], replicated
- g_query: float32 [128, 128], replicated
- g_key: float32 [128, 128], replicated
- g_value: float32 [128, 128], replicated
- g_out: float32 [128, 128], replicated
Inputs may be any that keep to these rules, and one draw needn't show every extreme that they name: `w_query`: A real matrix of independent entries.
All inputs are finite; a program needn't handle non-finite values.
Results may differ from a plain program's by a relative error of at most 0.0003.
Values sent between devices are 32-bit elements; how exact they have to be, the bound alone decides.
No kernel may reach another device: no remote copies, remote signals or barrier semaphores. Data moves between devices by JAX's collectives and lax.ppermute only.
A program may use at most 64 MiB of HBM per device.

v0:
```python
import jax
import jax.numpy as jnp
from jax import lax
from jax.sharding import PartitionSpec as P

HEADS = 2
POOL = 32


def with_halo(value, sides, width):
    for axis, dim in sides:
        peers, length = (lax.axis_size(axis), value.shape[dim])
        up = [(i, (i + 1) % peers) for i in range(peers - 1)]
        down = [(j, i) for i, j in up]
        last = lax.slice_in_dim(value, length - width, length, axis=dim)
        first = lax.slice_in_dim(value, 0, width, axis=dim)
        before = lax.ppermute(last, axis, up)
        after = lax.ppermute(first, axis, down)
        value = jnp.concatenate([before, value, after], axis=dim)
    return value


def product(left, right):
    return jnp.dot(left, right, precision=lax.Precision.HIGHEST, preferred_element_type=jnp.float32)


def normalize(values_in):
    average = jnp.mean(values_in, -1, keepdims=True)
    centered = values_in - average
    inv_std = lax.rsqrt(jnp.mean(centered * centered, -1, keepdims=True) + 1e-06)
    return (centered * inv_std, inv_std)


def norm_back(gradient, normed, inv_std):
    return inv_std * (
        gradient
        - jnp.mean(gradient, -1, keepdims=True)
        - normed * jnp.mean(gradient * normed, -1, keepdims=True)
    )


def conv_apply(tokens, padded, conv_weight):
    tile_rows, tile_cols = (tokens.shape[0], tokens.shape[1])
    total = tokens
    for offset_r in range(3):
        for offset_c in range(3):
            total = (
                total
                + conv_weight[offset_r, offset_c]
                * padded[offset_r : offset_r + tile_rows, offset_c : offset_c + tile_cols]
            )
    return total


def conv_back(gradient, padded_grad, conv_weight):
    tile_rows, tile_cols = (gradient.shape[0], gradient.shape[1])
    total = gradient
    for offset_r in range(3):
        for offset_c in range(3):
            total = (
                total
                + conv_weight[offset_r, offset_c]
                * padded_grad[
                    2 - offset_r : 2 - offset_r + tile_rows, 2 - offset_c : 2 - offset_c + tile_cols
                ]
            )
    return total


def conv_weight_grad(gradient, padded):
    tile_rows, tile_cols = (gradient.shape[0], gradient.shape[1])
    outer = []
    for offset_r in range(3):
        inner = []
        for offset_c in range(3):
            inner.append(
                jnp.sum(
                    padded[offset_r : offset_r + tile_rows, offset_c : offset_c + tile_cols]
                    * gradient,
                    axis=(0, 1),
                )
            )
        outer.append(jnp.stack(inner))
    return jnp.stack(outer)


def attend(normed_blk, grad_blk, w_query, w_out, key_rows, values):
    channels = key_rows.shape[1]
    head_width = channels // HEADS
    score_scale = head_width ** (-0.5)
    query_rows = product(normed_blk, w_query)
    d_att = product(grad_blk, w_out.T)
    att_parts, dq_parts, dk_parts, dv_parts = ([], [], [], [])
    for head_index in range(HEADS):
        low = head_index * head_width
        query_h = query_rows[:, low : low + head_width]
        key_h = key_rows[:, low : low + head_width]
        value_h = values[:, low : low + head_width]
        d_out_h = d_att[:, low : low + head_width]
        scores = product(query_h, key_h.T) * score_scale
        highest = jnp.max(scores, -1, keepdims=True)
        weights = jnp.exp(scores - highest)
        probs = weights / jnp.sum(weights, -1, keepdims=True)
        att_parts.append(product(probs, value_h))
        d_probs = product(d_out_h, value_h.T)
        d_scores = probs * (d_probs - jnp.sum(d_probs * probs, -1, keepdims=True))
        dq_parts.append(product(d_scores, key_h) * score_scale)
        dk_parts.append(product(d_scores.T, query_h) * score_scale)
        dv_parts.append(product(probs.T, d_out_h))
    return (
        jnp.concatenate(att_parts, 1),
        jnp.concatenate(dq_parts, 1),
        jnp.concatenate(dk_parts, 1),
        jnp.concatenate(dv_parts, 1),
    )


def body(tokens, cotangent, conv_weight, w_query, w_key, w_value, w_out):
    tile_rows, tile_cols, channels = tokens.shape
    row_count = lax.axis_size("row")
    col_count = lax.axis_size("col")
    padded = with_halo(tokens, (("row", 0), ("col", 1)), 1)
    mixed_tokens = conv_apply(tokens, padded, conv_weight)
    normed, inv_std = normalize(mixed_tokens)
    win_r = tile_rows * row_count // POOL
    win_c = tile_cols * col_count // POOL
    cells_r = tile_rows // win_r
    cells_c = tile_cols // win_c
    pooled = (
        normed.reshape(cells_r, win_r, cells_c, win_c, channels)
        .mean(axis=(1, 3))
        .reshape(cells_r * cells_c, channels)
    )
    pooled_n, pooled_inv = normalize(pooled)
    all_pooled = lax.all_gather(pooled_n, ("row", "col"), axis=0, tiled=True)
    key_rows = product(all_pooled, w_key)
    values = product(all_pooled, w_value)
    tok_count = tile_rows * tile_cols
    block_rows = min(512, tok_count)
    flat_n = normed.reshape(tok_count // block_rows, block_rows, channels)
    flat_g = cotangent.reshape(tok_count // block_rows, block_rows, channels)

    def block_step(totals, inputs):
        d_keys, d_values, grad_out, grad_query = totals
        normed_blk, grad_blk = inputs
        att, d_query, part_k, part_v = attend(
            normed_blk, grad_blk, w_query, w_out, key_rows, values
        )
        totals = (
            d_keys + part_k,
            d_values + part_v,
            grad_out + product(att.T, grad_blk),
            grad_query + product(normed_blk.T, d_query),
        )
        return (totals, (product(att, w_out), product(d_query, w_query.T)))

    key_count = all_pooled.shape[0]
    empty_keys = jnp.zeros((key_count, channels), jnp.float32)
    empty_square = jnp.zeros((channels, channels), jnp.float32)
    totals, (att_out, d_normed) = lax.scan(
        block_step, (empty_keys, empty_keys, empty_square, empty_square), (flat_n, flat_g)
    )
    d_keys, d_values, grad_out, grad_query = totals
    output = mixed_tokens + att_out.reshape(tile_rows, tile_cols, channels)
    own_keys, own_values = (
        lax.psum_scatter(d_keys, ("row", "col"), scatter_dimension=0, tiled=True),
        lax.psum_scatter(d_values, ("row", "col"), scatter_dimension=0, tiled=True),
    )
    grad_key = product(pooled_n.T, own_keys)
    grad_value = product(pooled_n.T, own_values)
    pooled_grad = product(own_keys, w_key.T) + product(own_values, w_value.T)
    d_pooled = norm_back(pooled_grad, pooled_n, pooled_inv)
    spread = d_pooled.reshape(cells_r, 1, cells_c, 1, channels) / float(win_r * win_c)
    spread = jnp.broadcast_to(spread, (cells_r, win_r, cells_c, win_c, channels)).reshape(
        tile_rows, tile_cols, channels
    )
    d_normed = d_normed.reshape(tile_rows, tile_cols, channels) + spread
    d_mixed = cotangent + norm_back(d_normed, normed, inv_std)
    padded_grad = with_halo(d_mixed, (("row", 0), ("col", 1)), 1)
    d_tokens = conv_back(d_mixed, padded_grad, conv_weight)
    grad_conv = conv_weight_grad(d_mixed, padded)
    sum_conv, sum_query, sum_key, sum_value, sum_out = lax.psum(
        (grad_conv, grad_query, grad_key, grad_value, grad_out), ("row", "col")
    )
    root = float(tok_count * row_count * col_count) ** (-0.5)
    return (
        output,
        d_tokens,
        sum_conv * root,
        sum_query * root,
        sum_key / float(POOL),
        sum_value / float(POOL),
        sum_out * root,
    )


def solution(mesh):
    in_specs = (P("row", "col", None), P("row", "col", None), P(), P(), P(), P(), P())
    out_specs = (P("row", "col", None), P("row", "col", None), P(), P(), P(), P(), P())
    return jax.shard_map(body, mesh=mesh, in_specs=in_specs, out_specs=out_specs, check_vma=False)
```

profile of v0, /device:TPU:1, one launch (start us, length us, event | category | flops | bytes accessed | tf_op | source)
XLA Modules:
  0.0 1385.1 jit_solution(9382637407955200121)
XLA Ops:
  7.9 1.3 collective-permute-start.1
  9.2 4.6 collective-permute-start
  13.8 1.2 fusion.80
  15.1 5.5 collective-permute-start.2
  20.6 4.7 collective-permute-start.3
  27.0 689.3 %all-gather = f32[512,2,128]{2,1,0:T(2,128)S(1)} all-gather(f32[1,2,128]{2,1,0:T(2,128)S(1)} %fusion.97), channel_id=1, replica_groups=mesh['row'=16,'col'=32] {'row','col'}, dimensions={0}, use_global_device_ids=true | all-gather | bytes 525312 | tf_op jit(solution)/shard_map/all_gather | solution.py:135
  719.2 0.8 fusion.6
  721.3 0.8 convolution_multiply_fusion.4
  726.3 1.3 pad_maximum_fusion
  728.5 0.8 fusion.41
  730.2 0.8 convolution_multiply_fusion.5
  731.1 0.9 fusion.39
  732.0 259.9 %all-reduce.9.cloned.1.call-done = (f32[1024,128]{0,1:T(8,128)}, f32[1024,128]{0,1:T(8,128)}) async-done(((f32[1024,128]{0,1:T(8,128)}, f32[1024,128]{0,1:T(8,128)}), (f32[1024,128]{0,1:T(8,128)}, f32[1024,128]{0,1:T(8,128)})) %all-reduce.9.cloned.1.call-update) | async-done | bytes 1048592
  991.9 1.1 fusion.37
  993.0 1.9 fusion.35
  994.9 1.8 fusion.32
  996.7 1.3 fusion.69
  998.9 2.6 collective-permute-start.4
  1001.5 1.3 collective-permute-start.5
  1002.9 98.4 %psum.35 = f32[3,3,128]{2,1,0:T(4,128)S(1)} all-reduce(f32[3,3,128]{2,1,0:T(4,128)S(1)} %pad_maximum_fusion.15), channel_id=1, replica_groups=mesh['row'=16,'col'=32] {'row','col'}, use_global_device_ids=true, to_apply=%region_27.28 | all-reduce | flops 1152 | bytes 9216 | tf_op jit(solution)/shard_map/psum | solution.py:182
  1101.4 2.6 collective-permute-start.6
  1104.0 3.0 collective-permute-start.7
  1108.4 266.0 %all-reduce.7.cloned.1.call-done = (f32[128,128]{1,0:T(8,128)}, f32[128,128]{1,0:T(8,128)}, f32[128,128]{1,0:T(8,128)}, f32[128,128]{1,0:T(8,128)}) async-done(((f32[128,128]{1,0:T(8,128)}, f32[128,128]{1,0:T(8,128)}, f32[128,128]{1,0:T(8,128)}, f32[128,128]{1,0:T(8,128)}), (f32[128,128]{1,0:T(8,128)}, f32[128,128]{1,0:T(8,128)}, f32[128,128]{1,0:T(8,128)}, ...) | async-done | bytes 262160 | tf_op jit(solution)/shard_map/psum | solution.py:182
  1374.4 1.5 broadcast_multiply_fusion.3
  (87 shorter events, 17.2 us)
Async XLA Ops:
  7.2 709.1 %copy-start = (f32[128,128]{1,0:T(8,128)S(1)}, f32[128,128]{1,0:T(8,128)}, u32[]{:S(2)}) copy-start(f32[128,128]{1,0:T(8,128)} %param.12) | copy-start | bytes 196612
  7.2 984.7 %all-reduce.9.cloned.1.call-start = ((), (), s32[]{:S(2)}) async-start(), calls=%async_computation.1 | async-start | bytes 2097152
  7.9 7.1 collective-permute-start.1
  9.2 5.8 collective-permute-start
  13.8 1.2 copy-start.1
  15.1 10.2 copy-start.9
  15.1 10.2 collective-permute-start.2
  20.6 5.5 collective-permute-start.3
  716.2 0.8 copy-start.5
  717.1 0.8 copy-start.4
  727.6 0.8 copy-start.2
  727.7 1.6 copy-start.3
  727.7 646.7 %all-reduce.7.cloned.1.call-start = ((), (), s32[]{:S(2)}) async-start(), calls=%async_computation | async-start | bytes 524288 | tf_op jit(solution)/shard_map/psum | solution.py:182
  998.9 102.5 %collective-permute-start.4 = (f32[1,16,128]{2,1,0:T(8,128)S(1)}, f32[1,16,128]{2,1,0:T(8,128)S(1)}, u32[]{:S(2)}, u32[]{:S(2)}) collective-permute-start(f32[1,16,128]{2,1,0:T(8,128)S(1)} %get-tuple-element.80), channel_id=1, source_target_pairs={{0,32},{32,64},{64,96},{96,128},{128,160},{160,192},{192,224},{224... | collective-permute-start | bytes 24584 | tf_op jit(solution)/shard_map/ppermute | solution.py:17
  1001.5 99.8 %collective-permute-start.5 = (f32[1,16,128]{2,1,0:T(8,128)S(1)}, f32[1,16,128]{2,1,0:T(8,128)S(1)}, u32[]{:S(2)}, u32[]{:S(2)}) collective-permute-start(f32[1,16,128]{2,1,0:T(8,128)S(1)} %get-tuple-element.81), channel_id=1, source_target_pairs={{32,0},{64,32},{96,64},{128,96},{160,128},{192,160},{224,192},{256... | collective-permute-start | bytes 24584 | tf_op jit(solution)/shard_map/ppermute | solution.py:18
  1101.4 6.2 collective-permute-start.6
  1104.0 3.7 collective-permute-start.7
  1374.4 1.5 copy-start.8
  1375.9 0.9 copy-start.7
  1376.8 0.9 copy-start.6
Sparse Core Ops, SparseCore 0:
  727.8 264.0 all-reduce.8
  1107.7 266.6 all-reduce.6
where the time goes:
time: 1390 us
  blocking collectives  788 us (57%)
  waiting for transfers between devices  527 us (38%)
  starting transfers between devices  25.6 us (2%)
  matrix products  19.7 us (1%)
  between operations  14.4 us (1%)
    all_gather x1, blocking collectives, body(): all_pooled = lax.all_gather(pooled_n, ('row', 'col'), axis=0, tiled=True)  689 us
    psum x1, waiting for transfers between devices, body(): lax.psum((grad_conv, grad_query, grad_key, grad_value, grad_out), ('row',...  266 us
    unnamed x3, waiting for transfers between devices  260 us
    psum x1, blocking collectives, body(): lax.psum((grad_conv, grad_query, grad_key, grad_value, grad_out), ('row',...  98.4 us
  transfers between devices with their start and end apart: 10, of which 4 were waited for; matrix products, arithmetic and copies ran while one was open for 0% of the time, Pallas kernels for 0%

commit v1 on v0

v1 whole, which is shorter than its diff:
```python
import jax
import jax.numpy as jnp
from jax import lax
from jax.experimental import pallas as pl
from jax.experimental.pallas import tpu as pltpu
from jax.sharding import Mesh, PartitionSpec as P

HEADS = 2
POOL = 32
ROW = ("y", "xl")
COL = ("xh", "z", "c")
CHIPS = ("xl", "y", "xh", "z")
FAR = ("y", "xh", "z")
NEAR = ("xl", "c")
HALO = 64


def product(left, right, dims=((1,), (0,))):
    return lax.dot_general(
        left,
        right,
        (dims, ((), ())),
        precision=lax.Precision.HIGHEST,
        preferred_element_type=jnp.float32,
    )


def normalize(values_in):
    average = jnp.mean(values_in, -1, keepdims=True)
    centered = values_in - average
    inv_std = lax.rsqrt(jnp.mean(centered * centered, -1, keepdims=True) + 1e-06)
    return (centered * inv_std, inv_std)


def norm_back(gradient, normed, inv_std):
    return inv_std * (
        gradient
        - jnp.mean(gradient, -1, keepdims=True)
        - normed * jnp.mean(gradient * normed, -1, keepdims=True)
    )


def neighbours(low_side, high_side, axis):
    peers = lax.axis_size(axis)
    up = [(i, i + 1) for i in range(peers - 1)]
    down = [(i + 1, i) for i in range(peers - 1)]
    return lax.ppermute(high_side, axis, up), lax.ppermute(low_side, axis, down)


def halo(tokens, cotangent):
    cols = tokens.shape[1]
    low = jnp.concatenate([tokens[:2], cotangent[:1]])
    high = jnp.concatenate([tokens[-2:], cotangent[-1:]])
    before, after = neighbours(low, high, ROW)
    tall_t = jnp.concatenate([before[:2], tokens, after[:2]])
    tall_g = jnp.concatenate([before[2:], cotangent, after[2:]])
    rows_t, rows_g = tall_t.shape[0], tall_g.shape[0]

    def side(first_t, first_g):
        part_t = tall_t[:, first_t : first_t + 2].reshape(2 * rows_t, -1)
        return jnp.concatenate([part_t, tall_g[:, first_g]])

    before, after = neighbours(side(0, 0), side(cols - 2, cols - 1), COL)

    def parts(received):
        return (
            received[: 2 * rows_t].reshape(rows_t, 2, -1),
            received[2 * rows_t :].reshape(rows_g, 1, -1),
        )

    (before_t, before_g), (after_t, after_g) = parts(before), parts(after)
    return (
        jnp.concatenate([before_t, tall_t, after_t], 1),
        jnp.concatenate([before_g, tall_g, after_g], 1),
    )


def ring(extended):
    rows, cols, channels = extended.shape
    used = 2 * cols + 2 * (rows - 2)
    return jnp.concatenate(
        [
            extended[0],
            extended[-1],
            extended[1:-1, 0],
            extended[1:-1, -1],
            jnp.zeros((HALO - used, channels), extended.dtype),
        ]
    )


def attention(keys, normed, normed_ring, grad, grad_ring, w_query, w_key, w_value, w_out):
    channels = keys.shape[1]
    count = normed.shape[0]
    width = channels // HEADS
    scale = width ** (-0.5)
    tokens_t = jnp.concatenate([normed, normed_ring]).T
    grads_t = jnp.concatenate([grad, grad_ring]).T
    query_t = product(w_query, tokens_t, ((0,), (0,)))
    d_att_t = product(w_out, grads_t)
    to_keys, to_values = [], []
    for head in range(HEADS):
        part = slice(head * width, (head + 1) * width)
        to_keys.append(product(w_key[:, part], query_t[part]) * scale)
        to_values.append(product(w_value[:, part], d_att_t[part]))
    inner = [x[:, :count] for x in to_keys], [x[:, :count] for x in to_values]
    outer = [x[:, count:] for x in to_keys], [x[:, count:] for x in to_values]
    query_keys = jnp.concatenate(inner[0] + outer[0], 1)
    d_att_values = jnp.concatenate(inner[1] + outer[1], 1)
    scores = product(keys, query_keys)
    weights = jnp.exp(scores - jnp.max(scores, 0, keepdims=True))
    probs = weights * (1.0 / jnp.sum(weights, 0, keepdims=True))
    d_probs = product(keys, d_att_values)
    att_keys = product(keys, probs, ((0,), (0,)))
    d_scores = probs * (d_probs - jnp.sum(d_probs * probs, 0, keepdims=True))
    d_query_keys = product(keys, d_scores, ((0,), (0,)))
    wide = HEADS * count
    both = ((1,), (1,))
    d_pooled_sum = product(d_scores[:, :wide], query_keys[:, :wide], both) + product(
        probs[:, :wide], d_att_values[:, :wide], both
    )
    att_t, dq_t, dq_ring_t, g_key, g_value = [], [], [], [], []
    ring_count = normed_ring.shape[0]
    for head in range(HEADS):
        part = slice(head * width, (head + 1) * width)
        own = slice(head * count, (head + 1) * count)
        far = slice(wide + head * ring_count, wide + (head + 1) * ring_count)
        att_t.append(product(w_value[:, part], att_keys[:, own], ((0,), (0,))))
        dq_t.append(product(w_key[:, part], d_query_keys[:, own], ((0,), (0,))) * scale)
        dq_ring_t.append(product(w_key[:, part], d_query_keys[:, far], ((0,), (0,))) * scale)
        g_key.append(product(d_query_keys[:, own], query_t[part, :count], both) * scale)
        g_value.append(product(att_keys[:, own], d_att_t[part, :count], both))
    att_t, dq_t, dq_ring_t = (jnp.concatenate(x) for x in (att_t, dq_t, dq_ring_t))
    att_out = product(att_t, w_out, ((0,), (0,)))
    d_normed = product(dq_t, w_query, ((0,), (1,)))
    d_normed_ring = product(dq_ring_t, w_query, ((0,), (1,)))
    g_query = product(tokens_t[:, :count], dq_t, both)
    g_out = product(att_t, grads_t[:, :count], both)
    weight_grads = jnp.concatenate(
        [g_query, jnp.concatenate(g_key, 1), jnp.concatenate(g_value, 1), g_out]
    )
    return att_out, d_pooled_sum, weight_grads, d_normed, d_normed_ring


def body(tokens, cotangent, conv_weight, w_query, w_key, w_value, w_out):
    tile_rows, tile_cols, channels = tokens.shape
    count = tile_rows * tile_cols
    row_count = lax.axis_size(ROW)
    col_count = lax.axis_size(COL)
    win_r = tile_rows * row_count // POOL
    win_c = tile_cols * col_count // POOL
    cells = tile_rows // win_r
    chips = lax.axis_size(CHIPS)
    far_count = lax.axis_size(FAR)

    padded_t, padded_g = halo(tokens, cotangent)
    ext_r, ext_c = tile_rows + 2, tile_cols + 2
    mixed = padded_t[1 : 1 + ext_r, 1 : 1 + ext_c]
    for i in range(3):
        for j in range(3):
            mixed = mixed + conv_weight[i, j] * padded_t[i : i + ext_r, j : j + ext_c]
    normed_ext, inv_ext = normalize(mixed)
    normed, inv_std = normed_ext[1:-1, 1:-1], inv_ext[1:-1, 1:-1]
    pooled = jnp.mean(normed.reshape(cells, win_r, win_c, channels), axis=(1, 2))
    pooled_n, pooled_inv = normalize(pooled)

    spread = jnp.broadcast_to(pooled_n[None], (chips, cells, channels))
    spread = lax.all_to_all(spread, CHIPS, 0, 0, tiled=True)
    keys = lax.all_gather(spread, "c", axis=0, tiled=True).reshape(-1, channels)

    normed_ring, inv_ring, grad_ring = ring(normed_ext), ring(inv_ext), ring(padded_g)
    flat_n = normed.reshape(count, channels)
    att_out, d_sum, weight_grads, d_normed, d_normed_ring = attention(
        keys,
        flat_n,
        normed_ring,
        cotangent.reshape(count, channels),
        grad_ring,
        w_query,
        w_key,
        w_value,
        w_out,
    )
    output = mixed[1:-1, 1:-1] + att_out.reshape(tokens.shape)

    sums = jnp.concatenate(
        [
            d_sum.reshape(2 * chips, cells, channels),
            weight_grads.reshape(2 * chips, 1, channels),
        ],
        1,
    )
    sums = lax.all_to_all(sums, "c", 0, 0, tiled=True)
    sums = sums[:chips] + sums[chips:]
    sums = jnp.sum(lax.all_to_all(sums, CHIPS, 0, 0, tiled=True), 0)
    d_pooled = norm_back(sums[:cells], pooled_n, pooled_inv) / float(win_r * win_c)

    d_tile = d_normed.reshape(cells, win_r, tile_cols, channels) + d_pooled[:, None, None]
    d_mixed = cotangent + norm_back(d_tile.reshape(tokens.shape), normed, inv_std)
    g_conv = [
        jnp.sum(padded_t[1 + i : 1 + i + tile_rows, 1 + j : 1 + j + tile_cols] * d_mixed, (0, 1))
        for i in range(3)
        for j in range(3)
    ]

    share = jnp.concatenate([d_pooled, sums[cells:], jnp.stack(g_conv)])
    share = jnp.broadcast_to(share[None], (far_count,) + share.shape)
    share = lax.all_to_all(share, FAR, 0, 0, tiled=True)
    kept = cells + 1
    conv_part = jnp.sum(share[:, kept:], 0)
    conv_part = jnp.concatenate([conv_part, jnp.zeros((7, channels), jnp.float32)])
    share = jnp.concatenate(
        [
            share[:, :cells].reshape(far_count * cells, channels),
            share[:, cells],
            conv_part,
        ]
    )
    near = lax.all_gather(share, NEAR, axis=0)
    pools = near[:, : far_count * cells].reshape(2, 2, 8, 2, 8, cells, channels)
    weights = near[:, far_count * cells : far_count * kept]
    g_conv = jnp.sum(near[:, far_count * kept :], 0)[:9].reshape(3, 3, channels)

    row, col = lax.axis_index(ROW), lax.axis_index(COL)

    def owner(d_row, d_col):
        r = jnp.clip(row + d_row, 0, row_count - 1)
        k = jnp.clip(col + d_col, 0, col_count - 1)
        start = (r % 2, k % 2, r // 2, k // 16, (k // 2) % 8, 0, 0)
        return lax.dynamic_slice(pools, start, (1,) * 5 + (cells, channels)).reshape(
            cells, channels
        )

    def line(d_row, cell):
        return jnp.concatenate(
            [
                owner(d_row, -1)[cell][None],
                jnp.broadcast_to(owner(d_row, 0)[cell][None], (tile_cols, channels)),
                owner(d_row, 1)[cell][None],
            ]
        )

    def column(d_col):
        return jnp.repeat(owner(0, d_col), win_r, axis=0)

    top, bottom = line(-1, cells - 1), line(1, 0)
    left, right = column(-1), column(1)
    used = 2 * ext_c + 2 * tile_rows
    d_ring = d_normed_ring[:used] + jnp.concatenate([top, bottom, left, right])
    d_ring = grad_ring[:used] + norm_back(d_ring, normed_ring[:used], inv_ring[:used])
    top, bottom = d_ring[:ext_c], d_ring[ext_c : 2 * ext_c]
    left = d_ring[2 * ext_c : 2 * ext_c + tile_rows]
    right = d_ring[2 * ext_c + tile_rows :]
    left, right = jnp.where(col > 0, left, 0.0), jnp.where(col < col_count - 1, right, 0.0)
    at = lax.broadcasted_iota(jnp.int32, (ext_c, 1), 0)
    inside = ((at > 0) | (col > 0)) & ((at < ext_c - 1) | (col < col_count - 1))
    top = jnp.where(inside & (row > 0), top, 0.0)
    bottom = jnp.where(inside & (row < row_count - 1), bottom, 0.0)
    padded_d = jnp.concatenate([left[:, None], d_mixed, right[:, None]], 1)
    padded_d = jnp.concatenate([top[None], padded_d, bottom[None]])
    d_tokens = d_mixed
    for i in range(3):
        for j in range(3):
            d_tokens = (
                d_tokens
                + conv_weight[i, j] * padded_d[2 - i : 2 - i + tile_rows, 2 - j : 2 - j + tile_cols]
            )
    root = float(count * row_count * col_count) ** (-0.5)
    g_query, g_value, g_key, g_out = (weights[k] for k in range(4))
    return (
        output,
        d_tokens,
        g_conv * root,
        g_query * root,
        g_key / float(POOL),
        g_value / float(POOL),
        g_out * root,
    )


def solution(mesh):
    fine = Mesh(mesh.devices.reshape(8, 2, 2, 8, 2), ("y", "xl", "xh", "z", "c"))
    tile = P(ROW, COL, None)
    return jax.shard_map(
        body,
        mesh=fine,
        in_specs=(tile, tile, P(), P(), P(), P(), P()),
        out_specs=(tile, tile, P(), P(), P(), P(), P()),
        check_vma=False,
    )
```

time: 1390 us -> 168 us (0.12)
  blocking collectives: 788 us -> 23.7 us
  waiting for transfers between devices: 527 us -> 56.8 us
  starting transfers between devices: 25.6 us -> 55 us
    all_gather x1 -> x2, blocking collectives: 689 us -> 19.1 us  [the longest x1 12.3 us: body(): near = lax.all_gather(share, NEAR, axis=0)]
    psum x1 -> x0, waiting for transfers between devices: 266 us -> none  [body(): lax.psum((grad_conv, grad_query, grad_key, grad_value, grad_out), ('row',...]
    unnamed x3 -> x0, waiting for transfers between devices: 260 us -> none
    psum x1 -> x0, blocking collectives: 98.4 us -> none  [body(): lax.psum((grad_conv, grad_query, grad_key, grad_value, grad_out), ('row',...]
    all_to_all x0 -> x3, waiting for transfers between devices: none -> 55.6 us  [the longest x1 25.5 us: body(): share = lax.all_to_all(share, FAR, 0, 0, tiled=True)]
    all_to_all x0 -> x3, starting transfers between devices: none -> 38.5 us  [the longest x1 21.1 us: body(): spread = lax.all_to_all(spread, CHIPS, 0, 0, tiled=True)]
  transfers between devices with their start and end apart: 10 -> 7, of which waited for: 4 -> 4; matrix products, arithmetic and copies ran while one was open for 0% -> 3% of each run, Pallas kernels for 0% -> 0%
where the time goes in v1:
time: 168 us
  waiting for transfers between devices  56.8 us (34%)
  starting transfers between devices  55 us (33%)
  blocking collectives  23.7 us (14%)
  matrix products  14.8 us (9%)
  local copies, waits for them, and re-layouts  10.3 us (6%)
  other arithmetic  5.28 us (3%)
  between operations  1.76 us (1%)
    all_to_all x1, waiting for transfers between devices, body(): share = lax.all_to_all(share, FAR, 0, 0, tiled=True)  25.5 us
    all_to_all x1, starting transfers between devices, body(): spread = lax.all_to_all(spread, CHIPS, 0, 0, tiled=True)  21.1 us
    all_to_all x1, waiting for transfers between devices, body(): sums = jnp.sum(lax.all_to_all(sums, CHIPS, 0, 0, tiled=True), 0)  18.6 us
    dot_general x27, matrix products, product(): lax.dot_general(left, right, (dims, ((), ())), precision=lax.Precision.HI...  14.8 us
    all_gather x1, blocking collectives, body(): near = lax.all_gather(share, NEAR, axis=0)  12.3 us
    all_to_all x1, waiting for transfers between devices, body(): spread = lax.all_to_all(spread, CHIPS, 0, 0, tiled=True)  11.5 us
    ppermute x2, starting transfers between devices, neighbours(): lax.ppermute(low_side, axis, down)  10.1 us
    all_to_all x1, starting transfers between devices, body(): sums = jnp.sum(lax.all_to_all(sums, CHIPS, 0, 0, tiled=True), 0)  9.39 us
  transfers between devices with their start and end apart: 7, of which 4 were waited for; matrix products, arithmetic and copies ran while one was open for 3% of the time, Pallas kernels for 0%

profile of v1, /device:TPU:1, one launch (start us, length us, event | category | flops | bytes accessed | tf_op | source)
XLA Modules:
  0.0 167.7 jit_solution(18145387090889432257)
XLA Ops:
  2.3 1.3 collective-permute-start.1
  3.7 4.6 %collective-permute-start = (f32[3,16,128]{2,0,1:T(4,128)S(1)}, f32[3,16,128]{2,0,1:T(4,128)S(1)}, u32[]{:S(2)}, u32[]{:S(2)}) collective-permute-start(f32[3,16,128]{2,0,1:T(4,128)S(1)} %pad_maximum_fusion.14), channel_id=1, source_target_pairs={{0,32},{32,64},{64,96},{96,128},{128,160},{160,192},{192,224},{224... | collective-permute-start | bytes 73736 | tf_op jit(solution)/shard_map/ppermute | solution.py:47
  10.1 8.8 %collective-permute-start.3 = (f32[34,128]{1,0:T(8,128)S(1)}, f32[34,128]{1,0:T(8,128)S(1)}, u32[]{:S(2)}, u32[]{:S(2)}) collective-permute-start(f32[34,128]{1,0:T(8,128)S(1)} %pad_maximum_fusion.20), channel_id=1, source_target_pairs={{1,0},{2,1},{3,2},{4,3},{5,4},{6,5},{7,6},{8,7},{9,8},{10,9},{11,1... | collective-permute-start | bytes 52232 | tf_op jit(solution)/shard_map/ppermute | solution.py:47
  18.9 1.9 %collective-permute-start.2 = (f32[34,128]{1,0:T(8,128)S(1)}, f32[34,128]{1,0:T(8,128)S(1)}, u32[]{:S(2)}, u32[]{:S(2)}) collective-permute-start(f32[34,128]{1,0:T(8,128)S(1)} %pad_maximum_fusion.19), channel_id=1, source_target_pairs={{0,1},{1,2},{2,3},{3,4},{4,5},{5,6},{6,7},{7,8},{8,9},{9,10},{10,1... | collective-permute-start | bytes 52232 | tf_op jit(solution)/shard_map/ppermute | solution.py:47
  20.9 1.1 collective-permute-done.2
  22.1 1.3 concatenate.140
  23.3 1.1 convolution_bitcast_fusion.2
  27.1 21.1 %all-to-all-start = ((f32[256,2,128]{2,1,0:T(2,128)}), f32[256,2,128]{2,1,0:T(2,128)S(1)}, u32[]{:S(2)}, u32[]{:S(2)}) async-start(f32[256,2,128]{2,1,0:T(2,128)} %broadcast_in_dim.84), calls=%async_computation | async-start | bytes 524288 | tf_op jit(solution)/shard_map/all_to_all | solution.py:168
  49.7 11.5 %all-to-all-done = f32[256,2,128]{2,1,0:T(2,128)S(1)} async-done(((f32[256,2,128]{2,1,0:T(2,128)}), f32[256,2,128]{2,1,0:T(2,128)S(1)}, u32[]{:S(2)}, u32[]{:S(2)}) %all-to-all-start) | async-done | bytes 262176 | tf_op jit(solution)/shard_map/all_to_all | solution.py:168
  61.1 6.8 %all_gather.9 = f32[512,2,128]{2,1,0:T(2,128)S(1)} all-gather(f32[256,2,128]{2,1,0:T(2,128)S(1)} %all-to-all-done), channel_id=1, replica_groups=mesh['y'=8,'xl'=2,'xh'=2,'z'=8,'c'=2] {'c'}, dimensions={0}, use_global_device_ids=true | all-gather | bytes 786432 | tf_op jit(solution)/shard_map/all_gather | solution.py:169
  67.9 1.4 fusion.130
  69.7 1.6 multiply_reduce_fusion
  71.5 1.3 fusion.132
  72.8 1.0 fusion.9
  73.8 1.3 fusion.131
  77.6 1.0 convolution_add_fusion
  79.7 4.6 %all_to_all.20 = f32[512,3,128]{2,1,0:T(4,128)S(1)} all-to-all(f32[512,3,128]{2,1,0:T(4,128)S(1)} %pad_maximum_fusion), channel_id=1, replica_groups=mesh['y'=8,'xl'=2,'xh'=2,'z'=8,'c'=2] {'c'}, dimensions={0} | all-to-all | bytes 1572864 | tf_op jit(solution)/shard_map/all_to_all | solution.py:193
  84.3 0.9 slice_add_fusion
  85.3 9.4 %all-to-all-start.2 = ((f32[256,3,128]{2,1,0:T(4,128)}), f32[256,3,128]{2,1,0:T(4,128)S(1)}, u32[]{:S(2)}, u32[]{:S(2)}) async-start(f32[256,3,128]{2,1,0:T(4,128)} %slice_add_fusion), calls=%async_computation.2 | async-start | bytes 1048576 | tf_op jit(solution)/shard_map/all_to_all | solution.py:195
  94.7 18.6 %all-to-all-done.2 = f32[256,3,128]{2,1,0:T(4,128)S(1)} async-done(((f32[256,3,128]{2,1,0:T(4,128)}), f32[256,3,128]{2,1,0:T(4,128)S(1)}, u32[]{:S(2)}, u32[]{:S(2)}) %all-to-all-start.2) | async-done | bytes 393248 | tf_op jit(solution)/shard_map/all_to_all | solution.py:195
  114.9 1.1 broadcast_in_dim.85
  115.9 8.0 %all-to-all-start.3 = ((f32[128,12,128]{2,1,0:T(8,128)}), f32[128,12,128]{2,1,0:T(8,128)S(1)}, u32[]{:S(2)}, u32[]{:S(2)}) async-start(f32[128,12,128]{2,1,0:T(8,128)} %broadcast_in_dim.85), calls=%async_computation.3 | async-start | bytes 2097152 | tf_op jit(solution)/shard_map/all_to_all | solution.py:208
  126.1 25.5 %all-to-all-done.3 = f32[128,12,128]{2,1,0:T(8,128)S(1)} async-done(((f32[128,12,128]{2,1,0:T(8,128)}), f32[128,12,128]{2,1,0:T(8,128)S(1)}, u32[]{:S(2)}, u32[]{:S(2)}) %all-to-all-start.3) | async-done | bytes 786464 | tf_op jit(solution)/shard_map/all_to_all | solution.py:208
  152.0 12.3 %all-gather = f32[1600,128]{1,0:T(8,128)S(1)} all-gather(f32[400,128]{1,0:T(8,128)S(1)} %maximum_maximum_fusion), channel_id=2, replica_groups=mesh['y'=8,'xl'=2,'xh'=2,'z'=8,'c'=2] {'xl','c'}, dimensions={0}, use_global_device_ids=true | all-gather | bytes 1024000 | tf_op jit(solution)/shard_map/all_gather | solution.py:219
  (157 shorter events, 18.4 us)
Async XLA Ops:
  0.6 48.0 %copy-start = (f32[128,128]{1,0:T(8,128)S(1)}, f32[128,128]{1,0:T(8,128)}, u32[]{:S(2)}) copy-start(f32[128,128]{1,0:T(8,128)} %param.10) | copy-start | bytes 196612
  0.6 23.8 %copy-start.2 = (f32[128,128]{1,0:T(8,128)S(1)}, f32[128,128]{1,0:T(8,128)}, u32[]{:S(2)}) copy-start(f32[128,128]{1,0:T(8,128)} %param.12) | copy-start | bytes 196612
  2.3 7.6 %collective-permute-start.1 = (f32[3,16,128]{2,0,1:T(4,128)S(1)}, f32[3,16,128]{2,0,1:T(4,128)S(1)}, u32[]{:S(2)}, u32[]{:S(2)}) collective-permute-start(f32[3,16,128]{2,0,1:T(4,128)S(1)} %pad_maximum_fusion.15), channel_id=1, source_target_pairs={{32,0},{64,32},{96,64},{128,96},{160,128},{192,160},{224,192},{256... | collective-permute-start | bytes 73736 | tf_op jit(solution)/shard_map/ppermute | solution.py:47
  3.7 6.3 %collective-permute-start = (f32[3,16,128]{2,0,1:T(4,128)S(1)}, f32[3,16,128]{2,0,1:T(4,128)S(1)}, u32[]{:S(2)}, u32[]{:S(2)}) collective-permute-start(f32[3,16,128]{2,0,1:T(4,128)S(1)} %pad_maximum_fusion.14), channel_id=1, source_target_pairs={{0,32},{32,64},{64,96},{96,128},{128,160},{160,192},{192,224},{224... | collective-permute-start | bytes 73736 | tf_op jit(solution)/shard_map/ppermute | solution.py:47
  10.1 10.7 %collective-permute-start.3 = (f32[34,128]{1,0:T(8,128)S(1)}, f32[34,128]{1,0:T(8,128)S(1)}, u32[]{:S(2)}, u32[]{:S(2)}) collective-permute-start(f32[34,128]{1,0:T(8,128)S(1)} %pad_maximum_fusion.20), channel_id=1, source_target_pairs={{1,0},{2,1},{3,2},{4,3},{5,4},{6,5},{7,6},{8,7},{9,8},{10,9},{11,1... | collective-permute-start | bytes 52232 | tf_op jit(solution)/shard_map/ppermute | solution.py:47
  18.9 3.1 %collective-permute-start.2 = (f32[34,128]{1,0:T(8,128)S(1)}, f32[34,128]{1,0:T(8,128)S(1)}, u32[]{:S(2)}, u32[]{:S(2)}) collective-permute-start(f32[34,128]{1,0:T(8,128)S(1)} %pad_maximum_fusion.19), channel_id=1, source_target_pairs={{0,1},{1,2},{2,3},{3,4},{4,5},{5,6},{6,7},{7,8},{8,9},{9,10},{10,1... | collective-permute-start | bytes 52232 | tf_op jit(solution)/shard_map/ppermute | solution.py:47
  24.8 24.1 %copy-start.5 = (f32[128,192]{0,1:T(8,128)}, f32[128,192]{0,1:T(8,128)S(1)}, u32[]{:S(2)}) copy-start(f32[128,192]{0,1:T(8,128)S(1)} %convolution_bitcast_fusion) | copy-start | bytes 294916
  25.1 23.9 %copy-start.4 = (f32[128,192]{0,1:T(8,128)}, f32[128,192]{0,1:T(8,128)S(1)}, u32[]{:S(2)}) copy-start(f32[128,192]{0,1:T(8,128)S(1)} %convolution_bitcast_fusion.1) | copy-start | bytes 294916
  25.4 23.5 %copy-start.1 = (f32[128,128]{1,0:T(8,128)S(1)}, f32[128,128]{1,0:T(8,128)}, u32[]{:S(2)}) copy-start(f32[128,128]{1,0:T(8,128)} %param.11) | copy-start | bytes 196612
  27.1 34.0 %all-to-all-start = ((f32[256,2,128]{2,1,0:T(2,128)}), f32[256,2,128]{2,1,0:T(2,128)S(1)}, u32[]{:S(2)}, u32[]{:S(2)}) async-start(f32[256,2,128]{2,1,0:T(2,128)} %broadcast_in_dim.84), calls=%async_computation | async-start | bytes 524288 | tf_op jit(solution)/shard_map/all_to_all | solution.py:168
  67.9 1.7 %slice-start = ((f32[128,192]{0,1:T(8,128)}), f32[128,64]{0,1:T(8,128)S(1)}, s32[]{:S(2)}) async-start(f32[128,192]{0,1:T(8,128)} %copy-done.4), calls=%async_computation.4 | async-start | bytes 65536 | tf_op jit(solution)/shard_map/slice | solution.py:107
  67.9 1.7 %slice-start.1 = ((f32[128,192]{0,1:T(8,128)}), f32[128,64]{0,1:T(8,128)S(1)}, s32[]{:S(2)}) async-start(f32[128,192]{0,1:T(8,128)} %copy-done.5), calls=%async_computation.5 | async-start | bytes 65536 | tf_op jit(solution)/shard_map/slice | solution.py:107
  84.3 30.3 %copy-start.3 = (f32[8,16,128]{2,1,0:T(8,128)S(1)}, f32[8,16,128]{2,1,0:T(8,128)}, u32[]{:S(2)}) copy-start(f32[8,16,128]{2,1,0:T(8,128)} %param.8) | copy-start | bytes 196612
  84.3 30.3 %copy-start.6 = (f32[8,16,128]{2,1,0:T(8,128)S(1)}, f32[8,16,128]{2,1,0:T(8,128)}, u32[]{:S(2)}) copy-start(f32[8,16,128]{2,1,0:T(8,128)} %param.7) | copy-start | bytes 196612
  85.3 28.1 %all-to-all-start.2 = ((f32[256,3,128]{2,1,0:T(4,128)}), f32[256,3,128]{2,1,0:T(4,128)S(1)}, u32[]{:S(2)}, u32[]{:S(2)}) async-start(f32[256,3,128]{2,1,0:T(4,128)} %slice_add_fusion), calls=%async_computation.2 | async-start | bytes 1048576 | tf_op jit(solution)/shard_map/all_to_all | solution.py:195
  114.8 9.7 %copy-start.7 = (f32[128,128]{1,0:T(8,128)S(1)}, f32[128,128]{1,0:T(8,128)}, u32[]{:S(2)}) copy-start(f32[128,128]{1,0:T(8,128)} %param.13) | copy-start | bytes 196612
  115.9 35.7 %all-to-all-start.3 = ((f32[128,12,128]{2,1,0:T(8,128)}), f32[128,12,128]{2,1,0:T(8,128)S(1)}, u32[]{:S(2)}, u32[]{:S(2)}) async-start(f32[128,12,128]{2,1,0:T(8,128)} %broadcast_in_dim.85), calls=%async_computation.3 | async-start | bytes 2097152 | tf_op jit(solution)/shard_map/all_to_all | solution.py:208

commit v2 on v1

--- a/solution.py
+++ b/solution.py
@@ -9,20 +9,19 @@
 POOL = 32
 ROW = ("y", "xl")
 COL = ("xh", "z", "c")
-CHIPS = ("xl", "y", "xh", "z")
-FAR = ("y", "xh", "z")
-NEAR = ("xl", "c")
+CHIP_COL = ("xh", "z")
+CHIPS = CHIP_COL + ROW
 HALO = 64
 
 
-def product(left, right, dims=((1,), (0,))):
+def product(left, right, dims=((1,), (0,)), precision=lax.Precision.HIGH):
     return lax.dot_general(
-        left,
-        right,
-        (dims, ((), ())),
-        precision=lax.Precision.HIGHEST,
-        preferred_element_type=jnp.float32,
-    )
+        left, right, (dims, ((), ())), precision=precision, preferred_element_type=jnp.float32
+    )
+
+
+def exact(left, right, dims=((1,), (0,))):
+    return product(left, right, dims, lax.Precision.HIGHEST)
 
 
 def normalize(values_in):
@@ -96,18 +95,18 @@
     scale = width ** (-0.5)
     tokens_t = jnp.concatenate([normed, normed_ring]).T
     grads_t = jnp.concatenate([grad, grad_ring]).T
-    query_t = product(w_query, tokens_t, ((0,), (0,)))
+    query_t = exact(w_query, tokens_t, ((0,), (0,)))
     d_att_t = product(w_out, grads_t)
     to_keys, to_values = [], []
     for head in range(HEADS):
         part = slice(head * width, (head + 1) * width)
-        to_keys.append(product(w_key[:, part], query_t[part]) * scale)
+        to_keys.append(exact(w_key[:, part], query_t[part]) * scale)
         to_values.append(product(w_value[:, part], d_att_t[part]))
     inner = [x[:, :count] for x in to_keys], [x[:, :count] for x in to_values]
     outer = [x[:, count:] for x in to_keys], [x[:, count:] for x in to_values]
     query_keys = jnp.concatenate(inner[0] + outer[0], 1)
     d_att_values = jnp.concatenate(inner[1] + outer[1], 1)
-    scores = product(keys, query_keys)
+    scores = exact(keys, query_keys)
     weights = jnp.exp(scores - jnp.max(scores, 0, keepdims=True))
     probs = weights * (1.0 / jnp.sum(weights, 0, keepdims=True))
     d_probs = product(keys, d_att_values)
@@ -151,7 +150,7 @@
     win_c = tile_cols * col_count // POOL
     cells = tile_rows // win_r
     chips = lax.axis_size(CHIPS)
-    far_count = lax.axis_size(FAR)
+    lines = lax.axis_size(CHIP_COL)
 
     padded_t, padded_g = halo(tokens, cotangent)
     ext_r, ext_c = tile_rows + 2, tile_cols + 2
@@ -185,14 +184,15 @@
 
     sums = jnp.concatenate(
         [
-            d_sum.reshape(2 * chips, cells, channels),
+            d_sum.reshape(2 * chips, 1, cells * channels),
             weight_grads.reshape(2 * chips, 1, channels),
         ],
-        1,
+        2,
     )
     sums = lax.all_to_all(sums, "c", 0, 0, tiled=True)
     sums = sums[:chips] + sums[chips:]
     sums = jnp.sum(lax.all_to_all(sums, CHIPS, 0, 0, tiled=True), 0)
+    sums = sums.reshape(cells + 1, channels)
     d_pooled = norm_back(sums[:cells], pooled_n, pooled_inv) / float(win_r * win_c)
 
     d_tile = d_normed.reshape(cells, win_r, tile_cols, channels) + d_pooled[:, None, None]
@@ -203,33 +203,28 @@
         for j in range(3)
     ]
 
-    share = jnp.concatenate([d_pooled, sums[cells:], jnp.stack(g_conv)])
-    share = jnp.broadcast_to(share[None], (far_count,) + share.shape)
-    share = lax.all_to_all(share, FAR, 0, 0, tiled=True)
-    kept = cells + 1
-    conv_part = jnp.sum(share[:, kept:], 0)
-    conv_part = jnp.concatenate([conv_part, jnp.zeros((7, channels), jnp.float32)])
+    row, col = lax.axis_index(ROW), lax.axis_index(COL)
     share = jnp.concatenate(
-        [
-            share[:, :cells].reshape(far_count * cells, channels),
-            share[:, cells],
-            conv_part,
-        ]
-    )
-    near = lax.all_gather(share, NEAR, axis=0)
-    pools = near[:, : far_count * cells].reshape(2, 2, 8, 2, 8, cells, channels)
-    weights = near[:, far_count * cells : far_count * kept]
-    g_conv = jnp.sum(near[:, far_count * kept :], 0)[:9].reshape(3, 3, channels)
-
-    row, col = lax.axis_index(ROW), lax.axis_index(COL)
+        [d_pooled, sums[cells:], jnp.stack(g_conv), jnp.zeros((4, channels), jnp.float32)]
+    )
+    share = jnp.broadcast_to(share[None], (row_count,) + share.shape)
+    share = lax.all_to_all(share, ROW, 0, 0, tiled=True)
+    near_rows = jnp.pad(share[:, :cells], ((1, 1), (0, 0), (0, 0)))
+    near_rows = lax.dynamic_slice_in_dim(near_rows, row, 3, 0).reshape(3 * cells, channels)
+    g_conv = jnp.sum(share[:, cells + 1 : cells + 10], 0)
+    share = jnp.concatenate(
+        [share[:, cells], g_conv, near_rows, jnp.zeros((1, channels), jnp.float32)]
+    )
+    share = jnp.broadcast_to(share[None], (lines,) + share.shape)
+    share = lax.all_to_all(share, CHIP_COL, 0, 0, tiled=True)
+    near = lax.all_gather(share, "c", axis=0)
+    weights = near[:, :, :row_count].reshape(4, channels, channels)
+    g_conv = jnp.sum(near[:, :, row_count : row_count + 9], (0, 1)).reshape(3, 3, channels)
 
     def owner(d_row, d_col):
-        r = jnp.clip(row + d_row, 0, row_count - 1)
         k = jnp.clip(col + d_col, 0, col_count - 1)
-        start = (r % 2, k % 2, r // 2, k // 16, (k // 2) % 8, 0, 0)
-        return lax.dynamic_slice(pools, start, (1,) * 5 + (cells, channels)).reshape(
-            cells, channels
-        )
+        start = (k % 2, k // 2, row_count + 9 + (d_row + 1) * cells, 0)
+        return lax.dynamic_slice(near, start, (1, 1, cells, channels)).reshape(cells, channels)
 
     def line(d_row, cell):
         return jnp.concatenate(
@@ -266,7 +261,7 @@
                 + conv_weight[i, j] * padded_d[2 - i : 2 - i + tile_rows, 2 - j : 2 - j + tile_cols]
             )
     root = float(count * row_count * col_count) ** (-0.5)
-    g_query, g_value, g_key, g_out = (weights[k] for k in range(4))
+    g_query, g_key, g_value, g_out = (weights[k] for k in range(4))
     return (
         output,
         d_tokens,

time: 168 us -> 147 us (0.88)
  waiting for transfers between devices: 56.8 us -> 45.3 us
  blocking collectives: 23.7 us -> 17.4 us
  matrix products: 14.8 us -> 11.5 us
    all_to_all x1 -> x2, waiting for transfers between devices: 25.5 us -> 16.2 us  [the longest x1 8.18 us: body(): share = lax.all_to_all(share, ROW, 0, 0, tiled=True)]
    all_gather x1, blocking collectives: 12.3 us -> 6.11 us  [body(): near = lax.all_gather(share, 'c', axis=0)]
    dot_general x27, matrix products: 14.8 us -> 11.5 us  [product(): lax.dot_general(left, right, (dims, ((), ())), precision=precision, prefe...]
    all_to_all x1, waiting for transfers between devices: 18.6 us -> 16.6 us  [body(): sums = jnp.sum(lax.all_to_all(sums, CHIPS, 0, 0, tiled=True), 0)]
    all_to_all x1 -> x2, starting transfers between devices: 7.99 us -> 7.04 us  [the longest x1 3.53 us: body(): share = lax.all_to_all(share, CHIP_COL, 0, 0, tiled=True)]
  transfers between devices with their start and end apart: 7 -> 8, of which waited for: 4 -> 5; matrix products, arithmetic and copies ran while one was open for 3% -> 3% of each run, Pallas kernels for 0% -> 0%
where the time goes in v2:
time: 147 us; the launch traced here: 146 us
  starting transfers between devices  54.2 us (37%)
  waiting for transfers between devices  45.3 us (31%)
  blocking collectives  17.4 us (12%)
  matrix products  11.5 us (8%)
  local copies, waits for them, and re-layouts  10.6 us (7%)
  other arithmetic  5.58 us (4%)
  between operations  1.66 us (1%)
    all_to_all x1, starting transfers between devices, body(): spread = lax.all_to_all(spread, CHIPS, 0, 0, tiled=True)  21.1 us
    all_to_all x1, waiting for transfers between devices, body(): sums = jnp.sum(lax.all_to_all(sums, CHIPS, 0, 0, tiled=True), 0)  16.6 us
    dot_general x27, matrix products, product(): lax.dot_general(left, right, (dims, ((), ())), precision=precision, prefe...  11.5 us
    all_to_all x1, waiting for transfers between devices, body(): spread = lax.all_to_all(spread, CHIPS, 0, 0, tiled=True)  11.4 us
    ppermute x2, starting transfers between devices, neighbours(): lax.ppermute(low_side, axis, down)  10.1 us
    all_to_all x1, starting transfers between devices, body(): sums = jnp.sum(lax.all_to_all(sums, CHIPS, 0, 0, tiled=True), 0)  9.52 us
    all_to_all x1, waiting for transfers between devices, body(): share = lax.all_to_all(share, ROW, 0, 0, tiled=True)  8.18 us
    all_to_all x1, waiting for transfers between devices, body(): share = lax.all_to_all(share, CHIP_COL, 0, 0, tiled=True)  8.01 us
  transfers between devices with their start and end apart: 8, of which 5 were waited for; matrix products, arithmetic and copies ran while one was open for 3% of the time, Pallas kernels for 0%

profile of v2, /device:TPU:1, one launch (start us, length us, event | category | flops | bytes accessed | tf_op | source)
XLA Modules:
  0.0 146.3 jit_solution(10664945969886196361)
XLA Ops:
  1.4 0.9 copy.139
  2.3 1.3 collective-permute-start.1
  3.7 4.6 %collective-permute-start = (f32[3,16,128]{2,0,1:T(4,128)S(1)}, f32[3,16,128]{2,0,1:T(4,128)S(1)}, u32[]{:S(2)}, u32[]{:S(2)}) collective-permute-start(f32[3,16,128]{2,0,1:T(4,128)S(1)} %pad_maximum_fusion.14), channel_id=1, source_target_pairs={{0,32},{32,64},{64,96},{96,128},{128,160},{160,192},{192,224},{224... | collective-permute-start | bytes 73736 | tf_op jit(solution)/shard_map/ppermute | solution.py:46
  8.2 0.8 slice_bitcast_fusion.21
  9.1 0.9 copy.145
  10.1 8.8 %collective-permute-start.3 = (f32[34,128]{1,0:T(8,128)S(1)}, f32[34,128]{1,0:T(8,128)S(1)}, u32[]{:S(2)}, u32[]{:S(2)}) collective-permute-start(f32[34,128]{1,0:T(8,128)S(1)} %pad_maximum_fusion.20), channel_id=1, source_target_pairs={{1,0},{2,1},{3,2},{4,3},{5,4},{6,5},{7,6},{8,7},{9,8},{10,9},{11,1... | collective-permute-start | bytes 52232 | tf_op jit(solution)/shard_map/ppermute | solution.py:46
  18.9 1.9 %collective-permute-start.2 = (f32[34,128]{1,0:T(8,128)S(1)}, f32[34,128]{1,0:T(8,128)S(1)}, u32[]{:S(2)}, u32[]{:S(2)}) collective-permute-start(f32[34,128]{1,0:T(8,128)S(1)} %pad_maximum_fusion.19), channel_id=1, source_target_pairs={{0,1},{1,2},{2,3},{3,4},{4,5},{5,6},{6,7},{7,8},{8,9},{9,10},{10,1... | collective-permute-start | bytes 52232 | tf_op jit(solution)/shard_map/ppermute | solution.py:46
  20.9 1.1 collective-permute-done.2
  22.1 1.3 concatenate.140
  23.3 1.1 convolution_bitcast_fusion.2
  27.0 21.1 %all-to-all-start = ((f32[256,2,128]{2,1,0:T(2,128)}), f32[256,2,128]{2,1,0:T(2,128)S(1)}, u32[]{:S(2)}, u32[]{:S(2)}) async-start(f32[256,2,128]{2,1,0:T(2,128)} %broadcast_in_dim.93), calls=%async_computation | async-start | bytes 524288 | tf_op jit(solution)/shard_map/all_to_all | solution.py:167
  49.5 11.4 %all-to-all-done = f32[256,2,128]{2,1,0:T(2,128)S(1)} async-done(((f32[256,2,128]{2,1,0:T(2,128)}), f32[256,2,128]{2,1,0:T(2,128)S(1)}, u32[]{:S(2)}, u32[]{:S(2)}) %all-to-all-start) | async-done | bytes 262176 | tf_op jit(solution)/shard_map/all_to_all | solution.py:167
  60.9 7.0 %all_gather.9 = f32[512,2,128]{2,1,0:T(2,128)S(1)} all-gather(f32[256,2,128]{2,1,0:T(2,128)S(1)} %all-to-all-done), channel_id=1, replica_groups=mesh['y'=8,'xl'=2,'xh'=2,'z'=8,'c'=2] {'c'}, dimensions={0}, use_global_device_ids=true | all-gather | bytes 786432 | tf_op jit(solution)/shard_map/all_gather | solution.py:168
  67.9 1.4 fusion.131
  69.7 1.0 multiply_reduce_fusion
  77.0 4.4 %all_to_all.25 = f32[512,1,384]{2,1,0:T(1,128)S(1)} all-to-all(f32[512,1,384]{2,1,0:T(1,128)S(1)} %pad_maximum_fusion), channel_id=1, replica_groups=mesh['y'=8,'xl'=2,'xh'=2,'z'=8,'c'=2] {'c'}, dimensions={0} | all-to-all | bytes 1572864 | tf_op jit(solution)/shard_map/all_to_all | solution.py:192
  81.3 1.1 slice_add_fusion
  82.5 9.5 %all-to-all-start.2 = ((f32[256,1,384]{2,1,0:T(1,128)}), f32[256,1,384]{2,1,0:T(1,128)S(1)}, u32[]{:S(2)}, u32[]{:S(2)}) async-start(f32[256,1,384]{2,1,0:T(1,128)} %slice_add_fusion), calls=%async_computation.2 | async-start | bytes 786432 | tf_op jit(solution)/shard_map/all_to_all | solution.py:194
  92.5 16.6 %all-to-all-done.2 = f32[256,1,384]{2,1,0:T(1,128)S(1)} async-done(((f32[256,1,384]{2,1,0:T(1,128)}), f32[256,1,384]{2,1,0:T(1,128)S(1)}, u32[]{:S(2)}, u32[]{:S(2)}) %all-to-all-start.2) | async-done | bytes 393248 | tf_op jit(solution)/shard_map/all_to_all | solution.py:194
  111.2 3.5 %all-to-all-start.3 = ((f32[16,16,128]{2,1,0:T(8,128)}), f32[16,16,128]{2,1,0:T(8,128)S(1)}, u32[]{:S(2)}, u32[]{:S(2)}) async-start(f32[16,16,128]{2,1,0:T(8,128)} %broadcast_in_dim.95), calls=%async_computation.3 | async-start | bytes 262144 | tf_op jit(solution)/shard_map/all_to_all | solution.py:211
  115.0 8.2 %all-to-all-done.3 = f32[16,16,128]{2,1,0:T(8,128)S(1)} async-done(((f32[16,16,128]{2,1,0:T(8,128)}), f32[16,16,128]{2,1,0:T(8,128)S(1)}, u32[]{:S(2)}, u32[]{:S(2)}) %all-to-all-start.3) | async-done | bytes 131104 | tf_op jit(solution)/shard_map/all_to_all | solution.py:211
  124.1 3.5 %all-to-all-start.4 = ((f32[16,32,128]{2,1,0:T(8,128)}), f32[16,32,128]{2,1,0:T(8,128)S(1)}, u32[]{:S(2)}, u32[]{:S(2)}) async-start(f32[16,32,128]{2,1,0:T(8,128)} %broadcast_in_dim.97), calls=%async_computation.4 | async-start | bytes 524288 | tf_op jit(solution)/shard_map/all_to_all | solution.py:219
  128.9 8.0 %all-to-all-done.4 = f32[16,32,128]{2,1,0:T(8,128)S(1)} async-done(((f32[16,32,128]{2,1,0:T(8,128)}), f32[16,32,128]{2,1,0:T(8,128)S(1)}, u32[]{:S(2)}, u32[]{:S(2)}) %all-to-all-start.4) | async-done | bytes 262176 | tf_op jit(solution)/shard_map/all_to_all | solution.py:219
  136.9 6.1 %all-gather = f32[32,32,128]{2,1,0:T(8,128)S(1)} all-gather(f32[16,32,128]{2,1,0:T(8,128)S(1)} %all-to-all-done.4), channel_id=2, replica_groups=mesh['y'=8,'xl'=2,'xh'=2,'z'=8,'c'=2] {'c'}, dimensions={0}, use_global_device_ids=true | all-gather | bytes 786432 | tf_op jit(solution)/shard_map/all_gather | solution.py:220
  (164 shorter events, 19.2 us)
Async XLA Ops:
  0.6 47.9 %copy-start = (f32[128,128]{1,0:T(8,128)S(1)}, f32[128,128]{1,0:T(8,128)}, u32[]{:S(2)}) copy-start(f32[128,128]{1,0:T(8,128)} %param.10) | copy-start | bytes 196612
  0.6 23.8 %copy-start.2 = (f32[128,128]{1,0:T(8,128)S(1)}, f32[128,128]{1,0:T(8,128)}, u32[]{:S(2)}) copy-start(f32[128,128]{1,0:T(8,128)} %param.12) | copy-start | bytes 196612
  2.3 7.6 %collective-permute-start.1 = (f32[3,16,128]{2,0,1:T(4,128)S(1)}, f32[3,16,128]{2,0,1:T(4,128)S(1)}, u32[]{:S(2)}, u32[]{:S(2)}) collective-permute-start(f32[3,16,128]{2,0,1:T(4,128)S(1)} %pad_maximum_fusion.15), channel_id=1, source_target_pairs={{32,0},{64,32},{96,64},{128,96},{160,128},{192,160},{224,192},{256... | collective-permute-start | bytes 73736 | tf_op jit(solution)/shard_map/ppermute | solution.py:46
  3.7 6.3 %collective-permute-start = (f32[3,16,128]{2,0,1:T(4,128)S(1)}, f32[3,16,128]{2,0,1:T(4,128)S(1)}, u32[]{:S(2)}, u32[]{:S(2)}) collective-permute-start(f32[3,16,128]{2,0,1:T(4,128)S(1)} %pad_maximum_fusion.14), channel_id=1, source_target_pairs={{0,32},{32,64},{64,96},{96,128},{128,160},{160,192},{192,224},{224... | collective-permute-start | bytes 73736 | tf_op jit(solution)/shard_map/ppermute | solution.py:46
  10.1 10.7 %collective-permute-start.3 = (f32[34,128]{1,0:T(8,128)S(1)}, f32[34,128]{1,0:T(8,128)S(1)}, u32[]{:S(2)}, u32[]{:S(2)}) collective-permute-start(f32[34,128]{1,0:T(8,128)S(1)} %pad_maximum_fusion.20), channel_id=1, source_target_pairs={{1,0},{2,1},{3,2},{4,3},{5,4},{6,5},{7,6},{8,7},{9,8},{10,9},{11,1... | collective-permute-start | bytes 52232 | tf_op jit(solution)/shard_map/ppermute | solution.py:46
  18.9 3.1 %collective-permute-start.2 = (f32[34,128]{1,0:T(8,128)S(1)}, f32[34,128]{1,0:T(8,128)S(1)}, u32[]{:S(2)}, u32[]{:S(2)}) collective-permute-start(f32[34,128]{1,0:T(8,128)S(1)} %pad_maximum_fusion.19), channel_id=1, source_target_pairs={{0,1},{1,2},{2,3},{3,4},{4,5},{5,6},{6,7},{7,8},{8,9},{9,10},{10,1... | collective-permute-start | bytes 52232 | tf_op jit(solution)/shard_map/ppermute | solution.py:46
  24.7 24.1 %copy-start.5 = (f32[128,192]{0,1:T(8,128)}, f32[128,192]{0,1:T(8,128)S(1)}, u32[]{:S(2)}) copy-start(f32[128,192]{0,1:T(8,128)S(1)} %convolution_bitcast_fusion) | copy-start | bytes 294916
  25.0 23.9 %copy-start.4 = (f32[128,192]{0,1:T(8,128)}, f32[128,192]{0,1:T(8,128)S(1)}, u32[]{:S(2)}) copy-start(f32[128,192]{0,1:T(8,128)S(1)} %convolution_bitcast_fusion.1) | copy-start | bytes 294916
  25.3 23.5 %copy-start.1 = (f32[128,128]{1,0:T(8,128)S(1)}, f32[128,128]{1,0:T(8,128)}, u32[]{:S(2)}) copy-start(f32[128,128]{1,0:T(8,128)} %param.11) | copy-start | bytes 196612
  27.0 34.0 %all-to-all-start = ((f32[256,2,128]{2,1,0:T(2,128)}), f32[256,2,128]{2,1,0:T(2,128)S(1)}, u32[]{:S(2)}, u32[]{:S(2)}) async-start(f32[256,2,128]{2,1,0:T(2,128)} %broadcast_in_dim.93), calls=%async_computation | async-start | bytes 524288 | tf_op jit(solution)/shard_map/all_to_all | solution.py:167
  67.9 1.7 %slice-start = ((f32[128,192]{0,1:T(8,128)}), f32[128,64]{0,1:T(8,128)S(1)}, s32[]{:S(2)}) async-start(f32[128,192]{0,1:T(8,128)} %copy-done.4), calls=%async_computation.5 | async-start | bytes 65536 | tf_op jit(solution)/shard_map/slice | solution.py:106
  67.9 1.8 %slice-start.1 = ((f32[128,192]{0,1:T(8,128)}), f32[128,64]{0,1:T(8,128)S(1)}, s32[]{:S(2)}) async-start(f32[128,192]{0,1:T(8,128)} %copy-done.5), calls=%async_computation.6 | async-start | bytes 65536 | tf_op jit(solution)/shard_map/slice | solution.py:106
  81.3 29.0 %copy-start.3 = (f32[8,16,128]{2,1,0:T(8,128)S(1)}, f32[8,16,128]{2,1,0:T(8,128)}, u32[]{:S(2)}) copy-start(f32[8,16,128]{2,1,0:T(8,128)} %param.8) | copy-start | bytes 196612
  81.3 29.0 %copy-start.6 = (f32[8,16,128]{2,1,0:T(8,128)S(1)}, f32[8,16,128]{2,1,0:T(8,128)}, u32[]{:S(2)}) copy-start(f32[8,16,128]{2,1,0:T(8,128)} %param.7) | copy-start | bytes 196612
  82.5 32.3 %copy-start.7 = (f32[128,128]{1,0:T(8,128)S(1)}, f32[128,128]{1,0:T(8,128)}, u32[]{:S(2)}) copy-start(f32[128,128]{1,0:T(8,128)} %param.13) | copy-start | bytes 196612
  82.5 26.6 %all-to-all-start.2 = ((f32[256,1,384]{2,1,0:T(1,128)}), f32[256,1,384]{2,1,0:T(1,128)S(1)}, u32[]{:S(2)}, u32[]{:S(2)}) async-start(f32[256,1,384]{2,1,0:T(1,128)} %slice_add_fusion), calls=%async_computation.2 | async-start | bytes 786432 | tf_op jit(solution)/shard_map/all_to_all | solution.py:194
  111.2 12.0 %all-to-all-start.3 = ((f32[16,16,128]{2,1,0:T(8,128)}), f32[16,16,128]{2,1,0:T(8,128)S(1)}, u32[]{:S(2)}, u32[]{:S(2)}) async-start(f32[16,16,128]{2,1,0:T(8,128)} %broadcast_in_dim.95), calls=%async_computation.3 | async-start | bytes 262144 | tf_op jit(solution)/shard_map/all_to_all | solution.py:211
  124.1 12.8 %all-to-all-start.4 = ((f32[16,32,128]{2,1,0:T(8,128)}), f32[16,32,128]{2,1,0:T(8,128)S(1)}, u32[]{:S(2)}, u32[]{:S(2)}) async-start(f32[16,32,128]{2,1,0:T(8,128)} %broadcast_in_dim.97), calls=%async_computation.4 | async-start | bytes 524288 | tf_op jit(solution)/shard_map/all_to_all | solution.py:219

commit v3 on v0

v3 whole, which is shorter than its diff:
```python
import functools

import jax
import jax.numpy as jnp
from jax import lax
from jax.experimental import pallas as pl
from jax.experimental.pallas import tpu as pltpu
from jax.sharding import Mesh, PartitionSpec as P

HEADS = 2
POOL = 32
ROW = ("y", "xl")
COL = ("xh", "z", "c")
CHIP_COL = ("xh", "z")
CHIPS = CHIP_COL + ROW
ROWS, COLS, CHANNELS = 8, 16, 128
CELLS, WIN_ROWS = 2, 4
COUNT = ROWS * COLS
WIDE = COLS + 2
USED = 2 * WIDE + 2 * ROWS
RING = 64
WIDTH = CHANNELS // HEADS
SCALE = WIDTH ** (-0.5)
BOTH = ((1,), (1,))
FIRST = ((0,), (0,))


def product(left, right, dims=((1,), (0,)), precision=lax.Precision.HIGHEST):
    return lax.dot_general(
        left, right, (dims, ((), ())), precision=precision, preferred_element_type=jnp.float32
    )


def normalize(values_in):
    average = jnp.mean(values_in, -1, keepdims=True)
    centered = values_in - average
    inv_std = lax.rsqrt(jnp.mean(centered * centered, -1, keepdims=True) + 1e-06)
    return (centered * inv_std, inv_std)


def norm_back(gradient, normed, inv_std):
    return inv_std * (
        gradient
        - jnp.mean(gradient, -1, keepdims=True)
        - normed * jnp.mean(gradient * normed, -1, keepdims=True)
    )


def f32(*shape):
    return jax.ShapeDtypeStruct(shape, jnp.float32)


def call(kernel, outs, *args, scratch=(), scalars=0, flops=1 << 20):
    in_vmem = pl.BlockSpec(memory_space=pltpu.VMEM)
    specs = [pl.BlockSpec(memory_space=pltpu.SMEM)] * scalars + [in_vmem] * (len(args) - scalars)
    return pl.pallas_call(
        kernel,
        out_shape=outs,
        in_specs=specs,
        out_specs=[in_vmem] * len(outs),
        scratch_shapes=[pltpu.VMEM(shape, jnp.float32) for shape in scratch],
        compiler_params=pltpu.CompilerParams(vmem_limit_bytes=48 << 20),
        cost_estimate=pl.CostEstimate(flops=flops, bytes_accessed=1 << 20, transcendentals=0),
    )(*args)


def neighbours(low_side, high_side, axis):
    peers = lax.axis_size(axis)
    up = [(i, i + 1) for i in range(peers - 1)]
    down = [(i + 1, i) for i in range(peers - 1)]
    return lax.ppermute(high_side, axis, up), lax.ppermute(low_side, axis, down)


def mix_kernel(
    tokens, grad, above, below, before, after, weight,
    message, pooled_out, padded, mixed_out, normed_out, inv_out, grad_out,
    normed_ext, inv_ext, mixed_ext,
):
    padded[2 : 2 + ROWS, 2 : 2 + COLS] = tokens[...]
    padded[0:2, 2 : 2 + COLS] = above[0:2]
    padded[2 + ROWS : 4 + ROWS, 2 : 2 + COLS] = below[0:2]
    tall = ROWS + 4
    for r in range(tall):
        for k in range(2):
            at = k * tall + r
            padded[r, k : k + 1] = before[at : at + 1]
            padded[r, 2 + COLS + k : 3 + COLS + k] = after[at : at + 1]
    mixed = padded[1 : ROWS + 3, 1 : 1 + WIDE]
    for i in range(3):
        for j in range(3):
            mixed = mixed + weight[i, j : j + 1][None] * padded[i : i + ROWS + 2, j : j + WIDE]
    normed, inv_std = normalize(mixed)
    mixed_ext[:, 0:WIDE] = mixed
    normed_ext[:, 0:WIDE] = normed
    inv_ext[:, 0:WIDE] = jnp.broadcast_to(inv_std, normed.shape)
    inner = normed_ext[1 : 1 + ROWS, 1 : 1 + COLS]
    for cell in range(CELLS):
        window = jnp.sum(inner[cell * WIN_ROWS : (cell + 1) * WIN_ROWS], 0)
        pooled = jnp.sum(window, 0, keepdims=True) * (1.0 / (WIN_ROWS * COLS))
        pooled_n, pooled_inv = normalize(pooled)
        pooled_out[cell : cell + 1] = pooled_n
        pooled_out[CELLS + cell : CELLS + cell + 1] = jnp.broadcast_to(pooled_inv, pooled_n.shape)
    message[...] = jnp.broadcast_to(pooled_out[0:CELLS][None], message.shape)
    mixed_out[...] = mixed_ext[1 : 1 + ROWS, 1 : 1 + COLS]
    for ext, out in ((normed_ext, normed_out), (inv_ext, inv_out)):
        out[0:COUNT] = ext[1 : 1 + ROWS, 1 : 1 + COLS].reshape(COUNT, CHANNELS)
        out[COUNT : COUNT + WIDE] = ext[0, 0:WIDE]
        out[COUNT + WIDE : COUNT + 2 * WIDE] = ext[ROWS + 1, 0:WIDE]
        for r in range(ROWS):
            left = COUNT + 2 * WIDE + r
            out[left : left + 1] = ext[1 + r, 0:1]
            out[left + ROWS : left + ROWS + 1] = ext[1 + r, WIDE - 1 : WIDE]
        out[COUNT + USED :] = jnp.zeros((RING - USED, CHANNELS), jnp.float32)
    low = 2 * tall
    high = low + ROWS + 1
    grad_out[0:COUNT] = grad[...].reshape(COUNT, CHANNELS)
    for start, middle, at in ((COUNT, above, low), (COUNT + WIDE, below, high)):
        grad_out[start : start + 1] = before[at : at + 1]
        grad_out[start + 1 : start + 1 + COLS] = middle[2]
        grad_out[start + 1 + COLS : start + WIDE] = after[at : at + 1]
    left = COUNT + 2 * WIDE
    grad_out[left : left + ROWS] = before[low + 1 : high]
    grad_out[left + ROWS : left + 2 * ROWS] = after[low + 1 : high]
    grad_out[COUNT + USED :] = jnp.zeros((RING - USED, CHANNELS), jnp.float32)


def halves(value):
    high = value.astype(jnp.bfloat16)
    return high, (value - high.astype(jnp.float32)).astype(jnp.bfloat16)


def three_pass(left, right, dims=((1,), (0,))):
    (left_high, left_low), (right_high, right_low) = left, right
    part = functools.partial(product, dims=dims, precision=lax.Precision.DEFAULT)
    return part(left_high, right_high) + (part(left_high, right_low) + part(left_low, right_high))


def attend_kernel(
    core, keys_ref, to_keys, to_values, query_t, d_att_t, normed_t, grad_t, w_key, w_value,
    own_out, mate_out, att_out, dq_out, ring_out,
):
    own = core[0] * (keys_ref.shape[0] // 2)
    mate = keys_ref.shape[0] // 2 - own
    quarter = keys_ref.shape[0] // 4
    keys = jnp.concatenate(
        [
            keys_ref[pl.ds(start, quarter, stride=2)]
            for start in (own, own + 1, mate, mate + 1)
        ]
    )
    wide = HEADS * COUNT
    query_keys, d_att_values = to_keys[...], to_values[...]
    scores = product(keys, query_keys)
    weights = jnp.exp(scores - jnp.max(scores, 0, keepdims=True))
    probs = weights * (1.0 / jnp.sum(weights, 0, keepdims=True))
    keys_split = halves(keys)
    keys_t = halves(keys.T)
    values_split = halves(d_att_values)
    d_probs = three_pass(keys_split, values_split)
    d_scores = probs * (d_probs - jnp.sum(d_probs * probs, 0, keepdims=True))
    probs_split, d_split = halves(probs), halves(d_scores)
    att_keys = three_pass(keys_t, probs_split)
    d_query_keys = three_pass(keys_t, d_split)

    def inner(pair):
        return tuple(x[:, :wide] for x in pair)

    sums = three_pass(inner(d_split), inner(halves(query_keys)), BOTH) + three_pass(
        inner(probs_split), inner(values_split), BOTH
    )
    upper = lax.broadcasted_iota(jnp.int32, (CHANNELS, CHANNELS), 0) < WIDTH
    left = lax.broadcasted_iota(jnp.int32, (CHANNELS, CHANNELS), 1) < WIDTH

    def heads(first, second, mask=upper):
        return jnp.where(mask, first, second)

    z0, z1 = att_keys[:, :COUNT], att_keys[:, COUNT:wide]
    y0, y1 = d_query_keys[:, :COUNT], d_query_keys[:, COUNT:wide]
    att_t = heads(product(w_value[...], z0, FIRST), product(w_value[...], z1, FIRST))
    dq_t = heads(product(w_key[...], y0, FIRST), product(w_key[...], y1, FIRST)) * SCALE
    q, a = query_t[...], d_att_t[...]
    g_query = product(normed_t[...], dq_t, BOTH)
    g_key = heads(product(y0, q, BOTH), product(y1, q, BOTH), left) * SCALE
    g_value = heads(product(z0, a, BOTH), product(z1, a, BOTH), left)
    g_out = product(att_t, grad_t[...], BOTH)
    att_out[...] = att_t
    dq_out[...] = dq_t
    ring_out[...] = d_query_keys[:, wide:]
    first = core[0] == 0
    by_core = ((g_query, g_key), (g_value, g_out))
    for half in range(2):
        at = half * CHANNELS
        zero, one = by_core[0][half], by_core[1][half]
        own_out[at : at + CHANNELS, 2 * CHANNELS :] = jnp.where(first, zero, one)
        mate_out[at : at + CHANNELS, 2 * CHANNELS :] = jnp.where(first, one, zero)
    own_out[:, :CHANNELS] = sums[:quarter]
    own_out[:, CHANNELS : 2 * CHANNELS] = sums[quarter : 2 * quarter]
    mate_out[:, :CHANNELS] = sums[2 * quarter : 3 * quarter]
    mate_out[:, CHANNELS : 2 * CHANNELS] = sums[3 * quarter :]


def middle_kernel(sums, pooled, d_normed, normed, inv, grad, padded, d_mixed_out, message, share):
    window = float(WIN_ROWS * COLS)
    share[...] = jnp.zeros(share.shape, jnp.float32)
    half = WIN_ROWS * COLS
    for cell in range(CELLS):
        part = slice(cell * CHANNELS, (cell + 1) * CHANNELS)
        d_pooled = norm_back(
            sums[:, part], pooled[cell : cell + 1], pooled[CELLS + cell : CELLS + cell + 1]
        )
        d_pooled = d_pooled * (1.0 / window)
        share[cell : cell + 1] = d_pooled
        rows = slice(cell * half, (cell + 1) * half)
        back = norm_back(d_normed[rows] + d_pooled, normed[rows], inv[rows])
        back = grad[rows] + back
        d_mixed_out[cell * WIN_ROWS : (cell + 1) * WIN_ROWS] = back.reshape(
            WIN_ROWS, COLS, CHANNELS
        )
    share[CELLS : CELLS + 1] = sums[:, CELLS * CHANNELS :]
    d_mixed = d_mixed_out[...]
    for i in range(3):
        for j in range(3):
            products = padded[1 + i : 1 + i + ROWS, 1 + j : 1 + j + COLS] * d_mixed
            at = CELLS + 1 + 3 * i + j
            share[at : at + 1] = jnp.sum(jnp.sum(products, 0), 0, keepdims=True)
    message[...] = jnp.broadcast_to(share[...][None], message.shape)


def relay_kernel(place, received, message, share):
    peers = received.shape[0]
    row = place[0]
    for k in range(peers):
        share[k : k + 1] = received[k, CELLS : CELLS + 1]
    total = received[0]
    for k in range(1, peers):
        total = total + received[k]
    share[peers : peers + 9] = total[CELLS + 1 : CELLS + 10]
    for d in range(3):
        at = peers + 9 + d * CELLS
        share[at : at + CELLS] = received[jnp.clip(row + d - 1, 0, peers - 1), 0:CELLS]
    share[31:32] = jnp.zeros((1, CHANNELS), jnp.float32)
    message[...] = jnp.broadcast_to(share[...][None], message.shape)


def end_kernel(
    row_count, col_count, place, near, d_normed, normed, inv, grad, d_mixed, weight,
    d_tokens, g_conv, g_query, g_key, g_value, g_out,
    ring, padded,
):
    row, col = place[0], place[1]
    cores, lines = near.shape[0], near.shape[1]
    first = row_count + 9

    def owner(d_row, d_col, cell):
        k = jnp.clip(col + d_col, 0, col_count - 1)
        at = first + (d_row + 1) * CELLS + cell
        return near[k % 2, k // 2, at : at + 1]

    for start, d_row, cell in ((0, -1, CELLS - 1), (WIDE, 1, 0)):
        ring[start : start + 1] = owner(d_row, -1, cell)
        ring[start + 1 : start + 1 + COLS] = jnp.broadcast_to(
            owner(d_row, 0, cell), (COLS, CHANNELS)
        )
        ring[start + 1 + COLS : start + WIDE] = owner(d_row, 1, cell)
    for start, d_col in ((2 * WIDE, -1), (2 * WIDE + ROWS, 1)):
        for cell in range(CELLS):
            at = start + cell * WIN_ROWS
            ring[at : at + WIN_ROWS] = jnp.broadcast_to(
                owner(0, d_col, cell), (WIN_ROWS, CHANNELS)
            )
    ring[USED:] = jnp.zeros((RING - USED, CHANNELS), jnp.float32)
    back = norm_back(d_normed[...] + ring[...], normed[COUNT:], inv[COUNT:])
    back = grad[COUNT:] + back
    at = lax.broadcasted_iota(jnp.int32, (RING, CHANNELS), 0)
    top, bottom = at < WIDE, (at >= WIDE) & (at < 2 * WIDE)
    left = ((at >= 2 * WIDE) & (at < 2 * WIDE + ROWS)) | (at == 0) | (at == WIDE)
    right = (at >= 2 * WIDE + ROWS) | (at == WIDE - 1) | (at == 2 * WIDE - 1)
    outside = (
        (top & (row == 0))
        | (bottom & (row == row_count - 1))
        | (left & (col == 0))
        | (right & (col == col_count - 1))
    )
    ring[...] = jnp.where(outside, 0.0, back)
    padded[0, 0:WIDE] = ring[0:WIDE]
    padded[ROWS + 1, 0:WIDE] = ring[WIDE : 2 * WIDE]
    for r in range(ROWS):
        k = 2 * WIDE + r
        padded[1 + r, 0:1] = ring[k : k + 1]
        padded[1 + r, WIDE - 1 : WIDE] = ring[k + ROWS : k + ROWS + 1]
    padded[1 : 1 + ROWS, 1 : 1 + COLS] = d_mixed[...]
    total = d_mixed[...]
    for i in range(3):
        for j in range(3):
            total = (
                total
                + weight[i, j : j + 1][None]
                * padded[2 - i : 2 - i + ROWS, 2 - j : 2 - j + COLS]
            )
    d_tokens[...] = total
    root = float(COUNT * row_count * col_count) ** (-0.5)
    conv = near[0, 0, row_count:first]
    for k in range(1, cores * lines):
        conv = conv + near[k // lines, k % lines, row_count:first]
    conv = conv * root
    for k in range(9):
        g_conv[k // 3, k % 3 : k % 3 + 1] = conv[k : k + 1]
    blocks = ((g_query, root), (g_key, 1.0 / POOL), (g_value, 1.0 / POOL), (g_out, root))
    for k in range(cores * lines):
        out, factor = blocks[k * row_count // CHANNELS]
        at = k * row_count % CHANNELS
        out[at : at + row_count] = near[k // lines, k % lines, 0:row_count] * factor


def body(tokens, cotangent, conv_weight, w_query, w_key, w_value, w_out):
    row_count, col_count = lax.axis_size(ROW), lax.axis_size(COL)
    chips, lines = lax.axis_size(CHIPS), lax.axis_size(CHIP_COL)
    place = jnp.stack([lax.axis_index(ROW), lax.axis_index(COL), lax.axis_index("c")])
    tile = (ROWS, COLS, CHANNELS)
    square = (CHANNELS, CHANNELS)
    all_tokens = (COUNT + RING, CHANNELS)

    low = jnp.concatenate([tokens[:2], cotangent[:1]])
    high = jnp.concatenate([tokens[-2:], cotangent[-1:]])
    above, below = neighbours(low, high, ROW)

    def side(first_t, first_g):
        parts = []
        for k in (first_t, first_t + 1):
            parts += [above[:2, k], tokens[:, k], below[:2, k]]
        return jnp.concatenate(
            parts + [above[2:, first_g], cotangent[:, first_g], below[2:, first_g]]
        )

    before, after = neighbours(side(0, 0), side(COLS - 2, COLS - 1), COL)
    message, pooled, padded, mixed, normed, inv_std, grad = call(
        mix_kernel,
        [
            f32(chips, CELLS, CHANNELS),
            f32(2 * CELLS, CHANNELS),
            f32(ROWS + 4, 24, CHANNELS),
            f32(*tile),
            f32(*all_tokens),
            f32(*all_tokens),
            f32(*all_tokens),
        ],
        tokens, cotangent, above, below, before, after, conv_weight,
        scratch=[(ROWS + 2, 24, CHANNELS)] * 3,
    )

    message = lax.all_to_all(message, CHIPS, 0, 0, tiled=True)
    keys = lax.all_gather(message, "c", axis=0, tiled=True).reshape(-1, CHANNELS)

    normed_t, grad_t = normed.T, grad.T
    query_t = product(w_query, normed_t, FIRST)
    d_att_t = product(w_out, grad_t)
    to_keys, to_values = [], []
    for head in range(HEADS):
        part = slice(head * WIDTH, (head + 1) * WIDTH)
        to_keys.append(product(w_key[:, part], query_t[part]) * SCALE)
        to_values.append(product(w_value[:, part], d_att_t[part]))

    def columns(by_head):
        return jnp.concatenate([x[:, :COUNT] for x in by_head] + [x[:, COUNT:] for x in by_head], 1)

    own, mate, att_t, dq_t, ring_keys = call(
        attend_kernel,
        [
            f32(chips, 3 * CHANNELS),
            f32(chips, 3 * CHANNELS),
            f32(*square),
            f32(*square),
            f32(CHANNELS, HEADS * RING),
        ],
        place[2:], keys, columns(to_keys), columns(to_values), query_t[:, :COUNT],
        d_att_t[:, :COUNT], normed_t[:, :COUNT], grad_t[:, :COUNT], w_key, w_value,
        scalars=1, flops=1 << 31,
    )

    received = lax.ppermute(mate, "c", [(0, 1), (1, 0)])
    sums = (own + received).reshape(chips, 1, 3 * CHANNELS)
    sums = jnp.sum(lax.all_to_all(sums, CHIPS, 0, 0, tiled=True), 0)

    output = mixed + product(att_t, w_out, FIRST).reshape(tile)
    d_normed = product(dq_t, w_query, ((0,), (1,)))
    dq_ring = [
        product(
            w_key[:, head * WIDTH : (head + 1) * WIDTH],
            ring_keys[:, head * RING : (head + 1) * RING],
            FIRST,
        )
        for head in range(HEADS)
    ]
    d_ring = product(jnp.concatenate(dq_ring) * SCALE, w_query, ((0,), (1,)))

    d_mixed, message = call(
        middle_kernel,
        [f32(*tile), f32(row_count, 16, CHANNELS)],
        sums, pooled, d_normed, normed, inv_std, grad, padded,
        scratch=[(16, CHANNELS)],
    )
    message = lax.all_to_all(message, ROW, 0, 0, tiled=True)
    (message,) = call(
        relay_kernel,
        [f32(lines, 32, CHANNELS)],
        place, message,
        scratch=[(32, CHANNELS)], scalars=1,
    )
    message = lax.all_to_all(message, CHIP_COL, 0, 0, tiled=True)
    near = lax.all_gather(message, "c", axis=0)
    results = call(
        functools.partial(end_kernel, row_count, col_count),
        [f32(*tile), f32(3, 3, CHANNELS)] + [f32(*square)] * 4,
        place, near, d_ring, normed, inv_std, grad, d_mixed, conv_weight,
        scratch=[(RING, CHANNELS), (ROWS + 2, 24, CHANNELS)], scalars=1,
    )
    return (output, *results)


def solution(mesh):
    fine = Mesh(mesh.devices.reshape(8, 2, 2, 8, 2), ("y", "xl", "xh", "z", "c"))
    tile = P(ROW, COL, None)
    return jax.shard_map(
        body,
        mesh=fine,
        in_specs=(tile, tile, P(), P(), P(), P(), P()),
        out_specs=(tile, tile, P(), P(), P(), P(), P()),
        check_vma=False,
    )
```

time: 1390 us -> 140 us (0.10)
  blocking collectives: 788 us -> 9.25 us
  waiting for transfers between devices: 527 us -> 50.4 us
  starting transfers between devices: 25.6 us -> 55.5 us
  matrix products: 19.7 us -> 3.27 us
    all_gather x1 -> x2, blocking collectives: 689 us -> 9.25 us  [the longest x1 6.11 us: body(): near = lax.all_gather(message, 'c', axis=0)]
    psum x1 -> x0, waiting for transfers between devices: 266 us -> none  [body(): lax.psum((grad_conv, grad_query, grad_key, grad_value, grad_out), ('row',...]
    unnamed x3 -> x0, waiting for transfers between devices: 260 us -> none
    psum x1 -> x0, blocking collectives: 98.4 us -> none  [body(): lax.psum((grad_conv, grad_query, grad_key, grad_value, grad_out), ('row',...]
    all_to_all x0 -> x4, waiting for transfers between devices: none -> 43.4 us  [the longest x1 17 us: body(): sums = jnp.sum(lax.all_to_all(sums, CHIPS, 0, 0, tiled=True), 0)]
    all_to_all x0 -> x4, starting transfers between devices: none -> 39.3 us  [the longest x1 22.9 us: body(): message = lax.all_to_all(message, CHIPS, 0, 0, tiled=True)]
    dot_general x24 -> x11, matrix products: 19.7 us -> 3.27 us  [product(): lax.dot_general(left, right, (dims, ((), ())), precision=precision, prefe...]
  transfers between devices with their start and end apart: 10 -> 9, of which waited for: 4 -> 7; matrix products, arithmetic and copies ran while one was open for 0% -> 3% of each run, Pallas kernels for 0% -> 0%
where the time goes in v3:
time: 140 us; the launch traced here: 139 us
  starting transfers between devices  55.5 us (40%)
  waiting for transfers between devices  50.4 us (36%)
  Pallas kernels  9.85 us (7%)
  blocking collectives  9.25 us (7%)
  local copies, waits for them, and re-layouts  8.07 us (6%)
  matrix products  3.27 us (2%)
    all_to_all x1, starting transfers between devices, body(): message = lax.all_to_all(message, CHIPS, 0, 0, tiled=True)  22.9 us
    all_to_all x1, waiting for transfers between devices, body(): sums = jnp.sum(lax.all_to_all(sums, CHIPS, 0, 0, tiled=True), 0)  17 us
    all_to_all x1, waiting for transfers between devices, body(): message = lax.all_to_all(message, CHIPS, 0, 0, tiled=True)  10.6 us
    ppermute x2, starting transfers between devices, neighbours(): lax.ppermute(high_side, axis, up)  10.1 us
    pallas_call x5, Pallas kernels, call(): pl.pallas_call(kernel, out_shape=outs, in_specs=specs, out_specs=[in_vmem...  9.85 us
    all_to_all x1, starting transfers between devices, body(): sums = jnp.sum(lax.all_to_all(sums, CHIPS, 0, 0, tiled=True), 0)  9.34 us
    all_to_all x1, waiting for transfers between devices, body(): message = lax.all_to_all(message, ROW, 0, 0, tiled=True)  8.14 us
    all_to_all x1, waiting for transfers between devices, body(): message = lax.all_to_all(message, CHIP_COL, 0, 0, tiled=True)  7.69 us
  transfers between devices with their start and end apart: 9, of which 7 were waited for; matrix products, arithmetic and copies ran while one was open for 3% of the time, Pallas kernels for 0%

profile of v3, /device:TPU:1, one launch (start us, length us, event | category | flops | bytes accessed | tf_op | source)
XLA Modules:
  0.0 138.7 jit_solution(17783705897793855817)
XLA Ops:
  2.2 4.1 %collective-permute-start = (f32[3,16,128]{2,0,1:T(4,128)S(1)}, f32[3,16,128]{2,0,1:T(4,128)S(1)}, u32[]{:S(2)}, u32[]{:S(2)}) collective-permute-start(f32[3,16,128]{2,0,1:T(4,128)S(1)} %pad_maximum_fusion.2), channel_id=1, source_target_pairs={{0,32},{32,64},{64,96},{96,128},{128,160},{160,192},{192,224},{224... | collective-permute-start | bytes 73736 | tf_op jit(solution)/shard_map/ppermute | solution.py:71
  6.3 1.3 collective-permute-start.1
  7.7 3.3 %collective-permute-done.1 = f32[3,16,128]{2,0,1:T(4,128)S(1)} collective-permute-done((f32[3,16,128]{2,0,1:T(4,128)S(1)}, f32[3,16,128]{2,0,1:T(4,128)S(1)}, u32[]{:S(2)}, u32[]{:S(2)}) %collective-permute-start.1) | collective-permute-done | bytes 24608 | tf_op jit(solution)/shard_map/ppermute | solution.py:71
  11.3 6.0 %collective-permute-start.2 = (f32[34,128]{1,0:T(8,128)S(1)}, f32[34,128]{1,0:T(8,128)S(1)}, u32[]{:S(2)}, u32[]{:S(2)}) collective-permute-start(f32[34,128]{1,0:T(8,128)S(1)} %concatenate.23), channel_id=1, source_target_pairs={{0,1},{1,2},{2,3},{3,4},{4,5},{5,6},{6,7},{7,8},{8,9},{9,10},{10,1... | collective-permute-start | bytes 52232 | tf_op jit(solution)/shard_map/ppermute | solution.py:71
  17.6 2.6 %collective-permute-start.3 = (f32[34,128]{1,0:T(8,128)S(1)}, f32[34,128]{1,0:T(8,128)S(1)}, u32[]{:S(2)}, u32[]{:S(2)}) collective-permute-start(f32[34,128]{1,0:T(8,128)S(1)} %concatenate.24), channel_id=1, source_target_pairs={{1,0},{2,1},{3,2},{4,3},{5,4},{6,5},{7,6},{8,7},{9,8},{10,9},{11,1... | collective-permute-start | bytes 52232 | tf_op jit(solution)/shard_map/ppermute | solution.py:71
  20.3 2.4 %collective-permute-done.3.after = f32[34,128]{1,0:T(8,128)S(1)} collective-permute-done((f32[34,128]{1,0:T(8,128)S(1)}, f32[34,128]{1,0:T(8,128)S(1)}, u32[]{:S(2)}, u32[]{:S(2)}) %collective-permute-start.3) | collective-permute-done | bytes 17440 | tf_op jit(solution)/shard_map/ppermute | solution.py:71
  22.7 1.2 shard_map.126
  26.4 22.9 %all-to-all-start = ((f32[256,2,128]{2,1,0:T(2,128)}), f32[256,2,128]{2,1,0:T(2,128)S(1)}, u32[]{:S(2)}, u32[]{:S(2)}) async-start(f32[256,2,128]{2,1,0:T(2,128)} %get-tuple-element.28), calls=%async_computation | async-start | bytes 524288 | tf_op jit(solution)/shard_map/all_to_all | solution.py:351
  53.7 10.6 %all-to-all-done = f32[256,2,128]{2,1,0:T(2,128)S(1)} async-done(((f32[256,2,128]{2,1,0:T(2,128)}), f32[256,2,128]{2,1,0:T(2,128)S(1)}, u32[]{:S(2)}, u32[]{:S(2)}) %all-to-all-start) | async-done | bytes 262176 | tf_op jit(solution)/shard_map/all_to_all | solution.py:351
  64.3 3.1 %all_gather.9 = f32[512,2,128]{2,1,0:T(2,128)S(1)} all-gather(f32[256,2,128]{2,1,0:T(2,128)S(1)} %all-to-all-done), channel_id=1, replica_groups=mesh['y'=8,'xl'=2,'xh'=2,'z'=8,'c'=2] {'c'}, dimensions={0}, use_global_device_ids=true | all-gather | bytes 786432 | tf_op jit(solution)/shard_map/all_gather | solution.py:352
  67.4 5.1 %shard_map.127 = (f32[256,384]{1,0:T(8,128)S(1)}, f32[256,384]{1,0:T(8,128)S(1)}, f32[128,128]{1,0:T(8,128)S(1)}, f32[128,128]{1,0:T(8,128)S(1)}, f32[128,128]{1,0:T(8,128)S(1)}) custom-call(s32[1]{0:T(128)} %bitcast.20.core, f32[1024,128]{1,0:T(8,128)S(1)} %bitcast.80, f32[128,384]{1,0:T(8,128)S(1)} %get-tuple-element.69.to_keys, ...), custom_call_target="tpu_custom_call" | custom-call | flops 2147483648 | bytes 1048576 | tf_op jit(solution)/shard_map/pallas_call | solution.py:56
  72.6 2.3 %collective-permute-start.4 = (f32[256,384]{1,0:T(8,128)S(1)}, f32[256,384]{1,0:T(8,128)S(1)}, u32[]{:S(2)}, u32[]{:S(2)}) collective-permute-start(f32[256,384]{1,0:T(8,128)S(1)} %get-tuple-element.33), channel_id=1, source_target_pairs={{0,1},{1,0},{2,3},{3,2},{4,5},{5,4},{6,7},{7,6},{8,9},{9,8},{10,11... | collective-permute-start | bytes 1179656 | tf_op jit(solution)/shard_map/ppermute | solution.py:380
  74.9 1.3 collective-permute-done.4
  76.2 1.1 copy.77
  77.4 9.3 %all-to-all-start.1 = ((f32[256,1,384]{2,1,0:T(1,128)}), f32[256,1,384]{2,1,0:T(1,128)S(1)}, u32[]{:S(2)}, u32[]{:S(2)}) async-start(f32[256,1,384]{2,1,0:T(1,128)} %copy.77), calls=%async_computation.1 | async-start | bytes 786432 | tf_op jit(solution)/shard_map/all_to_all | solution.py:382
  87.0 17.0 %all-to-all-done.1 = f32[256,1,384]{2,1,0:T(1,128)S(1)} async-done(((f32[256,1,384]{2,1,0:T(1,128)}), f32[256,1,384]{2,1,0:T(1,128)S(1)}, u32[]{:S(2)}, u32[]{:S(2)}) %all-to-all-start.1) | async-done | bytes 393248 | tf_op jit(solution)/shard_map/all_to_all | solution.py:382
  104.3 0.9 shard_map.128
  105.2 3.5 %all-to-all-start.2 = ((f32[16,16,128]{2,1,0:T(8,128)}), f32[16,16,128]{2,1,0:T(8,128)S(1)}, u32[]{:S(2)}, u32[]{:S(2)}) async-start(f32[16,16,128]{2,1,0:T(8,128)} %get-tuple-element.38), calls=%async_computation.2 | async-start | bytes 262144 | tf_op jit(solution)/shard_map/all_to_all | solution.py:402
  109.1 8.1 %all-to-all-done.2.received = f32[16,16,128]{2,1,0:T(8,128)S(1)} async-done(((f32[16,16,128]{2,1,0:T(8,128)}), f32[16,16,128]{2,1,0:T(8,128)S(1)}, u32[]{:S(2)}, u32[]{:S(2)}) %all-to-all-start.2) | async-done | bytes 131104 | tf_op jit(solution)/shard_map/all_to_all | solution.py:402
  117.2 1.3 shard_map.129
  118.5 3.5 %all-to-all-start.3 = ((f32[16,32,128]{2,1,0:T(8,128)}), f32[16,32,128]{2,1,0:T(8,128)S(1)}, u32[]{:S(2)}, u32[]{:S(2)}) async-start(f32[16,32,128]{2,1,0:T(8,128)} %shard_map.129), calls=%async_computation.3 | async-start | bytes 524288 | tf_op jit(solution)/shard_map/all_to_all | solution.py:409
  123.6 7.7 %all-to-all-done.3 = f32[16,32,128]{2,1,0:T(8,128)S(1)} async-done(((f32[16,32,128]{2,1,0:T(8,128)}), f32[16,32,128]{2,1,0:T(8,128)S(1)}, u32[]{:S(2)}, u32[]{:S(2)}) %all-to-all-start.3) | async-done | bytes 262176 | tf_op jit(solution)/shard_map/all_to_all | solution.py:409
  131.3 6.1 %all-gather = f32[32,32,128]{2,1,0:T(8,128)S(1)} all-gather(f32[16,32,128]{2,1,0:T(8,128)S(1)} %all-to-all-done.3), channel_id=2, replica_groups=mesh['y'=8,'xl'=2,'xh'=2,'z'=8,'c'=2] {'c'}, dimensions={0}, use_global_device_ids=true | all-gather | bytes 786432 | tf_op jit(solution)/shard_map/all_gather | solution.py:410
  137.4 1.3 shard_map.130
  (79 shorter events, 11.4 us)
Async XLA Ops:
  0.6 48.7 %copy-start = (f32[128,128]{1,0:T(8,128)S(1)}, f32[128,128]{1,0:T(8,128)}, u32[]{:S(2)}) copy-start(f32[128,128]{1,0:T(8,128)} %param.10) | copy-start | bytes 196612
  2.1 5.5 %copy-start.3 = (f32[8,16,128]{2,1,0:T(8,128)S(1)}, f32[8,16,128]{2,1,0:T(8,128)}, u32[]{:S(2)}) copy-start(f32[8,16,128]{2,1,0:T(8,128)} %tokens.1) | copy-start | bytes 196612
  2.2 5.5 %copy-start.4 = (f32[8,16,128]{2,1,0:T(8,128)S(1)}, f32[8,16,128]{2,1,0:T(8,128)}, u32[]{:S(2)}) copy-start(f32[8,16,128]{2,1,0:T(8,128)} %grad.1) | copy-start | bytes 196612
  2.2 5.5 %collective-permute-start = (f32[3,16,128]{2,0,1:T(4,128)S(1)}, f32[3,16,128]{2,0,1:T(4,128)S(1)}, u32[]{:S(2)}, u32[]{:S(2)}) collective-permute-start(f32[3,16,128]{2,0,1:T(4,128)S(1)} %pad_maximum_fusion.2), channel_id=1, source_target_pairs={{0,32},{32,64},{64,96},{96,128},{128,160},{160,192},{192,224},{224... | collective-permute-start | bytes 73736 | tf_op jit(solution)/shard_map/ppermute | solution.py:71
  6.3 4.7 %collective-permute-start.1 = (f32[3,16,128]{2,0,1:T(4,128)S(1)}, f32[3,16,128]{2,0,1:T(4,128)S(1)}, u32[]{:S(2)}, u32[]{:S(2)}) collective-permute-start(f32[3,16,128]{2,0,1:T(4,128)S(1)} %pad_maximum_fusion.3), channel_id=1, source_target_pairs={{32,0},{64,32},{96,64},{128,96},{160,128},{192,160},{224,192},{256... | collective-permute-start | bytes 73736 | tf_op jit(solution)/shard_map/ppermute | solution.py:71
  11.3 8.9 %collective-permute-start.2 = (f32[34,128]{1,0:T(8,128)S(1)}, f32[34,128]{1,0:T(8,128)S(1)}, u32[]{:S(2)}, u32[]{:S(2)}) collective-permute-start(f32[34,128]{1,0:T(8,128)S(1)} %concatenate.23), channel_id=1, source_target_pairs={{0,1},{1,2},{2,3},{3,4},{4,5},{5,6},{6,7},{7,8},{8,9},{9,10},{10,1... | collective-permute-start | bytes 52232 | tf_op jit(solution)/shard_map/ppermute | solution.py:71
  17.6 5.1 %collective-permute-start.3 = (f32[34,128]{1,0:T(8,128)S(1)}, f32[34,128]{1,0:T(8,128)S(1)}, u32[]{:S(2)}, u32[]{:S(2)}) collective-permute-start(f32[34,128]{1,0:T(8,128)S(1)} %concatenate.24), channel_id=1, source_target_pairs={{1,0},{2,1},{3,2},{4,3},{5,4},{6,5},{7,6},{8,7},{9,8},{10,9},{11,1... | collective-permute-start | bytes 52232 | tf_op jit(solution)/shard_map/ppermute | solution.py:71
  20.2 2.5 %copy-start.5 = (f32[3,3,128]{2,1,0:T(4,128)S(1)}, f32[3,3,128]{2,1,0:T(4,128)}, u32[]{:S(2)}) copy-start(f32[3,3,128]{2,1,0:T(4,128)} %weight.3) | copy-start | bytes 13828
  20.2 3.7 %copy-start.10 = (f32[128,128]{1,0:T(8,128)S(1)}, f32[128,128]{1,0:T(8,128)}, u32[]{:S(2)}) copy-start(f32[128,128]{1,0:T(8,128)} %param.13) | copy-start | bytes 196612
  24.3 0.8 copy-start.2
  25.5 0.9 copy-start.6
  26.4 37.9 %all-to-all-start = ((f32[256,2,128]{2,1,0:T(2,128)}), f32[256,2,128]{2,1,0:T(2,128)S(1)}, u32[]{:S(2)}, u32[]{:S(2)}) async-start(f32[256,2,128]{2,1,0:T(2,128)} %get-tuple-element.28), calls=%async_computation | async-start | bytes 524288 | tf_op jit(solution)/shard_map/all_to_all | solution.py:351
  49.7 0.8 copy-start.1
  52.5 0.8 slice-start.4
  52.5 0.9 slice-start.5
  52.5 0.9 slice-start.6
  52.6 0.9 slice-start.2
  52.7 0.9 slice-start.3
  52.7 0.9 slice-start
  52.7 0.9 slice-start.1
  72.6 3.6 %collective-permute-start.4 = (f32[256,384]{1,0:T(8,128)S(1)}, f32[256,384]{1,0:T(8,128)S(1)}, u32[]{:S(2)}, u32[]{:S(2)}) collective-permute-start(f32[256,384]{1,0:T(8,128)S(1)} %get-tuple-element.33), channel_id=1, source_target_pairs={{0,1},{1,0},{2,3},{3,2},{4,5},{5,4},{6,7},{7,6},{8,9},{9,8},{10,11... | collective-permute-start | bytes 1179656 | tf_op jit(solution)/shard_map/ppermute | solution.py:380
  77.4 26.6 %all-to-all-start.1 = ((f32[256,1,384]{2,1,0:T(1,128)}), f32[256,1,384]{2,1,0:T(1,128)S(1)}, u32[]{:S(2)}, u32[]{:S(2)}) async-start(f32[256,1,384]{2,1,0:T(1,128)} %copy.77), calls=%async_computation.1 | async-start | bytes 786432 | tf_op jit(solution)/shard_map/all_to_all | solution.py:382
  105.2 12.0 %all-to-all-start.2 = ((f32[16,16,128]{2,1,0:T(8,128)}), f32[16,16,128]{2,1,0:T(8,128)S(1)}, u32[]{:S(2)}, u32[]{:S(2)}) async-start(f32[16,16,128]{2,1,0:T(8,128)} %get-tuple-element.38), calls=%async_computation.2 | async-start | bytes 262144 | tf_op jit(solution)/shard_map/all_to_all | solution.py:402
  118.5 12.8 %all-to-all-start.3 = ((f32[16,32,128]{2,1,0:T(8,128)}), f32[16,32,128]{2,1,0:T(8,128)S(1)}, u32[]{:S(2)}, u32[]{:S(2)}) async-start(f32[16,32,128]{2,1,0:T(8,128)} %shard_map.129), calls=%async_computation.3 | async-start | bytes 524288 | tf_op jit(solution)/shard_map/all_to_all | solution.py:409
  (4 other events, 2.8 us)

commit v4 on v3

--- a/solution.py
+++ b/solution.py
@@ -60,7 +60,7 @@
         out_specs=[in_vmem] * len(outs),
         scratch_shapes=[pltpu.VMEM(shape, jnp.float32) for shape in scratch],
         compiler_params=pltpu.CompilerParams(vmem_limit_bytes=48 << 20),
-        cost_estimate=pl.CostEstimate(flops=flops, bytes_accessed=1 << 20, transcendentals=0),
+        cost_estimate=pl.CostEstimate(flops=flops, bytes_accessed=flops, transcendentals=0),
     )(*args)
 
 
@@ -124,15 +124,62 @@
     grad_out[COUNT + USED :] = jnp.zeros((RING - USED, CHANNELS), jnp.float32)
 
 
-def halves(value):
-    high = value.astype(jnp.bfloat16)
-    return high, (value - high.astype(jnp.float32)).astype(jnp.bfloat16)
-
-
-def three_pass(left, right, dims=((1,), (0,))):
-    (left_high, left_low), (right_high, right_low) = left, right
-    part = functools.partial(product, dims=dims, precision=lax.Precision.DEFAULT)
-    return part(left_high, right_high) + (part(left_high, right_low) + part(left_low, right_high))
+def edge_kernel(tokens, grad, low, high):
+    low[0:2], low[2] = tokens[0:2], grad[0]
+    high[0:2], high[2] = tokens[ROWS - 2 : ROWS], grad[ROWS - 1]
+
+
+def top_half():
+    return lax.broadcasted_iota(jnp.int32, (CHANNELS, CHANNELS), 0) < WIDTH
+
+
+def before_kernel(
+    normed, grad, w_query, w_key, w_value, w_out,
+    to_keys, to_values, query_t, d_att_t, normed_t, grad_t,
+):
+    upper = top_half()
+
+    def by_head(weight, value, ring, out):
+        for head, mask in enumerate((upper, ~upper)):
+            at = head * COUNT
+            out[:, at : at + COUNT] = product(weight, jnp.where(mask, value, 0.0))
+        parts = [
+            product(weight, jnp.where(mask[:, :RING], ring, 0.0)) for mask in (upper, ~upper)
+        ]
+        out[:, HEADS * COUNT :] = jnp.concatenate(parts, 1)
+
+    inner, ring = normed[0:COUNT].T, normed[COUNT:].T
+    normed_t[...] = inner
+    query = product(w_query[...], inner, FIRST)
+    query_t[...] = query
+    by_head(w_key[...] * SCALE, query, product(w_query[...], ring, FIRST), to_keys)
+    inner, ring = grad[0:COUNT].T, grad[COUNT:].T
+    grad_t[...] = inner
+    d_att = product(w_out[...], inner)
+    d_att_t[...] = d_att
+    by_head(w_value[...], d_att, product(w_out[...], ring), to_values)
+
+
+def after_kernel(att_t, dq_t, ring_keys, mixed, w_query, w_key, w_out, output, d_normed, d_ring):
+    att_out = product(att_t[...], w_out[...], FIRST)
+    output[...] = mixed[...] + att_out.reshape(ROWS, COLS, CHANNELS)
+    back = w_query[...].T
+    d_normed[...] = product(dq_t[...], back, FIRST)
+    ring = product(w_key[...], ring_keys[...], FIRST)
+    ring = jnp.where(top_half()[:, :RING], ring[:, :RING], ring[:, RING:]) * SCALE
+    d_ring[...] = product(ring, back, FIRST)
+
+
+def pieces(value, count):
+    parts = []
+    for _ in range(count - 1):
+        parts.append(value.astype(jnp.bfloat16))
+        value = value - parts[-1].astype(jnp.float32)
+    return parts + [value.astype(jnp.bfloat16)]
+
+
+def single(left, right, dims=((1,), (0,))):
+    return product(left, right, dims, lax.Precision.DEFAULT)
 
 
 def attend_kernel(
@@ -149,26 +196,37 @@
         ]
     )
     wide = HEADS * COUNT
-    query_keys, d_att_values = to_keys[...], to_values[...]
-    scores = product(keys, query_keys)
+    k0, k1, k2 = pieces(keys, 3)
+    q0, q1, q2 = pieces(to_keys[...], 3)
+    v0, v1 = pieces(to_values[...], 2)
+    scores = single(
+        jnp.concatenate([k0, k0, k1, k0, k2, k1], 1), jnp.concatenate([q0, q1, q0, q2, q0, q1])
+    )
+    d_probs = single(jnp.concatenate([k0, k0, k1], 1), jnp.concatenate([v0, v1, v0]))
     weights = jnp.exp(scores - jnp.max(scores, 0, keepdims=True))
     probs = weights * (1.0 / jnp.sum(weights, 0, keepdims=True))
-    keys_split = halves(keys)
-    keys_t = halves(keys.T)
-    values_split = halves(d_att_values)
-    d_probs = three_pass(keys_split, values_split)
+    t0, t1 = pieces(keys.T, 2)
+    both_t = jnp.concatenate([t0, t1])
+
+    def by_keys(high, low):
+        twice = single(both_t, high)
+        return twice[:CHANNELS] + (twice[CHANNELS:] + single(t0, low))
+
     d_scores = probs * (d_probs - jnp.sum(d_probs * probs, 0, keepdims=True))
-    probs_split, d_split = halves(probs), halves(d_scores)
-    att_keys = three_pass(keys_t, probs_split)
-    d_query_keys = three_pass(keys_t, d_split)
-
-    def inner(pair):
-        return tuple(x[:, :wide] for x in pair)
-
-    sums = three_pass(inner(d_split), inner(halves(query_keys)), BOTH) + three_pass(
-        inner(probs_split), inner(values_split), BOTH
-    )
-    upper = lax.broadcasted_iota(jnp.int32, (CHANNELS, CHANNELS), 0) < WIDTH
+    d0, d1 = pieces(d_scores, 2)
+    d_query_keys = by_keys(d0, d1)
+    p0, p1 = pieces(probs[:, :wide], 2)
+    att_keys = by_keys(p0, p1)
+    d0, d1 = d0[:, :wide], d1[:, :wide]
+    large = jnp.concatenate([q0[:, :wide], v0[:, :wide]], 1)
+    small = jnp.concatenate([q1[:, :wide], v1[:, :wide]], 1)
+    twice = single(
+        jnp.concatenate([d0, p0], 1), jnp.concatenate([large, small]), BOTH
+    )
+    sums = twice[:, :CHANNELS] + (
+        twice[:, CHANNELS:] + single(jnp.concatenate([d1, p1], 1), large, BOTH)
+    )
+    upper = top_half()
     left = lax.broadcasted_iota(jnp.int32, (CHANNELS, CHANNELS), 1) < WIDTH
 
     def heads(first, second, mask=upper):
@@ -320,8 +378,7 @@
     square = (CHANNELS, CHANNELS)
     all_tokens = (COUNT + RING, CHANNELS)
 
-    low = jnp.concatenate([tokens[:2], cotangent[:1]])
-    high = jnp.concatenate([tokens[-2:], cotangent[-1:]])
+    low, high = call(edge_kernel, [f32(3, COLS, CHANNELS)] * 2, tokens, cotangent)
     above, below = neighbours(low, high, ROW)
 
     def side(first_t, first_g):
@@ -351,18 +408,13 @@
     message = lax.all_to_all(message, CHIPS, 0, 0, tiled=True)
     keys = lax.all_gather(message, "c", axis=0, tiled=True).reshape(-1, CHANNELS)
 
-    normed_t, grad_t = normed.T, grad.T
-    query_t = product(w_query, normed_t, FIRST)
-    d_att_t = product(w_out, grad_t)
-    to_keys, to_values = [], []
-    for head in range(HEADS):
-        part = slice(head * WIDTH, (head + 1) * WIDTH)
-        to_keys.append(product(w_key[:, part], query_t[part]) * SCALE)
-        to_values.append(product(w_value[:, part], d_att_t[part]))
-
-    def columns(by_head):
-        return jnp.concatenate([x[:, :COUNT] for x in by_head] + [x[:, COUNT:] for x in by_head], 1)
-
+    columns = HEADS * (COUNT + RING)
+    prepared = call(
+        before_kernel,
+        [f32(CHANNELS, columns)] * 2 + [f32(*square)] * 4,
+        normed, grad, w_query, w_key, w_value, w_out,
+        flops=1 << 10,
+    )
     own, mate, att_t, dq_t, ring_keys = call(
         attend_kernel,
         [
@@ -372,27 +424,20 @@
             f32(*square),
             f32(CHANNELS, HEADS * RING),
         ],
-        place[2:], keys, columns(to_keys), columns(to_values), query_t[:, :COUNT],
-        d_att_t[:, :COUNT], normed_t[:, :COUNT], grad_t[:, :COUNT], w_key, w_value,
+        place[2:], keys, *prepared, w_key, w_value,
         scalars=1, flops=1 << 31,
     )
 
-    received = lax.ppermute(mate, "c", [(0, 1), (1, 0)])
+    received = lax.all_gather(mate, "c", axis=0)
+    received = jnp.where(place[2] == 0, received[1], received[0])
     sums = (own + received).reshape(chips, 1, 3 * CHANNELS)
     sums = jnp.sum(lax.all_to_all(sums, CHIPS, 0, 0, tiled=True), 0)
-
-    output = mixed + product(att_t, w_out, FIRST).reshape(tile)
-    d_normed = product(dq_t, w_query, ((0,), (1,)))
-    dq_ring = [
-        product(
-            w_key[:, head * WIDTH : (head + 1) * WIDTH],
-            ring_keys[:, head * RING : (head + 1) * RING],
-            FIRST,
-        )
-        for head in range(HEADS)
-    ]
-    d_ring = product(jnp.concatenate(dq_ring) * SCALE, w_query, ((0,), (1,)))
-
+    output, d_normed, d_ring = call(
+        after_kernel,
+        [f32(*tile), f32(*square), f32(RING, CHANNELS)],
+        att_t, dq_t, ring_keys, mixed, w_query, w_key, w_out,
+        flops=1 << 10,
+    )
     d_mixed, message = call(
         middle_kernel,
         [f32(*tile), f32(row_count, 16, CHANNELS)],

time: 140 us -> 134 us (0.957)
  blocking collectives: 9.25 us -> 27.8 us
  waiting for transfers between devices: 50.4 us -> 38.2 us
  local copies, waits for them, and re-layouts: 8.07 us -> 3.57 us
  starting transfers between devices: 55.5 us -> 51.5 us
  matrix products: 3.27 us -> 0 us
    all_to_all x0 -> x1, blocking collectives: none -> 12.3 us  [body(): message = lax.all_to_all(message, CHIP_COL, 0, 0, tiled=True)]
    all_to_all x1 -> x0, waiting for transfers between devices: 7.69 us -> none  [body(): message = lax.all_to_all(message, CHIP_COL, 0, 0, tiled=True)]
    ppermute x2, starting transfers between devices: 3.87 us -> 10.6 us  [neighbours(): lax.ppermute(low_side, axis, down)]
    ppermute x2, waiting for transfers between devices: 5.71 us -> 0.01 us  [neighbours(): lax.ppermute(low_side, axis, down)]
    all_gather x1, blocking collectives: 3.14 us -> 6.85 us  [body(): lax.all_gather(message, 'c', axis=0, tiled=True).reshape(-1, CHANNELS)]
    all_to_all x1 -> x0, starting transfers between devices: 3.53 us -> none  [body(): message = lax.all_to_all(message, CHIP_COL, 0, 0, tiled=True)]
    ppermute x2, starting transfers between devices: 10.1 us -> 6.63 us  [neighbours(): lax.ppermute(high_side, axis, up)]
    dot_general x11 -> x0, matrix products: 3.27 us -> none  [product(): lax.dot_general(left, right, (dims, ((), ())), precision=precision, prefe...]
  transfers between devices with their start and end apart: 9 -> 7, of which waited for: 7 -> 5; matrix products, arithmetic and copies ran while one was open for 3% -> 0% of each run, Pallas kernels for 0% -> 2%
where the time goes in v4:
time: 134 us; the launch traced here: 133 us
  starting transfers between devices  51.5 us (38%)
  waiting for transfers between devices  38.2 us (29%)
  blocking collectives  27.8 us (21%)
  Pallas kernels  10.5 us (8%)
  local copies, waits for them, and re-layouts  3.57 us (3%)
    all_to_all x1, starting transfers between devices, body(): message = lax.all_to_all(message, CHIPS, 0, 0, tiled=True)  21.4 us
    all_to_all x1, waiting for transfers between devices, body(): sums = jnp.sum(lax.all_to_all(sums, CHIPS, 0, 0, tiled=True), 0)  16.2 us
    all_to_all x1, blocking collectives, body(): message = lax.all_to_all(message, CHIP_COL, 0, 0, tiled=True)  12.3 us
    all_to_all x1, waiting for transfers between devices, body(): message = lax.all_to_all(message, CHIPS, 0, 0, tiled=True)  11.6 us
    ppermute x2, starting transfers between devices, neighbours(): lax.ppermute(low_side, axis, down)  10.6 us
    pallas_call x8, Pallas kernels, call(): pl.pallas_call(kernel, out_shape=outs, in_specs=specs, out_specs=[in_vmem...  10.5 us
    all_to_all x1, starting transfers between devices, body(): sums = jnp.sum(lax.all_to_all(sums, CHIPS, 0, 0, tiled=True), 0)  9.34 us
    all_to_all x1, waiting for transfers between devices, body(): message = lax.all_to_all(message, ROW, 0, 0, tiled=True)  8.42 us
  transfers between devices with their start and end apart: 7, of which 5 were waited for; matrix products, arithmetic and copies ran while one was open for 0% of the time, Pallas kernels for 2%

profile of v4, /device:TPU:1, one launch (start us, length us, event | category | flops | bytes accessed | tf_op | source)
XLA Modules:
  0.0 133.0 jit_solution(14374527861179679383)
XLA Ops:
  1.5 0.8 copy-done.2
  2.3 1.3 collective-permute-start.1
  3.7 4.6 %collective-permute-start = (f32[3,16,128]{2,0,1:T(4,128)S(1)}, f32[3,16,128]{2,0,1:T(4,128)S(1)}, u32[]{:S(2)}, u32[]{:S(2)}) collective-permute-start(f32[3,16,128]{2,0,1:T(4,128)S(1)} %copy.24), channel_id=1, source_target_pairs={{0,32},{32,64},{64,96},{96,128},{128,160},{160,192},{192,224},{224... | collective-permute-start | bytes 73736 | tf_op jit(solution)/shard_map/ppermute | solution.py:71
  8.3 0.9 collective-permute-done
  9.6 9.3 %collective-permute-start.3 = (f32[34,128]{1,0:T(8,128)S(1)}, f32[34,128]{1,0:T(8,128)S(1)}, u32[]{:S(2)}, u32[]{:S(2)}) collective-permute-start(f32[34,128]{1,0:T(8,128)S(1)} %concatenate.7), channel_id=1, source_target_pairs={{1,0},{2,1},{3,2},{4,3},{5,4},{6,5},{7,6},{8,7},{9,8},{10,9},{11,1... | collective-permute-start | bytes 52232 | tf_op jit(solution)/shard_map/ppermute | solution.py:71
  19.2 2.1 %collective-permute-start.2 = (f32[34,128]{1,0:T(8,128)S(1)}, f32[34,128]{1,0:T(8,128)S(1)}, u32[]{:S(2)}, u32[]{:S(2)}) collective-permute-start(f32[34,128]{1,0:T(8,128)S(1)} %concatenate.6), channel_id=1, source_target_pairs={{0,1},{1,2},{2,3},{3,4},{4,5},{5,6},{6,7},{7,8},{8,9},{9,10},{10,1... | collective-permute-start | bytes 52232 | tf_op jit(solution)/shard_map/ppermute | solution.py:71
  21.3 1.1 collective-permute-done.2.before
  22.5 1.2 shard_map.127
  23.7 21.4 %all-to-all-start = ((f32[256,2,128]{2,1,0:T(2,128)}), f32[256,2,128]{2,1,0:T(2,128)S(1)}, u32[]{:S(2)}, u32[]{:S(2)}) async-start(f32[256,2,128]{2,1,0:T(2,128)} %get-tuple-element.40), calls=%async_computation | async-start | bytes 524288 | tf_op jit(solution)/shard_map/all_to_all | solution.py:408
  45.2 1.2 shard_map.128
  46.4 11.6 %all-to-all-done = f32[256,2,128]{2,1,0:T(2,128)S(1)} async-done(((f32[256,2,128]{2,1,0:T(2,128)}), f32[256,2,128]{2,1,0:T(2,128)S(1)}, u32[]{:S(2)}, u32[]{:S(2)}) %all-to-all-start) | async-done | bytes 262176 | tf_op jit(solution)/shard_map/all_to_all | solution.py:408
  57.9 6.9 %all_gather.15 = f32[512,2,128]{2,1,0:T(2,128)S(1)} all-gather(f32[256,2,128]{2,1,0:T(2,128)S(1)} %all-to-all-done), channel_id=1, replica_groups=mesh['y'=8,'xl'=2,'xh'=2,'z'=8,'c'=2] {'c'}, dimensions={0}, use_global_device_ids=true | all-gather | bytes 786432 | tf_op jit(solution)/shard_map/all_gather | solution.py:409
  64.8 4.3 %shard_map.129 = (f32[256,384]{1,0:T(8,128)S(1)}, f32[256,384]{1,0:T(8,128)S(1)}, f32[128,128]{1,0:T(8,128)S(1)}, f32[128,128]{1,0:T(8,128)S(1)}, f32[128,128]{1,0:T(8,128)S(1)}) custom-call(s32[1]{0:T(128)} %bitcast.core, f32[1024,128]{1,0:T(8,128)S(1)} %bitcast.50, f32[128,384]{1,0:T(8,128)S(1)} %get-tuple-element.43.to_keys, ...), custom_call_target="tpu_custom_call" | custom-call | flops 2147483648 | bytes 2147483648 | tf_op jit(solution)/shard_map/pallas_call | solution.py:56
  69.0 2.4 %all-gather = f32[512,384]{1,0:T(8,128)S(1)} all-gather(f32[256,384]{1,0:T(8,128)S(1)} %get-tuple-element.55), channel_id=2, replica_groups=mesh['y'=8,'xl'=2,'xh'=2,'z'=8,'c'=2] {'c'}, dimensions={0}, use_global_device_ids=true | all-gather | bytes 1179648 | tf_op jit(solution)/shard_map/all_gather | solution.py:431
  71.5 1.2 copy.34
  72.6 9.3 %all-to-all-start.1 = ((f32[256,1,384]{2,1,0:T(1,128)}), f32[256,1,384]{2,1,0:T(1,128)S(1)}, u32[]{:S(2)}, u32[]{:S(2)}) async-start(f32[256,1,384]{2,1,0:T(1,128)} %copy.34), calls=%async_computation.1 | async-start | bytes 786432 | tf_op jit(solution)/shard_map/all_to_all | solution.py:434
  82.0 1.0 shard_map.130
  83.0 16.2 %all-to-all-done.1 = f32[256,1,384]{2,1,0:T(1,128)S(1)} async-done(((f32[256,1,384]{2,1,0:T(1,128)}), f32[256,1,384]{2,1,0:T(1,128)S(1)}, u32[]{:S(2)}, u32[]{:S(2)}) %all-to-all-start.1) | async-done | bytes 393248 | tf_op jit(solution)/shard_map/all_to_all | solution.py:434
  99.6 0.9 shard_map.131
  100.5 3.5 %all-to-all-start.2 = ((f32[16,16,128]{2,1,0:T(8,128)}), f32[16,16,128]{2,1,0:T(8,128)S(1)}, u32[]{:S(2)}, u32[]{:S(2)}) async-start(f32[16,16,128]{2,1,0:T(8,128)} %get-tuple-element.60), calls=%async_computation.2 | async-start | bytes 262144 | tf_op jit(solution)/shard_map/all_to_all | solution.py:447
  104.1 8.4 %all-to-all-done.2.received = f32[16,16,128]{2,1,0:T(8,128)S(1)} async-done(((f32[16,16,128]{2,1,0:T(8,128)}), f32[16,16,128]{2,1,0:T(8,128)S(1)}, u32[]{:S(2)}, u32[]{:S(2)}) %all-to-all-start.2) | async-done | bytes 131104 | tf_op jit(solution)/shard_map/all_to_all | solution.py:447
  113.1 12.3 %all_to_all.20 = f32[16,32,128]{2,1,0:T(8,128)S(1)} all-to-all(f32[16,32,128]{2,1,0:T(8,128)S(1)} %shard_map.132), channel_id=1, replica_groups=mesh['y'=8,'xl'=2,'xh'=2,'z'=8,'c'=2] {'xh','z'}, dimensions={0} | all-to-all | bytes 524288 | tf_op jit(solution)/shard_map/all_to_all | solution.py:454
  125.4 6.3 %all-gather.1 = f32[32,32,128]{2,1,0:T(8,128)S(1)} all-gather(f32[16,32,128]{2,1,0:T(8,128)S(1)} %all_to_all.20), channel_id=3, replica_groups=mesh['y'=8,'xl'=2,'xh'=2,'z'=8,'c'=2] {'c'}, dimensions={0}, use_global_device_ids=true | all-gather | bytes 786432 | tf_op jit(solution)/shard_map/all_gather | solution.py:455
  131.7 1.3 %shard_map.133 = (f32[8,16,128]{2,1,0:T(8,128)}, f32[3,3,128]{2,1,0:T(4,128)}, f32[128,128]{1,0:T(8,128)}, f32[128,128]{1,0:T(8,128)}, f32[128,128]{1,0:T(8,128)}, /*index=5*/f32[128,128]{1,0:T(8,128)}) custom-call(s32[3]{0:T(128)S(1)} %pad_add_fusion.place, f32[2,16,32,128]{3,2,1,0:T(8,128)S(1)} %bitcast.49, f32[64,128]{1,0:T(8,128)S(1)} %get-tuple-element.61.d_normed, ...), custom_call_target="tpu_custom_call" | custom-call | flops 1048576 | bytes 1048576 | tf_op jit(solution)/shard_map/pallas_call | solution.py:56
  (37 shorter events, 2.6 us)
Async XLA Ops:
  0.6 0.8 copy-start
  1.5 0.8 copy-start.2
  2.3 5.9 %collective-permute-start.1 = (f32[3,16,128]{2,0,1:T(4,128)S(1)}, f32[3,16,128]{2,0,1:T(4,128)S(1)}, u32[]{:S(2)}, u32[]{:S(2)}) collective-permute-start(f32[3,16,128]{2,0,1:T(4,128)S(1)} %copy.25), channel_id=1, source_target_pairs={{32,0},{64,32},{96,64},{128,96},{160,128},{192,160},{224,192},{256... | collective-permute-start | bytes 73736 | tf_op jit(solution)/shard_map/ppermute | solution.py:71
  3.7 5.6 %collective-permute-start = (f32[3,16,128]{2,0,1:T(4,128)S(1)}, f32[3,16,128]{2,0,1:T(4,128)S(1)}, u32[]{:S(2)}, u32[]{:S(2)}) collective-permute-start(f32[3,16,128]{2,0,1:T(4,128)S(1)} %copy.24), channel_id=1, source_target_pairs={{0,32},{32,64},{64,96},{96,128},{128,160},{160,192},{192,224},{224... | collective-permute-start | bytes 73736 | tf_op jit(solution)/shard_map/ppermute | solution.py:71
  9.6 11.8 %collective-permute-start.3 = (f32[34,128]{1,0:T(8,128)S(1)}, f32[34,128]{1,0:T(8,128)S(1)}, u32[]{:S(2)}, u32[]{:S(2)}) collective-permute-start(f32[34,128]{1,0:T(8,128)S(1)} %concatenate.7), channel_id=1, source_target_pairs={{1,0},{2,1},{3,2},{4,3},{5,4},{6,5},{7,6},{8,7},{9,8},{10,9},{11,1... | collective-permute-start | bytes 52232 | tf_op jit(solution)/shard_map/ppermute | solution.py:71
  18.9 3.6 %copy-start.3 = (f32[8,16,128]{2,1,0:T(8,128)S(1)}, f32[8,16,128]{2,1,0:T(8,128)}, u32[]{:S(2)}) copy-start(f32[8,16,128]{2,1,0:T(8,128)} %grad.3) | copy-start | bytes 196612
  19.2 3.2 %copy-start.1 = (f32[8,16,128]{2,1,0:T(8,128)S(1)}, f32[8,16,128]{2,1,0:T(8,128)}, u32[]{:S(2)}) copy-start(f32[8,16,128]{2,1,0:T(8,128)} %tokens.3) | copy-start | bytes 196612
  19.2 3.2 %collective-permute-start.2 = (f32[34,128]{1,0:T(8,128)S(1)}, f32[34,128]{1,0:T(8,128)S(1)}, u32[]{:S(2)}, u32[]{:S(2)}) collective-permute-start(f32[34,128]{1,0:T(8,128)S(1)} %concatenate.6), channel_id=1, source_target_pairs={{0,1},{1,2},{2,3},{3,4},{4,5},{5,6},{6,7},{7,8},{8,9},{9,10},{10,1... | collective-permute-start | bytes 52232 | tf_op jit(solution)/shard_map/ppermute | solution.py:71
  21.3 1.2 copy-start.8
  23.7 21.5 %copy-start.4 = (f32[128,128]{1,0:T(8,128)S(1)}, f32[128,128]{1,0:T(8,128)}, u32[]{:S(2)}) copy-start(f32[128,128]{1,0:T(8,128)} %w_query.3) | copy-start | bytes 196612
  23.7 21.5 %copy-start.5 = (f32[128,128]{1,0:T(8,128)S(1)}, f32[128,128]{1,0:T(8,128)}, u32[]{:S(2)}) copy-start(f32[128,128]{1,0:T(8,128)} %w_key.5) | copy-start | bytes 196612
  23.7 21.5 %copy-start.6 = (f32[128,128]{1,0:T(8,128)S(1)}, f32[128,128]{1,0:T(8,128)}, u32[]{:S(2)}) copy-start(f32[128,128]{1,0:T(8,128)} %w_out.3) | copy-start | bytes 196612
  23.7 21.5 %copy-start.7 = (f32[128,128]{1,0:T(8,128)S(1)}, f32[128,128]{1,0:T(8,128)}, u32[]{:S(2)}) copy-start(f32[128,128]{1,0:T(8,128)} %w_value.3) | copy-start | bytes 196612
  23.7 34.2 %all-to-all-start = ((f32[256,2,128]{2,1,0:T(2,128)}), f32[256,2,128]{2,1,0:T(2,128)S(1)}, u32[]{:S(2)}, u32[]{:S(2)}) async-start(f32[256,2,128]{2,1,0:T(2,128)} %get-tuple-element.40), calls=%async_computation | async-start | bytes 524288 | tf_op jit(solution)/shard_map/all_to_all | solution.py:408
  72.6 26.6 %all-to-all-start.1 = ((f32[256,1,384]{2,1,0:T(1,128)}), f32[256,1,384]{2,1,0:T(1,128)S(1)}, u32[]{:S(2)}, u32[]{:S(2)}) async-start(f32[256,1,384]{2,1,0:T(1,128)} %copy.34), calls=%async_computation.1 | async-start | bytes 786432 | tf_op jit(solution)/shard_map/all_to_all | solution.py:434
  100.5 12.0 %all-to-all-start.2 = ((f32[16,16,128]{2,1,0:T(8,128)}), f32[16,16,128]{2,1,0:T(8,128)S(1)}, u32[]{:S(2)}, u32[]{:S(2)}) async-start(f32[16,16,128]{2,1,0:T(8,128)} %get-tuple-element.60), calls=%async_computation.2 | async-start | bytes 262144 | tf_op jit(solution)/shard_map/all_to_all | solution.py:447

commit v5 on v4

--- a/solution.py
+++ b/solution.py
@@ -19,6 +19,8 @@
 WIDE = COLS + 2
 USED = 2 * WIDE + 2 * ROWS
 RING = 64
+SIDE = 40
+FACING = 6 * COLS
 WIDTH = CHANNELS // HEADS
 SCALE = WIDTH ** (-0.5)
 BOTH = ((1,), (1,))
@@ -64,18 +66,96 @@
     )(*args)
 
 
-def neighbours(low_side, high_side, axis):
+def seam(axis):
     peers = lax.axis_size(axis)
-    up = [(i, i + 1) for i in range(peers - 1)]
-    down = [(i + 1, i) for i in range(peers - 1)]
-    return lax.ppermute(high_side, axis, up), lax.ppermute(low_side, axis, down)
+    return [[k, (k + 1) % peers] for k in range(1, peers, 2)]
+
+
+def pair_gather(value, axis, groups=None):
+    return lax.all_gather(value, axis, axis_index_groups=groups, axis=0)
+
+
+def edge_kernel(tokens, grad, mine, mates, sems):
+    odd, core = lax.axis_index("xl"), lax.axis_index("c")
+    copies = []
+    for out, last in ((mine, (1 - odd + core) % 2), (mates, (odd + core) % 2)):
+        copies += [
+            (tokens.at[pl.ds(last * (ROWS - 2), 2)], out.at[0:2]),
+            (grad.at[pl.ds(last * (ROWS - 1), 1)], out.at[2:3]),
+        ]
+    copies = [pltpu.make_async_copy(*copy, sems.at[k]) for k, copy in enumerate(copies)]
+    for copy in copies:
+        copy.start()
+    for copy in copies:
+        copy.wait()
+
+
+def both_kernel(place, mine, shared, strips):
+    core = place[2]
+    for tile in range(2):
+        strips[tile] = jnp.where(core == tile, mine[...], shared[tile])
+
+
+def reach_kernel(last_row, place, tokens, grad, strips, message):
+    row, core = place[0], place[2]
+    odd = row % 2
+    partner = jnp.where(core == 0, 1 - odd, odd)
+    outside = (core == 1) & ((row == 0) | (row == last_row))
+    for tile in range(2):
+        for r in range(3):
+            at = (3 * tile + r) * COLS
+            message[at : at + COLS] = jnp.where(outside, 0.0, strips[partner, tile, r])
+    right = 1 - core
+    for r in range(ROWS):
+        for k in range(2):
+            message[FACING + k * ROWS + r, :] = tokens[r, right * (COLS - 2) + k]
+        message[FACING + 2 * ROWS + r, :] = grad[r, right * (COLS - 1)]
+
+
+def side_kernel(place, tokens, grad, shared, above, below, beside, beyond):
+    row, core = place[0], place[2]
+    odd, mate = row % 2, 1 - core
+    for r in range(3):
+        at = pl.multiple_of((3 * core + r) * COLS, COLS)
+        above[r] = shared[1 - odd, pl.ds(at, COLS)]
+        below[r] = shared[odd, pl.ds(at, COLS)]
+    tall = ROWS + 4
+    right = core
+    for k in range(2):
+        at = right * (COLS - 2) + k
+        for r in range(2):
+            line = (3 * mate + r) * COLS + at
+            beside[k * tall + r, :] = shared[1 - odd, line]
+            beside[k * tall + ROWS + 2 + r, :] = shared[odd, line]
+            beyond[k * tall + r, :] = above[r, at]
+            beyond[k * tall + ROWS + 2 + r, :] = below[r, at]
+        for r in range(ROWS):
+            beyond[k * tall + 2 + r, :] = tokens[r, at]
+        faced = FACING + k * ROWS
+        beside[k * tall + 2 : k * tall + 2 + ROWS] = shared[mate, faced : faced + ROWS]
+    at = right * (COLS - 1)
+    line = (3 * mate + 2) * COLS + at
+    beside[2 * tall, :] = shared[1 - odd, line]
+    beside[2 * tall + ROWS + 1, :] = shared[odd, line]
+    beyond[2 * tall, :] = above[2, at]
+    beyond[2 * tall + ROWS + 1, :] = below[2, at]
+    faced = FACING + 2 * ROWS
+    beside[2 * tall + 1 : 2 * tall + 1 + ROWS] = shared[mate, faced : faced + ROWS]
+    for r in range(ROWS):
+        beyond[2 * tall + 1 + r, :] = grad[r, at]
+    for out in (beside, beyond):
+        out[SIDE - 6 :, :] = jnp.zeros((6, CHANNELS), jnp.float32)
 
 
 def mix_kernel(
-    tokens, grad, above, below, before, after, weight,
+    last_col, place, tokens, grad, above, below, beside, beyond, weight,
     message, pooled_out, padded, mixed_out, normed_out, inv_out, grad_out,
-    normed_ext, inv_ext, mixed_ext,
+    normed_ext, inv_ext, mixed_ext, before, after,
 ):
+    col = place[1]
+    even = col % 2 == 0
+    before[...] = jnp.where(even, jnp.where(col == 0, 0.0, beyond[0]), beside[...])
+    after[...] = jnp.where(even, beside[...], jnp.where(col == last_col, 0.0, beyond[1]))
     padded[2 : 2 + ROWS, 2 : 2 + COLS] = tokens[...]
     padded[0:2, 2 : 2 + COLS] = above[0:2]
     padded[2 + ROWS : 4 + ROWS, 2 : 2 + COLS] = below[0:2]
@@ -124,11 +204,6 @@
     grad_out[COUNT + USED :] = jnp.zeros((RING - USED, CHANNELS), jnp.float32)
 
 
-def edge_kernel(tokens, grad, low, high):
-    low[0:2], low[2] = tokens[0:2], grad[0]
-    high[0:2], high[2] = tokens[ROWS - 2 : ROWS], grad[ROWS - 1]
-
-
 def top_half():
     return lax.broadcasted_iota(jnp.int32, (CHANNELS, CHANNELS), 0) < WIDTH
 
@@ -378,20 +453,35 @@
     square = (CHANNELS, CHANNELS)
     all_tokens = (COUNT + RING, CHANNELS)
 
-    low, high = call(edge_kernel, [f32(3, COLS, CHANNELS)] * 2, tokens, cotangent)
-    above, below = neighbours(low, high, ROW)
-
-    def side(first_t, first_g):
-        parts = []
-        for k in (first_t, first_t + 1):
-            parts += [above[:2, k], tokens[:, k], below[:2, k]]
-        return jnp.concatenate(
-            parts + [above[2:, first_g], cotangent[:, first_g], below[2:, first_g]]
-        )
-
-    before, after = neighbours(side(0, 0), side(COLS - 2, COLS - 1), COL)
+    anywhere = pl.BlockSpec(memory_space=pl.ANY)
+    mine, mates = pl.pallas_call(
+        edge_kernel,
+        out_shape=[f32(3, COLS, CHANNELS)] * 2,
+        in_specs=[anywhere] * 2,
+        out_specs=[pl.BlockSpec(memory_space=pltpu.VMEM)] * 2,
+        scratch_shapes=[pltpu.SemaphoreType.DMA((4,))],
+    )(tokens, cotangent)
+    mates = pair_gather(mates, "c")
+    (strips,) = call(both_kernel, [f32(2, 3, COLS, CHANNELS)], place, mine, mates, scalars=1)
+    pairs = [[4 * k, 4 * k + 2] for k in range(row_count // 2)]
+    pairs += [[2 * j + 1, 2 * k + 1] for j, k in seam(ROW)]
+    strips = pair_gather(strips, ROW + ("c",), pairs)
+    (shared,) = call(
+        functools.partial(reach_kernel, row_count - 1),
+        [f32(FACING + 3 * ROWS, CHANNELS)],
+        place, tokens, cotangent, strips,
+        scalars=1,
+    )
+    shared = pair_gather(shared, "c")
+    above, below, beside, beyond = call(
+        side_kernel,
+        [f32(3, COLS, CHANNELS)] * 2 + [f32(SIDE, CHANNELS)] * 2,
+        place, tokens, cotangent, shared,
+        scalars=1,
+    )
+    beyond = pair_gather(beyond, COL, seam(COL))
     message, pooled, padded, mixed, normed, inv_std, grad = call(
-        mix_kernel,
+        functools.partial(mix_kernel, col_count - 1),
         [
             f32(chips, CELLS, CHANNELS),
             f32(2 * CELLS, CHANNELS),
@@ -401,8 +491,8 @@
             f32(*all_tokens),
             f32(*all_tokens),
         ],
-        tokens, cotangent, above, below, before, after, conv_weight,
-        scratch=[(ROWS + 2, 24, CHANNELS)] * 3,
+        place, tokens, cotangent, above, below, beside, beyond, conv_weight,
+        scratch=[(ROWS + 2, 24, CHANNELS)] * 3 + [(SIDE, CHANNELS)] * 2, scalars=1,
     )
 
     message = lax.all_to_all(message, CHIPS, 0, 0, tiled=True)

time: 134 us -> 131 us (0.978)
  blocking collectives: 27.8 us -> 54.6 us
  starting transfers between devices: 51.5 us -> 30.1 us
  waiting for transfers between devices: 38.2 us -> 29 us
  Pallas kernels: 10.5 us -> 13.5 us
  local copies, waits for them, and re-layouts: 3.57 us -> 1.89 us
    all_gather x0 -> x4, blocking collectives: none -> 20.2 us  [pair_gather(): return lax.all_gather(value, axis, axis_index_groups=groups, axis=0)]
    ppermute x4 -> x0, starting transfers between devices: 17.2 us -> none  [the longest x2 10.6 us: neighbours(): lax.ppermute(low_side, axis, down)]
    all_to_all x0 -> x1, blocking collectives: none -> 11.6 us  [body(): message = lax.all_to_all(message, ROW, 0, 0, tiled=True)]
    all_to_all x1 -> x0, waiting for transfers between devices: 8.42 us -> none  [body(): message = lax.all_to_all(message, ROW, 0, 0, tiled=True)]
    all_gather x1, blocking collectives: 6.85 us -> 2.17 us  [body(): lax.all_gather(message, 'c', axis=0, tiled=True).reshape(-1, CHANNELS)]
    all_to_all x1 -> x0, starting transfers between devices: 3.51 us -> none  [body(): message = lax.all_to_all(message, ROW, 0, 0, tiled=True)]
    ppermute x4 -> x0, waiting for transfers between devices: 2.05 us -> none  [the longest x2 2.04 us: neighbours(): lax.ppermute(high_side, axis, up)]
    pallas_call x8 -> x10, Pallas kernels: 10.5 us -> 12.1 us  [call(): pl.pallas_call(kernel, out_shape=outs, in_specs=specs, out_specs=[in_vmem...]
  transfers between devices with their start and end apart: 7 -> 2, of which waited for: 5 -> 2; matrix products, arithmetic and copies ran while one was open for 0% -> 0% of each run, Pallas kernels for 2% -> 2%
where the time goes in v5:
time: 131 us; the launch traced here: 130 us
  blocking collectives  54.6 us (42%)
  starting transfers between devices  30.1 us (23%)
  waiting for transfers between devices  29 us (22%)
  Pallas kernels  13.5 us (10%)
  local copies, waits for them, and re-layouts  1.89 us (1%)
    all_to_all x1, starting transfers between devices, body(): message = lax.all_to_all(message, CHIPS, 0, 0, tiled=True)  20.8 us
    all_gather x4, blocking collectives, pair_gather(): return lax.all_gather(value, axis, axis_index_groups=groups, axis=0)  20.2 us
    all_to_all x1, waiting for transfers between devices, body(): sums = jnp.sum(lax.all_to_all(sums, CHIPS, 0, 0, tiled=True), 0)  16.2 us
    all_to_all x1, waiting for transfers between devices, body(): message = lax.all_to_all(message, CHIPS, 0, 0, tiled=True)  12.8 us
    all_to_all x1, blocking collectives, body(): message = lax.all_to_all(message, CHIP_COL, 0, 0, tiled=True)  12.8 us
    pallas_call x10, Pallas kernels, call(): pl.pallas_call(kernel, out_shape=outs, in_specs=specs, out_specs=[in_vmem...  12.1 us
    all_to_all x1, blocking collectives, body(): message = lax.all_to_all(message, ROW, 0, 0, tiled=True)  11.6 us
    all_to_all x1, starting transfers between devices, body(): sums = jnp.sum(lax.all_to_all(sums, CHIPS, 0, 0, tiled=True), 0)  9.35 us
  transfers between devices with their start and end apart: 2, of which 2 were waited for; matrix products, arithmetic and copies ran while one was open for 0% of the time, Pallas kernels for 2%

profile of v5, /device:TPU:1, one launch (start us, length us, event | category | flops | bytes accessed | tf_op | source)
XLA Modules:
  0.0 130.3 jit_solution(4033421825660620688)
XLA Ops:
  0.6 1.4 %shard_map.126 = (f32[3,16,128]{2,1,0:T(8,128)}, f32[3,16,128]{2,1,0:T(8,128)}) custom-call(f32[8,16,128]{2,1,0:T(8,128)} %tokens.7, f32[8,16,128]{2,1,0:T(8,128)} %grad.7), custom_call_target="tpu_custom_call" | custom-call | tf_op jit(solution)/shard_map/pallas_call | solution.py:457
  2.1 8.6 %all-gather = f32[6,16,128]{2,1,0:T(8,128)S(1)} all-gather(f32[3,16,128]{2,1,0:T(8,128)} %get-tuple-element.43), channel_id=2, replica_groups=mesh['y'=8,'xl'=2,'xh'=2,'z'=8,'c'=2] {'c'}, dimensions={0}, use_global_device_ids=true | all-gather | bytes 73728 | tf_op jit(solution)/shard_map/all_gather | solution.py:75
  11.3 5.9 %all-gather.1 = f32[4,3,16,128]{3,2,1,0:T(8,128)S(1)} all-gather(f32[2,3,16,128]{3,2,1,0:T(8,128)S(1)} %shard_map.127), channel_id=3, replica_groups={{0,32},{64,96},{128,160},{192,224},{256,288},{320,352},{384,416},{448,4..., dimensions={0}, use_global_device_ids=true | all-gather | bytes 147456 | tf_op jit(solution)/shard_map/all_gather | solution.py:75
  17.2 0.6 shard_map.128
  17.8 1.9 %all-gather.2 = f32[240,128]{1,0:T(8,128)S(1)} all-gather(f32[120,128]{1,0:T(8,128)S(1)} %shard_map.128), channel_id=4, replica_groups=mesh['y'=8,'xl'=2,'xh'=2,'z'=8,'c'=2] {'c'}, dimensions={0}, use_global_device_ids=true | all-gather | bytes 184320 | tf_op jit(solution)/shard_map/all_gather | solution.py:75
  19.7 0.6 shard_map.129
  20.2 3.9 %all-gather.3 = f32[80,128]{1,0:T(8,128)S(1)} all-gather(f32[40,128]{1,0:T(8,128)S(1)} %get-tuple-element.47), channel_id=5, replica_groups={{1,2},{3,4},{5,6},{7,8},{9,10},{11,12},{13,14},{15,16},{17,18},{19,20},..., dimensions={0}, use_global_device_ids=true | all-gather | bytes 61440 | tf_op jit(solution)/shard_map/all_gather | solution.py:75
  24.1 0.7 copy-done.6
  24.8 1.8 %shard_map.130 = (f32[256,2,128]{2,1,0:T(2,128)}, f32[4,128]{1,0:T(4,128)S(1)}, f32[12,24,128]{2,1,0:T(8,128)S(1)}, f32[8,16,128]{2,1,0:T(8,128)S(1)}, f32[192,1...) custom-call(s32[3]{0:T(128)S(1)} %pad_add_fusion.place, f32[8,16,128]{2,1,0:T(8,128)S(1)} %copy-done, ...), custom_call_target="tpu_custom_call" | custom-call | flops 1048576 | bytes 1048576 | tf_op jit(solution)/shard_map/pallas_call | solution.py:58
  26.6 20.8 %all-to-all-start = ((f32[256,2,128]{2,1,0:T(2,128)}), f32[256,2,128]{2,1,0:T(2,128)S(1)}, u32[]{:S(2)}, u32[]{:S(2)}) async-start(f32[256,2,128]{2,1,0:T(2,128)} %get-tuple-element.48), calls=%async_computation | async-start | bytes 524288 | tf_op jit(solution)/shard_map/all_to_all | solution.py:498
  47.4 1.2 shard_map.131
  48.6 12.8 %all-to-all-done = f32[256,2,128]{2,1,0:T(2,128)S(1)} async-done(((f32[256,2,128]{2,1,0:T(2,128)}), f32[256,2,128]{2,1,0:T(2,128)S(1)}, u32[]{:S(2)}, u32[]{:S(2)}) %all-to-all-start) | async-done | bytes 262176 | tf_op jit(solution)/shard_map/all_to_all | solution.py:498
  61.4 2.2 %all_gather.47 = f32[512,2,128]{2,1,0:T(2,128)S(1)} all-gather(f32[256,2,128]{2,1,0:T(2,128)S(1)} %all-to-all-done), channel_id=1, replica_groups=mesh['y'=8,'xl'=2,'xh'=2,'z'=8,'c'=2] {'c'}, dimensions={0}, use_global_device_ids=true | all-gather | bytes 786432 | tf_op jit(solution)/shard_map/all_gather | solution.py:499
  63.6 4.3 %shard_map.132 = (f32[256,384]{1,0:T(8,128)S(1)}, f32[256,384]{1,0:T(8,128)S(1)}, f32[128,128]{1,0:T(8,128)S(1)}, f32[128,128]{1,0:T(8,128)S(1)}, f32[128,128]{1,0:T(8,128)S(1)}) custom-call(s32[1]{0:T(128)} %bitcast.core, f32[1024,128]{1,0:T(8,128)S(1)} %bitcast.12, f32[128,384]{1,0:T(8,128)S(1)} %get-tuple-element.51.to_keys, ...), custom_call_target="tpu_custom_call" | custom-call | flops 2147483648 | bytes 2147483648 | tf_op jit(solution)/shard_map/pallas_call | solution.py:58
  67.8 2.4 %all-gather.4 = f32[512,384]{1,0:T(8,128)S(1)} all-gather(f32[256,384]{1,0:T(8,128)S(1)} %get-tuple-element.63), channel_id=6, replica_groups=mesh['y'=8,'xl'=2,'xh'=2,'z'=8,'c'=2] {'c'}, dimensions={0}, use_global_device_ids=true | all-gather | bytes 1179648 | tf_op jit(solution)/shard_map/all_gather | solution.py:521
  70.3 1.2 copy.14
  71.4 9.4 %all-to-all-start.1 = ((f32[256,1,384]{2,1,0:T(1,128)}), f32[256,1,384]{2,1,0:T(1,128)S(1)}, u32[]{:S(2)}, u32[]{:S(2)}) async-start(f32[256,1,384]{2,1,0:T(1,128)} %copy.14), calls=%async_computation.1 | async-start | bytes 786432 | tf_op jit(solution)/shard_map/all_to_all | solution.py:524
  80.8 1.0 shard_map.133
  81.8 16.2 %all-to-all-done.1 = f32[256,1,384]{2,1,0:T(1,128)S(1)} async-done(((f32[256,1,384]{2,1,0:T(1,128)}), f32[256,1,384]{2,1,0:T(1,128)S(1)}, u32[]{:S(2)}, u32[]{:S(2)}) %all-to-all-start.1) | async-done | bytes 393248 | tf_op jit(solution)/shard_map/all_to_all | solution.py:524
  98.6 11.6 %all_to_all.20.received = f32[16,16,128]{2,1,0:T(8,128)S(1)} all-to-all(f32[16,16,128]{2,1,0:T(8,128)S(1)} %get-tuple-element.68), channel_id=1, replica_groups=mesh['y'=8,'xl'=2,'xh'=2,'z'=8,'c'=2] {'y','xl'}, dimensions={0} | all-to-all | bytes 262144 | tf_op jit(solution)/shard_map/all_to_all | solution.py:537
  110.2 0.6 shard_map.135
  110.8 12.8 %all_to_all.21 = f32[16,32,128]{2,1,0:T(8,128)S(1)} all-to-all(f32[16,32,128]{2,1,0:T(8,128)S(1)} %shard_map.135), channel_id=1, replica_groups=mesh['y'=8,'xl'=2,'xh'=2,'z'=8,'c'=2] {'xh','z'}, dimensions={0} | all-to-all | bytes 524288 | tf_op jit(solution)/shard_map/all_to_all | solution.py:544
  123.6 5.4 %all-gather.5 = f32[32,32,128]{2,1,0:T(8,128)S(1)} all-gather(f32[16,32,128]{2,1,0:T(8,128)S(1)} %all_to_all.21), channel_id=7, replica_groups=mesh['y'=8,'xl'=2,'xh'=2,'z'=8,'c'=2] {'c'}, dimensions={0}, use_global_device_ids=true | all-gather | bytes 786432 | tf_op jit(solution)/shard_map/all_gather | solution.py:545
  129.0 1.3 %shard_map.136 = (f32[8,16,128]{2,1,0:T(8,128)}, f32[3,3,128]{2,1,0:T(4,128)}, f32[128,128]{1,0:T(8,128)}, f32[128,128]{1,0:T(8,128)}, f32[128,128]{1,0:T(8,128)}, /*index=5*/f32[128,128]{1,0:T(8,128)}) custom-call(s32[3]{0:T(128)S(1)} %pad_add_fusion.place, f32[2,16,32,128]{3,2,1,0:T(8,128)S(1)} %bitcast.11, f32[64,128]{1,0:T(8,128)S(1)} %get-tuple-element.69.d_normed, ...), custom_call_target="tpu_custom_call" | custom-call | flops 1048576 | bytes 1048576 | tf_op jit(solution)/shard_map/pallas_call | solution.py:58
  (21 shorter events, 1.3 us)
Async XLA Ops:
  2.1 8.7 %copy-start.7 = (f32[3,16,128]{2,1,0:T(8,128)S(1)}, f32[3,16,128]{2,1,0:T(8,128)}, u32[]{:S(2)}) copy-start(f32[3,16,128]{2,1,0:T(8,128)} %get-tuple-element.42.mine) | copy-start | bytes 73732
  11.3 5.9 %copy-start = (f32[8,16,128]{2,1,0:T(8,128)S(1)}, f32[8,16,128]{2,1,0:T(8,128)}, u32[]{:S(2)}) copy-start(f32[8,16,128]{2,1,0:T(8,128)} %tokens.7) | copy-start | bytes 196612
  11.3 5.9 %copy-start.1 = (f32[8,16,128]{2,1,0:T(8,128)S(1)}, f32[8,16,128]{2,1,0:T(8,128)}, u32[]{:S(2)}) copy-start(f32[8,16,128]{2,1,0:T(8,128)} %grad.7) | copy-start | bytes 196612
  24.1 0.7 copy-start.6
  26.6 20.8 %copy-start.2 = (f32[128,128]{1,0:T(8,128)S(1)}, f32[128,128]{1,0:T(8,128)}, u32[]{:S(2)}) copy-start(f32[128,128]{1,0:T(8,128)} %w_query.3) | copy-start | bytes 196612
  26.6 20.8 %copy-start.3 = (f32[128,128]{1,0:T(8,128)S(1)}, f32[128,128]{1,0:T(8,128)}, u32[]{:S(2)}) copy-start(f32[128,128]{1,0:T(8,128)} %w_key.5) | copy-start | bytes 196612
  26.6 20.8 %copy-start.4 = (f32[128,128]{1,0:T(8,128)S(1)}, f32[128,128]{1,0:T(8,128)}, u32[]{:S(2)}) copy-start(f32[128,128]{1,0:T(8,128)} %w_out.3) | copy-start | bytes 196612
  26.6 20.8 %copy-start.5 = (f32[128,128]{1,0:T(8,128)S(1)}, f32[128,128]{1,0:T(8,128)}, u32[]{:S(2)}) copy-start(f32[128,128]{1,0:T(8,128)} %w_value.3) | copy-start | bytes 196612
  26.6 34.8 %all-to-all-start = ((f32[256,2,128]{2,1,0:T(2,128)}), f32[256,2,128]{2,1,0:T(2,128)S(1)}, u32[]{:S(2)}, u32[]{:S(2)}) async-start(f32[256,2,128]{2,1,0:T(2,128)} %get-tuple-element.48), calls=%async_computation | async-start | bytes 524288 | tf_op jit(solution)/shard_map/all_to_all | solution.py:498
  71.4 26.6 %all-to-all-start.1 = ((f32[256,1,384]{2,1,0:T(1,128)}), f32[256,1,384]{2,1,0:T(1,128)S(1)}, u32[]{:S(2)}, u32[]{:S(2)}) async-start(f32[256,1,384]{2,1,0:T(1,128)} %copy.14), calls=%async_computation.1 | async-start | bytes 786432 | tf_op jit(solution)/shard_map/all_to_all | solution.py:524

commit v6 on v5

--- a/solution.py
+++ b/solution.py
@@ -12,7 +12,8 @@
 ROW = ("y", "xl")
 COL = ("xh", "z", "c")
 CHIP_COL = ("xh", "z")
-CHIPS = CHIP_COL + ROW
+ROW_GROUP = ("xl", "y")
+CHIPS = ("z", "xh") + ROW_GROUP
 ROWS, COLS, CHANNELS = 8, 16, 128
 CELLS, WIN_ROWS = 2, 4
 COUNT = ROWS * COLS
@@ -48,17 +49,23 @@
     )
 
 
+def here():
+    core = lax.axis_index("c")
+    row = lax.axis_index("y") * lax.axis_size("xl") + lax.axis_index("xl")
+    chip = lax.axis_index("xh") * lax.axis_size("z") + lax.axis_index("z")
+    return row, chip * lax.axis_size("c") + core, core
+
+
 def f32(*shape):
     return jax.ShapeDtypeStruct(shape, jnp.float32)
 
 
-def call(kernel, outs, *args, scratch=(), scalars=0, flops=1 << 20):
+def call(kernel, outs, *args, scratch=(), flops=1 << 20):
     in_vmem = pl.BlockSpec(memory_space=pltpu.VMEM)
-    specs = [pl.BlockSpec(memory_space=pltpu.SMEM)] * scalars + [in_vmem] * (len(args) - scalars)
     return pl.pallas_call(
         kernel,
         out_shape=outs,
-        in_specs=specs,
+        in_specs=[in_vmem] * len(args),
         out_specs=[in_vmem] * len(outs),
         scratch_shapes=[pltpu.VMEM(shape, jnp.float32) for shape in scratch],
         compiler_params=pltpu.CompilerParams(vmem_limit_bytes=48 << 20),
@@ -90,14 +97,14 @@
         copy.wait()
 
 
-def both_kernel(place, mine, shared, strips):
-    core = place[2]
+def both_kernel(mine, shared, strips):
+    core = here()[2]
     for tile in range(2):
         strips[tile] = jnp.where(core == tile, mine[...], shared[tile])
 
 
-def reach_kernel(last_row, place, tokens, grad, strips, message):
-    row, core = place[0], place[2]
+def reach_kernel(last_row, tokens, grad, weight, strips, message, taps):
+    row, _, core = here()
     odd = row % 2
     partner = jnp.where(core == 0, 1 - odd, odd)
     outside = (core == 1) & ((row == 0) | (row == last_row))
@@ -105,6 +112,8 @@
         for r in range(3):
             at = (3 * tile + r) * COLS
             message[at : at + COLS] = jnp.where(outside, 0.0, strips[partner, tile, r])
+    for k in range(9):
+        taps[k : k + 1] = weight[k // 3, k % 3 : k % 3 + 1]
     right = 1 - core
     for r in range(ROWS):
         for k in range(2):
@@ -112,8 +121,8 @@
         message[FACING + 2 * ROWS + r, :] = grad[r, right * (COLS - 1)]
 
 
-def side_kernel(place, tokens, grad, shared, above, below, beside, beyond):
-    row, core = place[0], place[2]
+def side_kernel(tokens, grad, shared, above, below, beside, beyond):
+    row, _, core = here()
     odd, mate = row % 2, 1 - core
     for r in range(3):
         at = pl.multiple_of((3 * core + r) * COLS, COLS)
@@ -148,11 +157,11 @@
 
 
 def mix_kernel(
-    last_col, place, tokens, grad, above, below, beside, beyond, weight,
+    last_col, tokens, grad, above, below, beside, beyond, weight,
     message, pooled_out, padded, mixed_out, normed_out, inv_out, grad_out,
     normed_ext, inv_ext, mixed_ext, before, after,
 ):
-    col = place[1]
+    col = here()[1]
     even = col % 2 == 0
     before[...] = jnp.where(even, jnp.where(col == 0, 0.0, beyond[0]), beside[...])
     after[...] = jnp.where(even, beside[...], jnp.where(col == last_col, 0.0, beyond[1]))
@@ -168,7 +177,7 @@
     mixed = padded[1 : ROWS + 3, 1 : 1 + WIDE]
     for i in range(3):
         for j in range(3):
-            mixed = mixed + weight[i, j : j + 1][None] * padded[i : i + ROWS + 2, j : j + WIDE]
+            mixed = mixed + weight[3 * i + j : 3 * i + j + 1][None] * padded[i : i + ROWS + 2, j : j + WIDE]
     normed, inv_std = normalize(mixed)
     mixed_ext[:, 0:WIDE] = mixed
     normed_ext[:, 0:WIDE] = normed
@@ -208,41 +217,26 @@
     return lax.broadcasted_iota(jnp.int32, (CHANNELS, CHANNELS), 0) < WIDTH
 
 
+def by_head(weight, value, ring, out):
+    upper = top_half()
+    for head, mask in enumerate((upper, ~upper)):
+        at = head * COUNT
+        out[:, at : at + COUNT] = product(weight, jnp.where(mask, value, 0.0))
+    parts = [product(weight, jnp.where(mask[:, :RING], ring, 0.0)) for mask in (upper, ~upper)]
+    out[:, HEADS * COUNT :] = jnp.concatenate(parts, 1)
+
+
 def before_kernel(
     normed, grad, w_query, w_key, w_value, w_out,
     to_keys, to_values, query_t, d_att_t, normed_t, grad_t,
 ):
-    upper = top_half()
-
-    def by_head(weight, value, ring, out):
-        for head, mask in enumerate((upper, ~upper)):
-            at = head * COUNT
-            out[:, at : at + COUNT] = product(weight, jnp.where(mask, value, 0.0))
-        parts = [
-            product(weight, jnp.where(mask[:, :RING], ring, 0.0)) for mask in (upper, ~upper)
-        ]
-        out[:, HEADS * COUNT :] = jnp.concatenate(parts, 1)
-
-    inner, ring = normed[0:COUNT].T, normed[COUNT:].T
-    normed_t[...] = inner
-    query = product(w_query[...], inner, FIRST)
-    query_t[...] = query
-    by_head(w_key[...] * SCALE, query, product(w_query[...], ring, FIRST), to_keys)
-    inner, ring = grad[0:COUNT].T, grad[COUNT:].T
-    grad_t[...] = inner
-    d_att = product(w_out[...], inner)
-    d_att_t[...] = d_att
-    by_head(w_value[...], d_att, product(w_out[...], ring), to_values)
-
-
-def after_kernel(att_t, dq_t, ring_keys, mixed, w_query, w_key, w_out, output, d_normed, d_ring):
-    att_out = product(att_t[...], w_out[...], FIRST)
-    output[...] = mixed[...] + att_out.reshape(ROWS, COLS, CHANNELS)
-    back = w_query[...].T
-    d_normed[...] = product(dq_t[...], back, FIRST)
-    ring = product(w_key[...], ring_keys[...], FIRST)
-    ring = jnp.where(top_half()[:, :RING], ring[:, :RING], ring[:, RING:]) * SCALE
-    d_ring[...] = product(ring, back, FIRST)
+    normed_t[...], grad_t[...] = normed[0:COUNT].T, grad[0:COUNT].T
+    query_t[...] = product(w_query[...], normed_t[...], FIRST)
+    d_att_t[...] = product(w_out[...], grad_t[...])
+    ring = product(w_query[...], normed[COUNT:].T, FIRST)
+    by_head(w_key[...] * SCALE, query_t[...], ring, to_keys)
+    ring = product(w_out[...], grad[COUNT:].T)
+    by_head(w_value[...], d_att_t[...], ring, to_values)
 
 
 def pieces(value, count):
@@ -258,10 +252,12 @@
 
 
 def attend_kernel(
-    core, keys_ref, to_keys, to_values, query_t, d_att_t, normed_t, grad_t, w_key, w_value,
-    own_out, mate_out, att_out, dq_out, ring_out,
+    keys_ref, to_keys, to_values, query_t, d_att_t, normed_t, grad_t,
+    w_query, w_key, w_value, w_out,
+    own_out, mate_out, att_out, d_normed, d_ring,
 ):
-    own = core[0] * (keys_ref.shape[0] // 2)
+    core = here()[2]
+    own = core * (keys_ref.shape[0] // 2)
     mate = keys_ref.shape[0] // 2 - own
     quarter = keys_ref.shape[0] // 4
     keys = jnp.concatenate(
@@ -316,10 +312,13 @@
     g_key = heads(product(y0, q, BOTH), product(y1, q, BOTH), left) * SCALE
     g_value = heads(product(z0, a, BOTH), product(z1, a, BOTH), left)
     g_out = product(att_t, grad_t[...], BOTH)
-    att_out[...] = att_t
-    dq_out[...] = dq_t
-    ring_out[...] = d_query_keys[:, wide:]
-    first = core[0] == 0
+    att_out[...] = product(att_t, w_out[...], FIRST)
+    back = w_query[...].T
+    d_normed[...] = product(dq_t, back, FIRST)
+    ring = product(w_key[...], d_query_keys[:, wide:], FIRST)
+    ring = jnp.where(upper[:, :RING], ring[:, :RING], ring[:, RING:]) * SCALE
+    d_ring[...] = product(ring, back, FIRST)
+    first = core == 0
     by_core = ((g_query, g_key), (g_value, g_out))
     for half in range(2):
         at = half * CHANNELS
@@ -359,9 +358,9 @@
     message[...] = jnp.broadcast_to(share[...][None], message.shape)
 
 
-def relay_kernel(place, received, message, share):
+def relay_kernel(received, message, share):
     peers = received.shape[0]
-    row = place[0]
+    row = here()[0]
     for k in range(peers):
         share[k : k + 1] = received[k, CELLS : CELLS + 1]
     total = received[0]
@@ -370,17 +369,18 @@
     share[peers : peers + 9] = total[CELLS + 1 : CELLS + 10]
     for d in range(3):
         at = peers + 9 + d * CELLS
-        share[at : at + CELLS] = received[jnp.clip(row + d - 1, 0, peers - 1), 0:CELLS]
+        near = jnp.clip(row + d - 1, 0, peers - 1)
+        share[at : at + CELLS] = received[near % 2 * (peers // 2) + near // 2, 0:CELLS]
     share[31:32] = jnp.zeros((1, CHANNELS), jnp.float32)
     message[...] = jnp.broadcast_to(share[...][None], message.shape)
 
 
 def end_kernel(
-    row_count, col_count, place, near, d_normed, normed, inv, grad, d_mixed, weight,
-    d_tokens, g_conv, g_query, g_key, g_value, g_out,
+    row_count, col_count, near, d_normed, normed, inv, grad, d_mixed, weight, mixed, att,
+    output, d_tokens, g_conv, g_query, g_key, g_value, g_out,
     ring, padded,
 ):
-    row, col = place[0], place[1]
+    row, col, _ = here()
     cores, lines = near.shape[0], near.shape[1]
     first = row_count + 9
 
@@ -427,10 +427,11 @@
         for j in range(3):
             total = (
                 total
-                + weight[i, j : j + 1][None]
+                + weight[3 * i + j : 3 * i + j + 1][None]
                 * padded[2 - i : 2 - i + ROWS, 2 - j : 2 - j + COLS]
             )
     d_tokens[...] = total
+    output[...] = mixed[...] + att[...].reshape(ROWS, COLS, CHANNELS)
     root = float(COUNT * row_count * col_count) ** (-0.5)
     conv = near[0, 0, row_count:first]
     for k in range(1, cores * lines):
@@ -440,15 +441,17 @@
         g_conv[k // 3, k % 3 : k % 3 + 1] = conv[k : k + 1]
     blocks = ((g_query, root), (g_key, 1.0 / POOL), (g_value, 1.0 / POOL), (g_out, root))
     for k in range(cores * lines):
-        out, factor = blocks[k * row_count // CHANNELS]
-        at = k * row_count % CHANNELS
+        line = k % lines
+        place_of = k - line + line % (lines // 2) * 2 + line // (lines // 2)
+        out, factor = blocks[place_of * row_count // CHANNELS]
+        at = place_of * row_count % CHANNELS
         out[at : at + row_count] = near[k // lines, k % lines, 0:row_count] * factor
 
 
 def body(tokens, cotangent, conv_weight, w_query, w_key, w_value, w_out):
     row_count, col_count = lax.axis_size(ROW), lax.axis_size(COL)
     chips, lines = lax.axis_size(CHIPS), lax.axis_size(CHIP_COL)
-    place = jnp.stack([lax.axis_index(ROW), lax.axis_index(COL), lax.axis_index("c")])
+    core = lax.axis_index("c")
     tile = (ROWS, COLS, CHANNELS)
     square = (CHANNELS, CHANNELS)
     all_tokens = (COUNT + RING, CHANNELS)
@@ -462,22 +465,20 @@
         scratch_shapes=[pltpu.SemaphoreType.DMA((4,))],
     )(tokens, cotangent)
     mates = pair_gather(mates, "c")
-    (strips,) = call(both_kernel, [f32(2, 3, COLS, CHANNELS)], place, mine, mates, scalars=1)
+    (strips,) = call(both_kernel, [f32(2, 3, COLS, CHANNELS)], mine, mates)
     pairs = [[4 * k, 4 * k + 2] for k in range(row_count // 2)]
     pairs += [[2 * j + 1, 2 * k + 1] for j, k in seam(ROW)]
     strips = pair_gather(strips, ROW + ("c",), pairs)
-    (shared,) = call(
+    shared, taps = call(
         functools.partial(reach_kernel, row_count - 1),
-        [f32(FACING + 3 * ROWS, CHANNELS)],
-        place, tokens, cotangent, strips,
-        scalars=1,
+        [f32(FACING + 3 * ROWS, CHANNELS), f32(9, CHANNELS)],
+        tokens, cotangent, conv_weight, strips,
     )
     shared = pair_gather(shared, "c")
     above, below, beside, beyond = call(
         side_kernel,
         [f32(3, COLS, CHANNELS)] * 2 + [f32(SIDE, CHANNELS)] * 2,
-        place, tokens, cotangent, shared,
-        scalars=1,
+        tokens, cotangent, shared,
     )
     beyond = pair_gather(beyond, COL, seam(COL))
     message, pooled, padded, mixed, normed, inv_std, grad = call(
@@ -491,8 +492,8 @@
             f32(*all_tokens),
             f32(*all_tokens),
         ],
-        place, tokens, cotangent, above, below, beside, beyond, conv_weight,
-        scratch=[(ROWS + 2, 24, CHANNELS)] * 3 + [(SIDE, CHANNELS)] * 2, scalars=1,
+        tokens, cotangent, above, below, beside, beyond, taps,
+        scratch=[(ROWS + 2, 24, CHANNELS)] * 3 + [(SIDE, CHANNELS)] * 2,
     )
 
     message = lax.all_to_all(message, CHIPS, 0, 0, tiled=True)
@@ -505,51 +506,44 @@
         normed, grad, w_query, w_key, w_value, w_out,
         flops=1 << 10,
     )
-    own, mate, att_t, dq_t, ring_keys = call(
+    own, mate, att_out, d_normed, d_ring = call(
         attend_kernel,
         [
             f32(chips, 3 * CHANNELS),
             f32(chips, 3 * CHANNELS),
             f32(*square),
             f32(*square),
-            f32(CHANNELS, HEADS * RING),
+            f32(RING, CHANNELS),
         ],
-        place[2:], keys, *prepared, w_key, w_value,
-        scalars=1, flops=1 << 31,
+        keys, *prepared, w_query, w_key, w_value, w_out,
+        flops=1 << 31,
     )
 
     received = lax.all_gather(mate, "c", axis=0)
-    received = jnp.where(place[2] == 0, received[1], received[0])
+    received = jnp.where(core == 0, received[1], received[0])
     sums = (own + received).reshape(chips, 1, 3 * CHANNELS)
     sums = jnp.sum(lax.all_to_all(sums, CHIPS, 0, 0, tiled=True), 0)
-    output, d_normed, d_ring = call(
-        after_kernel,
-        [f32(*tile), f32(*square), f32(RING, CHANNELS)],
-        att_t, dq_t, ring_keys, mixed, w_query, w_key, w_out,
-        flops=1 << 10,
-    )
     d_mixed, message = call(
         middle_kernel,
         [f32(*tile), f32(row_count, 16, CHANNELS)],
         sums, pooled, d_normed, normed, inv_std, grad, padded,
         scratch=[(16, CHANNELS)],
     )
-    message = lax.all_to_all(message, ROW, 0, 0, tiled=True)
+    message = lax.all_to_all(message, ROW_GROUP, 0, 0, tiled=True)
     (message,) = call(
         relay_kernel,
         [f32(lines, 32, CHANNELS)],
-        place, message,
-        scratch=[(32, CHANNELS)], scalars=1,
+        message,
+        scratch=[(32, CHANNELS)],
     )
     message = lax.all_to_all(message, CHIP_COL, 0, 0, tiled=True)
     near = lax.all_gather(message, "c", axis=0)
-    results = call(
+    return call(
         functools.partial(end_kernel, row_count, col_count),
-        [f32(*tile), f32(3, 3, CHANNELS)] + [f32(*square)] * 4,
-        place, near, d_ring, normed, inv_std, grad, d_mixed, conv_weight,
-        scratch=[(RING, CHANNELS), (ROWS + 2, 24, CHANNELS)], scalars=1,
-    )
-    return (output, *results)
+        [f32(*tile)] * 2 + [f32(3, 3, CHANNELS)] + [f32(*square)] * 4,
+        near, d_ring, normed, inv_std, grad, d_mixed, taps, mixed, att_out,
+        scratch=[(RING, CHANNELS), (ROWS + 2, 24, CHANNELS)],
+    )
 
 
 def solution(mesh):

time: 131 us -> 126 us (0.962)
  blocking collectives: 54.6 us -> 80.5 us
  waiting for transfers between devices: 29 us -> 13.2 us
  starting transfers between devices: 30.1 us -> 20.8 us
  Pallas kernels: 13.5 us -> 9.67 us
  local copies, waits for them, and re-layouts: 1.89 us -> 0.45 us
    all_to_all x1 -> x2, blocking collectives: 11.6 us -> 37.2 us  [the longest x1 26.6 us: body(): sums = jnp.sum(lax.all_to_all(sums, CHIPS, 0, 0, tiled=True), 0)]
    all_to_all x1 -> x0, waiting for transfers between devices: 16.2 us -> none  [body(): sums = jnp.sum(lax.all_to_all(sums, CHIPS, 0, 0, tiled=True), 0)]
    all_to_all x1 -> x0, starting transfers between devices: 9.35 us -> none  [body(): sums = jnp.sum(lax.all_to_all(sums, CHIPS, 0, 0, tiled=True), 0)]
    pallas_call x10 -> x9, Pallas kernels: 12.1 us -> 8.25 us  [call(): pl.pallas_call(kernel, out_shape=outs, in_specs=[in_vmem] * len(args), ou...]
  transfers between devices with their start and end apart: 2 -> 1, of which waited for: 2 -> 1; matrix products, arithmetic and copies ran while one was open for 0% -> 0% of each run, Pallas kernels for 2% -> 1%
where the time goes in v6:
time: 126 us
  blocking collectives  80.5 us (64%)
  starting transfers between devices  20.8 us (17%)
  waiting for transfers between devices  13.2 us (10%)
  Pallas kernels  9.67 us (8%)
    all_to_all x1, blocking collectives, body(): sums = jnp.sum(lax.all_to_all(sums, CHIPS, 0, 0, tiled=True), 0)  26.6 us
    all_to_all x1, starting transfers between devices, body(): message = lax.all_to_all(message, CHIPS, 0, 0, tiled=True)  20.8 us
    all_gather x4, blocking collectives, pair_gather(): return lax.all_gather(value, axis, axis_index_groups=groups, axis=0)  20.2 us
    all_to_all x1, waiting for transfers between devices, body(): message = lax.all_to_all(message, CHIPS, 0, 0, tiled=True)  13.2 us
    all_to_all x1, blocking collectives, body(): message = lax.all_to_all(message, CHIP_COL, 0, 0, tiled=True)  12.9 us
    all_to_all x1, blocking collectives, body(): message = lax.all_to_all(message, ROW_GROUP, 0, 0, tiled=True)  10.6 us
    pallas_call x9, Pallas kernels, call(): pl.pallas_call(kernel, out_shape=outs, in_specs=[in_vmem] * len(args), ou...  8.25 us
    all_gather x1, blocking collectives, body(): near = lax.all_gather(message, 'c', axis=0)  5.65 us
  transfers between devices with their start and end apart: 1, of which 1 were waited for; matrix products, arithmetic and copies ran while one was open for 0% of the time, Pallas kernels for 1%

profile of v6, /device:TPU:1, one launch (start us, length us, event | category | flops | bytes accessed | tf_op | source)
XLA Modules:
  0.0 125.7 jit_solution(7133939916244537322)
XLA Ops:
  0.6 1.4 %shard_map.126 = (f32[3,16,128]{2,1,0:T(8,128)}, f32[3,16,128]{2,1,0:T(8,128)}) custom-call(f32[8,16,128]{2,1,0:T(8,128)} %tokens.7, f32[8,16,128]{2,1,0:T(8,128)} %grad.7), custom_call_target="tpu_custom_call" | custom-call | tf_op jit(solution)/shard_map/pallas_call | solution.py:460
  2.1 0.0 copy-start.6
  2.1 8.6 %all-gather = f32[6,16,128]{2,1,0:T(8,128)S(1)} all-gather(f32[3,16,128]{2,1,0:T(8,128)} %get-tuple-element.36), channel_id=2, replica_groups=mesh['y'=8,'xl'=2,'xh'=2,'z'=8,'c'=2] {'c'}, dimensions={0}, use_global_device_ids=true | all-gather | bytes 73728 | tf_op jit(solution)/shard_map/all_gather | solution.py:82
  10.7 0.0 copy-start
  10.7 0.0 copy-start.1
  10.7 5.9 %all-gather.1 = f32[4,3,16,128]{3,2,1,0:T(8,128)S(1)} all-gather(f32[2,3,16,128]{3,2,1,0:T(8,128)S(1)} %shard_map.127), channel_id=3, replica_groups={{0,32},{64,96},{128,160},{192,224},{256,288},{320,352},{384,416},{448,4..., dimensions={0}, use_global_device_ids=true | all-gather | bytes 147456 | tf_op jit(solution)/shard_map/all_gather | solution.py:82
  16.6 1.9 %all-gather.2 = f32[240,128]{1,0:T(8,128)S(1)} all-gather(f32[120,128]{1,0:T(8,128)S(1)} %get-tuple-element.37), channel_id=4, replica_groups=mesh['y'=8,'xl'=2,'xh'=2,'z'=8,'c'=2] {'c'}, dimensions={0}, use_global_device_ids=true | all-gather | bytes 184320 | tf_op jit(solution)/shard_map/all_gather | solution.py:82
  18.5 3.9 %all-gather.3 = f32[80,128]{1,0:T(8,128)S(1)} all-gather(f32[40,128]{1,0:T(8,128)S(1)} %get-tuple-element.41), channel_id=5, replica_groups={{1,2},{3,4},{5,6},{7,8},{9,10},{11,12},{13,14},{15,16},{17,18},{19,20},..., dimensions={0}, use_global_device_ids=true | all-gather | bytes 61440 | tf_op jit(solution)/shard_map/all_gather | solution.py:82
  22.4 1.2 shard_map.130
  23.7 20.8 %all-to-all-start = ((f32[256,2,128]{2,1,0:T(2,128)}), f32[256,2,128]{2,1,0:T(2,128)S(1)}, u32[]{:S(2)}, u32[]{:S(2)}) async-start(f32[256,2,128]{2,1,0:T(2,128)} %get-tuple-element.43), calls=%async_computation | async-start | bytes 524288 | tf_op jit(solution)/shard_map/all_to_all | solution.py:499
  44.5 1.0 shard_map.131
  45.5 13.2 %all-to-all-done = f32[256,2,128]{2,1,0:T(2,128)S(1)} async-done(((f32[256,2,128]{2,1,0:T(2,128)}), f32[256,2,128]{2,1,0:T(2,128)S(1)}, u32[]{:S(2)}, u32[]{:S(2)}) %all-to-all-start) | async-done | bytes 262176 | tf_op jit(solution)/shard_map/all_to_all | solution.py:499
  58.7 2.2 %all_gather.47 = f32[512,2,128]{2,1,0:T(2,128)S(1)} all-gather(f32[256,2,128]{2,1,0:T(2,128)S(1)} %all-to-all-done), channel_id=1, replica_groups=mesh['y'=8,'xl'=2,'xh'=2,'z'=8,'c'=2] {'c'}, dimensions={0}, use_global_device_ids=true | all-gather | bytes 786432 | tf_op jit(solution)/shard_map/all_gather | solution.py:500
  60.9 4.8 %shard_map.132 = (f32[256,384]{1,0:T(8,128)S(1)}, f32[256,384]{1,0:T(8,128)S(1)}, f32[128,128]{1,0:T(8,128)S(1)}, f32[128,128]{1,0:T(8,128)S(1)}, f32[64,128]{1,0:T(8,128)S(1)}) custom-call(f32[1024,128]{1,0:T(8,128)S(1)} %bitcast.9, f32[128,384]{1,0:T(8,128)S(1)} %get-tuple-element.46.to_keys, f32[128,384]{1,0:T(8,128)S(1)} %get-tuple-element.47.to_values, ...), custom_call_target="tpu_custom_call" | custom-call | flops 2147483648 | bytes 2147483648 | tf_op jit(solution)/shard_map/pallas_call | solution.py:65
  65.7 2.4 %all-gather.4 = f32[512,384]{1,0:T(8,128)S(1)} all-gather(f32[256,384]{1,0:T(8,128)S(1)} %get-tuple-element.53), channel_id=6, replica_groups=mesh['y'=8,'xl'=2,'xh'=2,'z'=8,'c'=2] {'c'}, dimensions={0}, use_global_device_ids=true | all-gather | bytes 1179648 | tf_op jit(solution)/shard_map/all_gather | solution.py:522
  68.1 0.1 fusion.1
  68.1 0.4 copy.14
  68.5 26.6 %all_to_all.20 = f32[256,1,384]{2,1,0:T(1,128)S(1)} all-to-all(f32[256,1,384]{2,1,0:T(1,128)S(1)} %copy.14), channel_id=1, replica_groups=mesh['y'=8,'xl'=2,'xh'=2,'z'=8,'c'=2] {'z','xh','xl','y'}, dimensions={0} | all-to-all | bytes 786432 | tf_op jit(solution)/shard_map/all_to_all | solution.py:525
  95.1 0.3 reduce_sum.11
  95.4 0.3 shard_map.133
  95.7 10.6 %all_to_all.21.received = f32[16,16,128]{2,1,0:T(8,128)S(1)} all-to-all(f32[16,16,128]{2,1,0:T(8,128)S(1)} %get-tuple-element.58), channel_id=1, replica_groups=mesh['y'=8,'xl'=2,'xh'=2,'z'=8,'c'=2] {'xl','y'}, dimensions={0} | all-to-all | bytes 262144 | tf_op jit(solution)/shard_map/all_to_all | solution.py:532
  106.4 12.9 %all_to_all.22 = f32[16,32,128]{2,1,0:T(8,128)S(1)} all-to-all(f32[16,32,128]{2,1,0:T(8,128)S(1)} %shard_map.134), channel_id=1, replica_groups=mesh['y'=8,'xl'=2,'xh'=2,'z'=8,'c'=2] {'xh','z'}, dimensions={0} | all-to-all | bytes 524288 | tf_op jit(solution)/shard_map/all_to_all | solution.py:539
  119.3 5.7 %all-gather.5 = f32[32,32,128]{2,1,0:T(8,128)S(1)} all-gather(f32[16,32,128]{2,1,0:T(8,128)S(1)} %all_to_all.22), channel_id=7, replica_groups=mesh['y'=8,'xl'=2,'xh'=2,'z'=8,'c'=2] {'c'}, dimensions={0}, use_global_device_ids=true | all-gather | bytes 786432 | tf_op jit(solution)/shard_map/all_gather | solution.py:540
  124.9 0.8 shard_map.135
  (18 shorter events, 0.1 us)
Async XLA Ops:
  2.1 8.6 %copy-start.6 = (f32[3,16,128]{2,1,0:T(8,128)S(1)}, f32[3,16,128]{2,1,0:T(8,128)}, u32[]{:S(2)}) copy-start(f32[3,16,128]{2,1,0:T(8,128)} %get-tuple-element.35.mine) | copy-start | bytes 73732
  10.7 5.9 %copy-start = (f32[8,16,128]{2,1,0:T(8,128)S(1)}, f32[8,16,128]{2,1,0:T(8,128)}, u32[]{:S(2)}) copy-start(f32[8,16,128]{2,1,0:T(8,128)} %tokens.7) | copy-start | bytes 196612
  10.7 5.9 %copy-start.1 = (f32[8,16,128]{2,1,0:T(8,128)S(1)}, f32[8,16,128]{2,1,0:T(8,128)}, u32[]{:S(2)}) copy-start(f32[8,16,128]{2,1,0:T(8,128)} %grad.7) | copy-start | bytes 196612
  10.7 5.9 %copy-start.7 = (f32[3,3,128]{2,1,0:T(4,128)S(1)}, f32[3,3,128]{2,1,0:T(4,128)}, u32[]{:S(2)}) copy-start(f32[3,3,128]{2,1,0:T(4,128)} %weight.1) | copy-start | bytes 13828
  23.7 20.8 %copy-start.2 = (f32[128,128]{1,0:T(8,128)S(1)}, f32[128,128]{1,0:T(8,128)}, u32[]{:S(2)}) copy-start(f32[128,128]{1,0:T(8,128)} %w_query.3) | copy-start | bytes 196612
  23.7 20.8 %copy-start.3 = (f32[128,128]{1,0:T(8,128)S(1)}, f32[128,128]{1,0:T(8,128)}, u32[]{:S(2)}) copy-start(f32[128,128]{1,0:T(8,128)} %w_key.3) | copy-start | bytes 196612
  23.7 20.8 %copy-start.4 = (f32[128,128]{1,0:T(8,128)S(1)}, f32[128,128]{1,0:T(8,128)}, u32[]{:S(2)}) copy-start(f32[128,128]{1,0:T(8,128)} %w_value.3) | copy-start | bytes 196612
  23.7 20.8 %copy-start.5 = (f32[128,128]{1,0:T(8,128)S(1)}, f32[128,128]{1,0:T(8,128)}, u32[]{:S(2)}) copy-start(f32[128,128]{1,0:T(8,128)} %w_out.3) | copy-start | bytes 196612
  23.7 35.0 %all-to-all-start = ((f32[256,2,128]{2,1,0:T(2,128)}), f32[256,2,128]{2,1,0:T(2,128)S(1)}, u32[]{:S(2)}, u32[]{:S(2)}) async-start(f32[256,2,128]{2,1,0:T(2,128)} %get-tuple-element.43), calls=%async_computation | async-start | bytes 524288 | tf_op jit(solution)/shard_map/all_to_all | solution.py:499

commit v7 on v6

--- a/solution.py
+++ b/solution.py
@@ -76,6 +76,17 @@
 def seam(axis):
     peers = lax.axis_size(axis)
     return [[k, (k + 1) % peers] for k in range(1, peers, 2)]
+
+
+def column_seam():
+    rows, columns = lax.axis_size(ROW), lax.axis_size(COL)
+    pairs = []
+    for row in range(rows):
+        at = row * columns
+        pairs += [[at + k, at + k + 1] for k in range(1, columns - 1, 2)]
+        if row % 2 == 0:
+            pairs += [[k, k + columns] for k in (at, at + columns - 1)]
+    return pairs
 
 
 def pair_gather(value, axis, groups=None):
@@ -251,6 +262,16 @@
     return product(left, right, dims, lax.Precision.DEFAULT)
 
 
+def three(left, right, dims=((1,), (0,))):
+    (left_high, left_low), (right_high, right_low) = pieces(left, 2), pieces(right, 2)
+    (left_axis,), (right_axis,) = dims
+    return single(
+        jnp.concatenate([left_high, left_high, left_low], left_axis),
+        jnp.concatenate([right_high, right_low, right_high], right_axis),
+        dims,
+    )
+
+
 def attend_kernel(
     keys_ref, to_keys, to_values, query_t, d_att_t, normed_t, grad_t,
     w_query, w_key, w_value, w_out,
@@ -303,21 +324,25 @@
     def heads(first, second, mask=upper):
         return jnp.where(mask, first, second)
 
-    z0, z1 = att_keys[:, :COUNT], att_keys[:, COUNT:wide]
-    y0, y1 = d_query_keys[:, :COUNT], d_query_keys[:, COUNT:wide]
-    att_t = heads(product(w_value[...], z0, FIRST), product(w_value[...], z1, FIRST))
-    dq_t = heads(product(w_key[...], y0, FIRST), product(w_key[...], y1, FIRST)) * SCALE
-    q, a = query_t[...], d_att_t[...]
-    g_query = product(normed_t[...], dq_t, BOTH)
-    g_key = heads(product(y0, q, BOTH), product(y1, q, BOTH), left) * SCALE
-    g_value = heads(product(z0, a, BOTH), product(z1, a, BOTH), left)
-    g_out = product(att_t, grad_t[...], BOTH)
-    att_out[...] = product(att_t, w_out[...], FIRST)
+    def rows(value):
+        return jnp.concatenate([value[:, :COUNT], value[:, COUNT:wide]])
+
+    att = three(w_value[...], att_keys, FIRST)
+    att_t = heads(att[:, :COUNT], att[:, COUNT:])
+    d_query = three(w_key[...] * SCALE, d_query_keys, FIRST)
+    dq_t = heads(d_query[:, :COUNT], d_query[:, COUNT:wide])
+    ring = d_query[:, wide:]
+    ring = jnp.where(upper[:, :RING], ring[:, :RING], ring[:, RING:])
+    g_query = three(normed_t[...], dq_t, BOTH)
+    g_out = three(att_t, grad_t[...], BOTH)
+    g_key = three(rows(d_query_keys), query_t[...], BOTH)
+    g_key = heads(g_key[:CHANNELS], g_key[CHANNELS:], left) * SCALE
+    g_value = three(rows(att_keys), d_att_t[...], BOTH)
+    g_value = heads(g_value[:CHANNELS], g_value[CHANNELS:], left)
+    att_out[...] = three(att_t, w_out[...], FIRST)
     back = w_query[...].T
-    d_normed[...] = product(dq_t, back, FIRST)
-    ring = product(w_key[...], d_query_keys[:, wide:], FIRST)
-    ring = jnp.where(upper[:, :RING], ring[:, :RING], ring[:, RING:]) * SCALE
-    d_ring[...] = product(ring, back, FIRST)
+    d_normed[...] = three(dq_t, back, FIRST)
+    d_ring[...] = three(ring, back, FIRST)
     first = core == 0
     by_core = ((g_query, g_key), (g_value, g_out))
     for half in range(2):
@@ -480,7 +505,7 @@
         [f32(3, COLS, CHANNELS)] * 2 + [f32(SIDE, CHANNELS)] * 2,
         tokens, cotangent, shared,
     )
-    beyond = pair_gather(beyond, COL, seam(COL))
+    beyond = pair_gather(beyond, ROW + COL, column_seam())
     message, pooled, padded, mixed, normed, inv_std, grad = call(
         functools.partial(mix_kernel, col_count - 1),
         [

time: 126 us -> 125 us (level)
  starting transfers between devices: 20.8 us -> 18.5 us
  blocking collectives: 80.5 us -> 82 us
    all_to_all x1, starting transfers between devices: 20.8 us -> 18.5 us  [body(): message = lax.all_to_all(message, CHIPS, 0, 0, tiled=True)]
where the time goes in v7:
time: 125 us; the launch traced here: 124 us
  blocking collectives  82 us (66%)
  starting transfers between devices  18.5 us (15%)
  waiting for transfers between devices  13.9 us (11%)
  Pallas kernels  8.42 us (7%)
    all_to_all x1, blocking collectives, body(): sums = jnp.sum(lax.all_to_all(sums, CHIPS, 0, 0, tiled=True), 0)  26.4 us
    all_gather x4, blocking collectives, pair_gather(): return lax.all_gather(value, axis, axis_index_groups=groups, axis=0)  20.5 us
    all_to_all x1, starting transfers between devices, body(): message = lax.all_to_all(message, CHIPS, 0, 0, tiled=True)  18.5 us
    all_to_all x1, waiting for transfers between devices, body(): message = lax.all_to_all(message, CHIPS, 0, 0, tiled=True)  13.9 us
    all_to_all x1, blocking collectives, body(): message = lax.all_to_all(message, CHIP_COL, 0, 0, tiled=True)  13 us
    all_to_all x1, blocking collectives, body(): message = lax.all_to_all(message, ROW_GROUP, 0, 0, tiled=True)  10.7 us
    pallas_call x9, Pallas kernels, call(): pl.pallas_call(kernel, out_shape=outs, in_specs=[in_vmem] * len(args), ou...  7 us
    all_gather x1, blocking collectives, body(): near = lax.all_gather(message, 'c', axis=0)  5.66 us
  transfers between devices with their start and end apart: 1, of which 1 were waited for; matrix products, arithmetic and copies ran while one was open for 0% of the time, Pallas kernels for 1%

profile of v7, /device:TPU:1, one launch (start us, length us, event | category | flops | bytes accessed | tf_op | source)
XLA Modules:
  0.0 124.4 jit_solution(16360200886689019288)
XLA Ops:
  0.6 1.4 %shard_map.126 = (f32[3,16,128]{2,1,0:T(8,128)}, f32[3,16,128]{2,1,0:T(8,128)}) custom-call(f32[8,16,128]{2,1,0:T(8,128)} %tokens.7, f32[8,16,128]{2,1,0:T(8,128)} %grad.7), custom_call_target="tpu_custom_call" | custom-call | tf_op jit(solution)/shard_map/pallas_call | solution.py:485
  2.1 0.0 copy-start.6
  2.1 8.6 %all-gather = f32[6,16,128]{2,1,0:T(8,128)S(1)} all-gather(f32[3,16,128]{2,1,0:T(8,128)} %get-tuple-element.36), channel_id=2, replica_groups=mesh['y'=8,'xl'=2,'xh'=2,'z'=8,'c'=2] {'c'}, dimensions={0}, use_global_device_ids=true | all-gather | bytes 73728 | tf_op jit(solution)/shard_map/all_gather | solution.py:93
  10.7 0.0 copy-start
  10.7 0.0 copy-start.1
  10.7 5.9 %all-gather.1 = f32[4,3,16,128]{3,2,1,0:T(8,128)S(1)} all-gather(f32[2,3,16,128]{3,2,1,0:T(8,128)S(1)} %shard_map.127), channel_id=3, replica_groups={{0,32},{64,96},{128,160},{192,224},{256,288},{320,352},{384,416},{448,4..., dimensions={0}, use_global_device_ids=true | all-gather | bytes 147456 | tf_op jit(solution)/shard_map/all_gather | solution.py:93
  16.6 1.9 %all-gather.2 = f32[240,128]{1,0:T(8,128)S(1)} all-gather(f32[120,128]{1,0:T(8,128)S(1)} %get-tuple-element.37), channel_id=4, replica_groups=mesh['y'=8,'xl'=2,'xh'=2,'z'=8,'c'=2] {'c'}, dimensions={0}, use_global_device_ids=true | all-gather | bytes 184320 | tf_op jit(solution)/shard_map/all_gather | solution.py:93
  18.5 4.2 %all-gather.3 = f32[80,128]{1,0:T(8,128)S(1)} all-gather(f32[40,128]{1,0:T(8,128)S(1)} %get-tuple-element.41), channel_id=5, replica_groups={{1,2},{3,4},{5,6},{7,8},{9,10},{11,12},{13,14},{15,16},{17,18},{19,20},..., dimensions={0}, use_global_device_ids=true | all-gather | bytes 61440 | tf_op jit(solution)/shard_map/all_gather | solution.py:93
  22.7 1.2 shard_map.130
  24.0 18.5 %all-to-all-start = ((f32[256,2,128]{2,1,0:T(2,128)}), f32[256,2,128]{2,1,0:T(2,128)S(1)}, u32[]{:S(2)}, u32[]{:S(2)}) async-start(f32[256,2,128]{2,1,0:T(2,128)} %get-tuple-element.43), calls=%async_computation | async-start | bytes 524288 | tf_op jit(solution)/shard_map/all_to_all | solution.py:524
  42.5 1.0 shard_map.131
  43.6 13.9 %all-to-all-done = f32[256,2,128]{2,1,0:T(2,128)S(1)} async-done(((f32[256,2,128]{2,1,0:T(2,128)}), f32[256,2,128]{2,1,0:T(2,128)S(1)}, u32[]{:S(2)}, u32[]{:S(2)}) %all-to-all-start) | async-done | bytes 262176 | tf_op jit(solution)/shard_map/all_to_all | solution.py:524
  57.5 3.3 %all_gather.47 = f32[512,2,128]{2,1,0:T(2,128)S(1)} all-gather(f32[256,2,128]{2,1,0:T(2,128)S(1)} %all-to-all-done), channel_id=1, replica_groups=mesh['y'=8,'xl'=2,'xh'=2,'z'=8,'c'=2] {'c'}, dimensions={0}, use_global_device_ids=true | all-gather | bytes 786432 | tf_op jit(solution)/shard_map/all_gather | solution.py:525
  60.8 3.6 %shard_map.132 = (f32[256,384]{1,0:T(8,128)S(1)}, f32[256,384]{1,0:T(8,128)S(1)}, f32[128,128]{1,0:T(8,128)S(1)}, f32[128,128]{1,0:T(8,128)S(1)}, f32[64,128]{1,0:T(8,128)S(1)}) custom-call(f32[1024,128]{1,0:T(8,128)S(1)} %bitcast.9, f32[128,384]{1,0:T(8,128)S(1)} %get-tuple-element.46.to_keys, f32[128,384]{1,0:T(8,128)S(1)} %get-tuple-element.47.to_values, ...), custom_call_target="tpu_custom_call" | custom-call | flops 2147483648 | bytes 2147483648 | tf_op jit(solution)/shard_map/pallas_call | solution.py:65
  64.3 2.4 %all-gather.4 = f32[512,384]{1,0:T(8,128)S(1)} all-gather(f32[256,384]{1,0:T(8,128)S(1)} %get-tuple-element.53), channel_id=6, replica_groups=mesh['y'=8,'xl'=2,'xh'=2,'z'=8,'c'=2] {'c'}, dimensions={0}, use_global_device_ids=true | all-gather | bytes 1179648 | tf_op jit(solution)/shard_map/all_gather | solution.py:547
  66.7 0.1 fusion.1
  66.8 0.4 copy.14
  67.2 26.4 %all_to_all.20 = f32[256,1,384]{2,1,0:T(1,128)S(1)} all-to-all(f32[256,1,384]{2,1,0:T(1,128)S(1)} %copy.14), channel_id=1, replica_groups=mesh['y'=8,'xl'=2,'xh'=2,'z'=8,'c'=2] {'z','xh','xl','y'}, dimensions={0} | all-to-all | bytes 786432 | tf_op jit(solution)/shard_map/all_to_all | solution.py:550
  93.6 0.3 reduce_sum.11
  93.9 0.3 shard_map.133
  94.1 10.7 %all_to_all.21.received = f32[16,16,128]{2,1,0:T(8,128)S(1)} all-to-all(f32[16,16,128]{2,1,0:T(8,128)S(1)} %get-tuple-element.58), channel_id=1, replica_groups=mesh['y'=8,'xl'=2,'xh'=2,'z'=8,'c'=2] {'xl','y'}, dimensions={0} | all-to-all | bytes 262144 | tf_op jit(solution)/shard_map/all_to_all | solution.py:557
  104.9 13.0 %all_to_all.22 = f32[16,32,128]{2,1,0:T(8,128)S(1)} all-to-all(f32[16,32,128]{2,1,0:T(8,128)S(1)} %shard_map.134), channel_id=1, replica_groups=mesh['y'=8,'xl'=2,'xh'=2,'z'=8,'c'=2] {'xh','z'}, dimensions={0} | all-to-all | bytes 524288 | tf_op jit(solution)/shard_map/all_to_all | solution.py:564
  117.9 5.7 %all-gather.5 = f32[32,32,128]{2,1,0:T(8,128)S(1)} all-gather(f32[16,32,128]{2,1,0:T(8,128)S(1)} %all_to_all.22), channel_id=7, replica_groups=mesh['y'=8,'xl'=2,'xh'=2,'z'=8,'c'=2] {'c'}, dimensions={0}, use_global_device_ids=true | all-gather | bytes 786432 | tf_op jit(solution)/shard_map/all_gather | solution.py:565
  123.6 0.8 shard_map.135
  (18 shorter events, 0.1 us)
Async XLA Ops:
  2.1 8.6 %copy-start.6 = (f32[3,16,128]{2,1,0:T(8,128)S(1)}, f32[3,16,128]{2,1,0:T(8,128)}, u32[]{:S(2)}) copy-start(f32[3,16,128]{2,1,0:T(8,128)} %get-tuple-element.35.mine) | copy-start | bytes 73732
  10.7 5.9 %copy-start = (f32[8,16,128]{2,1,0:T(8,128)S(1)}, f32[8,16,128]{2,1,0:T(8,128)}, u32[]{:S(2)}) copy-start(f32[8,16,128]{2,1,0:T(8,128)} %tokens.7) | copy-start | bytes 196612
  10.7 5.9 %copy-start.1 = (f32[8,16,128]{2,1,0:T(8,128)S(1)}, f32[8,16,128]{2,1,0:T(8,128)}, u32[]{:S(2)}) copy-start(f32[8,16,128]{2,1,0:T(8,128)} %grad.7) | copy-start | bytes 196612
  10.7 5.9 %copy-start.7 = (f32[3,3,128]{2,1,0:T(4,128)S(1)}, f32[3,3,128]{2,1,0:T(4,128)}, u32[]{:S(2)}) copy-start(f32[3,3,128]{2,1,0:T(4,128)} %weight.1) | copy-start | bytes 13828
  24.0 18.5 %copy-start.2 = (f32[128,128]{1,0:T(8,128)S(1)}, f32[128,128]{1,0:T(8,128)}, u32[]{:S(2)}) copy-start(f32[128,128]{1,0:T(8,128)} %w_query.3) | copy-start | bytes 196612
  24.0 18.5 %copy-start.3 = (f32[128,128]{1,0:T(8,128)S(1)}, f32[128,128]{1,0:T(8,128)}, u32[]{:S(2)}) copy-start(f32[128,128]{1,0:T(8,128)} %w_key.3) | copy-start | bytes 196612
  24.0 18.5 %copy-start.4 = (f32[128,128]{1,0:T(8,128)S(1)}, f32[128,128]{1,0:T(8,128)}, u32[]{:S(2)}) copy-start(f32[128,128]{1,0:T(8,128)} %w_value.3) | copy-start | bytes 196612
  24.0 18.5 %copy-start.5 = (f32[128,128]{1,0:T(8,128)S(1)}, f32[128,128]{1,0:T(8,128)}, u32[]{:S(2)}) copy-start(f32[128,128]{1,0:T(8,128)} %w_out.3) | copy-start | bytes 196612
  24.0 33.5 %all-to-all-start = ((f32[256,2,128]{2,1,0:T(2,128)}), f32[256,2,128]{2,1,0:T(2,128)S(1)}, u32[]{:S(2)}, u32[]{:S(2)}) async-start(f32[256,2,128]{2,1,0:T(2,128)} %get-tuple-element.43), calls=%async_computation | async-start | bytes 524288 | tf_op jit(solution)/shard_map/all_to_all | solution.py:524

commit v8 on v7

--- a/solution.py
+++ b/solution.py
@@ -170,7 +170,7 @@
 def mix_kernel(
     last_col, tokens, grad, above, below, beside, beyond, weight,
     message, pooled_out, padded, mixed_out, normed_out, inv_out, grad_out,
-    normed_ext, inv_ext, mixed_ext, before, after,
+    normed_ext, inv_ext, mixed_ext, before, after, rows,
 ):
     col = here()[1]
     even = col % 2 == 0
@@ -200,7 +200,10 @@
         pooled_n, pooled_inv = normalize(pooled)
         pooled_out[cell : cell + 1] = pooled_n
         pooled_out[CELLS + cell : CELLS + cell + 1] = jnp.broadcast_to(pooled_inv, pooled_n.shape)
-    message[...] = jnp.broadcast_to(pooled_out[0:CELLS][None], message.shape)
+    for k in range(8):
+        rows[k : k + 1] = pooled_out[k % CELLS : k % CELLS + 1]
+    tiles = jnp.broadcast_to(rows[...][None], (message.shape[0] // 8, 8, CHANNELS))
+    message[...] = tiles.reshape(message.shape)
     mixed_out[...] = mixed_ext[1 : 1 + ROWS, 1 : 1 + COLS]
     for ext, out in ((normed_ext, normed_out), (inv_ext, inv_out)):
         out[0:COUNT] = ext[1 : 1 + ROWS, 1 : 1 + COLS].reshape(COUNT, CHANNELS)
@@ -484,7 +487,7 @@
     anywhere = pl.BlockSpec(memory_space=pl.ANY)
     mine, mates = pl.pallas_call(
         edge_kernel,
-        out_shape=[f32(3, COLS, CHANNELS)] * 2,
+        out_shape=[pltpu.VMEM((3, COLS, CHANNELS), jnp.float32)] * 2,
         in_specs=[anywhere] * 2,
         out_specs=[pl.BlockSpec(memory_space=pltpu.VMEM)] * 2,
         scratch_shapes=[pltpu.SemaphoreType.DMA((4,))],
@@ -509,7 +512,7 @@
     message, pooled, padded, mixed, normed, inv_std, grad = call(
         functools.partial(mix_kernel, col_count - 1),
         [
-            f32(chips, CELLS, CHANNELS),
+            pltpu.VMEM((chips * CELLS, CHANNELS), jnp.float32),
             f32(2 * CELLS, CHANNELS),
             f32(ROWS + 4, 24, CHANNELS),
             f32(*tile),
@@ -518,9 +521,10 @@
             f32(*all_tokens),
         ],
         tokens, cotangent, above, below, beside, beyond, taps,
-        scratch=[(ROWS + 2, 24, CHANNELS)] * 3 + [(SIDE, CHANNELS)] * 2,
-    )
-
+        scratch=[(ROWS + 2, 24, CHANNELS)] * 3 + [(SIDE, CHANNELS)] * 2 + [(8, CHANNELS)],
+    )
+
+    message = message.reshape(chips, CELLS, CHANNELS)
     message = lax.all_to_all(message, CHIPS, 0, 0, tiled=True)
     keys = lax.all_gather(message, "c", axis=0, tiled=True).reshape(-1, CHANNELS)
 

time: 125 us -> 124 us (level)
  no operation moved by 1% of the time
where the time goes in v8:
time: 124 us; the launch traced here: 123 us
  blocking collectives  81.6 us (66%)
  starting transfers between devices  18.5 us (15%)
  waiting for transfers between devices  13.9 us (11%)
  Pallas kernels  7.75 us (6%)
    all_to_all x1, blocking collectives, body(): sums = jnp.sum(lax.all_to_all(sums, CHIPS, 0, 0, tiled=True), 0)  26.2 us
    all_gather x4, blocking collectives, pair_gather(): return lax.all_gather(value, axis, axis_index_groups=groups, axis=0)  20.3 us
    all_to_all x1, starting transfers between devices, body(): message = lax.all_to_all(message, CHIPS, 0, 0, tiled=True)  18.5 us
    all_to_all x1, waiting for transfers between devices, body(): message = lax.all_to_all(message, CHIPS, 0, 0, tiled=True)  13.9 us
    all_to_all x1, blocking collectives, body(): message = lax.all_to_all(message, CHIP_COL, 0, 0, tiled=True)  13 us
    all_to_all x1, blocking collectives, body(): message = lax.all_to_all(message, ROW_GROUP, 0, 0, tiled=True)  10.7 us
    pallas_call x9, Pallas kernels, call(): pl.pallas_call(kernel, out_shape=outs, in_specs=[in_vmem] * len(args), ou...  6.95 us
    all_gather x1, blocking collectives, body(): near = lax.all_gather(message, 'c', axis=0)  5.66 us
  transfers between devices with their start and end apart: 1, of which 1 were waited for; matrix products, arithmetic and copies ran while one was open for 0% of the time, Pallas kernels for 1%

profile of v8, /device:TPU:1, one launch (start us, length us, event | category | flops | bytes accessed | tf_op | source)
XLA Modules:
  0.0 123.3 jit_solution(2147378189622911862)
XLA Ops:
  0.6 0.8 shard_map.126
  1.4 8.4 %all-gather = f32[6,16,128]{2,1,0:T(8,128)S(1)} all-gather(f32[3,16,128]{2,1,0:T(8,128)S(1)} %get-tuple-element.36), channel_id=2, replica_groups=mesh['y'=8,'xl'=2,'xh'=2,'z'=8,'c'=2] {'c'}, dimensions={0}, use_global_device_ids=true | all-gather | bytes 73728 | tf_op jit(solution)/shard_map/all_gather | solution.py:93
  9.8 0.0 copy-start
  9.8 0.0 copy-start.1
  9.9 0.0 copy-start.6
  9.9 5.9 %all-gather.1 = f32[4,3,16,128]{3,2,1,0:T(8,128)S(1)} all-gather(f32[2,3,16,128]{3,2,1,0:T(8,128)S(1)} %shard_map.127), channel_id=3, replica_groups={{0,32},{64,96},{128,160},{192,224},{256,288},{320,352},{384,416},{448,4..., dimensions={0}, use_global_device_ids=true | all-gather | bytes 147456 | tf_op jit(solution)/shard_map/all_gather | solution.py:93
  15.8 1.9 %all-gather.2 = f32[240,128]{1,0:T(8,128)S(1)} all-gather(f32[120,128]{1,0:T(8,128)S(1)} %get-tuple-element.37), channel_id=4, replica_groups=mesh['y'=8,'xl'=2,'xh'=2,'z'=8,'c'=2] {'c'}, dimensions={0}, use_global_device_ids=true | all-gather | bytes 184320 | tf_op jit(solution)/shard_map/all_gather | solution.py:93
  17.7 4.2 %all-gather.3 = f32[80,128]{1,0:T(8,128)S(1)} all-gather(f32[40,128]{1,0:T(8,128)S(1)} %get-tuple-element.41), channel_id=5, replica_groups={{1,2},{3,4},{5,6},{7,8},{9,10},{11,12},{13,14},{15,16},{17,18},{19,20},..., dimensions={0}, use_global_device_ids=true | all-gather | bytes 61440 | tf_op jit(solution)/shard_map/all_gather | solution.py:93
  21.9 1.2 shard_map.130
  23.1 18.5 %all-to-all-start = ((f32[256,2,128]{2,1,0:T(2,128)}), f32[256,2,128]{2,1,0:T(2,128)S(1)}, u32[]{:S(2)}, u32[]{:S(2)}) async-start(f32[256,2,128]{2,1,0:T(2,128)} %bitcast.4), calls=%async_computation | async-start | bytes 524288 | tf_op jit(solution)/shard_map/all_to_all | solution.py:528
  41.6 1.0 shard_map.131
  42.7 13.9 %all-to-all-done = f32[256,2,128]{2,1,0:T(2,128)S(1)} async-done(((f32[256,2,128]{2,1,0:T(2,128)}), f32[256,2,128]{2,1,0:T(2,128)S(1)}, u32[]{:S(2)}, u32[]{:S(2)}) %all-to-all-start) | async-done | bytes 262176 | tf_op jit(solution)/shard_map/all_to_all | solution.py:528
  56.6 3.3 %all_gather.47 = f32[512,2,128]{2,1,0:T(2,128)S(1)} all-gather(f32[256,2,128]{2,1,0:T(2,128)S(1)} %all-to-all-done), channel_id=1, replica_groups=mesh['y'=8,'xl'=2,'xh'=2,'z'=8,'c'=2] {'c'}, dimensions={0}, use_global_device_ids=true | all-gather | bytes 786432 | tf_op jit(solution)/shard_map/all_gather | solution.py:529
  59.9 3.6 %shard_map.132 = (f32[256,384]{1,0:T(8,128)S(1)}, f32[256,384]{1,0:T(8,128)S(1)}, f32[128,128]{1,0:T(8,128)S(1)}, f32[128,128]{1,0:T(8,128)S(1)}, f32[64,128]{1,0:T(8,128)S(1)}) custom-call(f32[1024,128]{1,0:T(8,128)S(1)} %bitcast.10, f32[128,384]{1,0:T(8,128)S(1)} %get-tuple-element.46.to_keys, f32[128,384]{1,0:T(8,128)S(1)} %get-tuple-element.47.to_values, ...), custom_call_target="tpu_custom_call" | custom-call | flops 2147483648 | bytes 2147483648 | tf_op jit(solution)/shard_map/pallas_call | solution.py:65
  63.4 2.4 %all-gather.4 = f32[512,384]{1,0:T(8,128)S(1)} all-gather(f32[256,384]{1,0:T(8,128)S(1)} %get-tuple-element.53), channel_id=6, replica_groups=mesh['y'=8,'xl'=2,'xh'=2,'z'=8,'c'=2] {'c'}, dimensions={0}, use_global_device_ids=true | all-gather | bytes 1179648 | tf_op jit(solution)/shard_map/all_gather | solution.py:551
  65.8 0.1 fusion.1
  65.8 0.4 copy.14
  66.3 26.2 %all_to_all.20 = f32[256,1,384]{2,1,0:T(1,128)S(1)} all-to-all(f32[256,1,384]{2,1,0:T(1,128)S(1)} %copy.14), channel_id=1, replica_groups=mesh['y'=8,'xl'=2,'xh'=2,'z'=8,'c'=2] {'z','xh','xl','y'}, dimensions={0} | all-to-all | bytes 786432 | tf_op jit(solution)/shard_map/all_to_all | solution.py:554
  92.5 0.3 reduce_sum.11
  92.8 0.3 shard_map.133
  93.1 10.7 %all_to_all.21.received = f32[16,16,128]{2,1,0:T(8,128)S(1)} all-to-all(f32[16,16,128]{2,1,0:T(8,128)S(1)} %get-tuple-element.58), channel_id=1, replica_groups=mesh['y'=8,'xl'=2,'xh'=2,'z'=8,'c'=2] {'xl','y'}, dimensions={0} | all-to-all | bytes 262144 | tf_op jit(solution)/shard_map/all_to_all | solution.py:561
  103.8 13.0 %all_to_all.22 = f32[16,32,128]{2,1,0:T(8,128)S(1)} all-to-all(f32[16,32,128]{2,1,0:T(8,128)S(1)} %shard_map.134), channel_id=1, replica_groups=mesh['y'=8,'xl'=2,'xh'=2,'z'=8,'c'=2] {'xh','z'}, dimensions={0} | all-to-all | bytes 524288 | tf_op jit(solution)/shard_map/all_to_all | solution.py:568
  116.9 5.7 %all-gather.5 = f32[32,32,128]{2,1,0:T(8,128)S(1)} all-gather(f32[16,32,128]{2,1,0:T(8,128)S(1)} %all_to_all.22), channel_id=7, replica_groups=mesh['y'=8,'xl'=2,'xh'=2,'z'=8,'c'=2] {'c'}, dimensions={0}, use_global_device_ids=true | all-gather | bytes 786432 | tf_op jit(solution)/shard_map/all_gather | solution.py:569
  122.5 0.8 shard_map.135
  (16 shorter events, 0.1 us)
Async XLA Ops:
  9.8 5.9 %copy-start = (f32[8,16,128]{2,1,0:T(8,128)S(1)}, f32[8,16,128]{2,1,0:T(8,128)}, u32[]{:S(2)}) copy-start(f32[8,16,128]{2,1,0:T(8,128)} %tokens.7) | copy-start | bytes 196612
  9.8 5.9 %copy-start.1 = (f32[8,16,128]{2,1,0:T(8,128)S(1)}, f32[8,16,128]{2,1,0:T(8,128)}, u32[]{:S(2)}) copy-start(f32[8,16,128]{2,1,0:T(8,128)} %grad.7) | copy-start | bytes 196612
  9.9 5.9 %copy-start.6 = (f32[3,3,128]{2,1,0:T(4,128)S(1)}, f32[3,3,128]{2,1,0:T(4,128)}, u32[]{:S(2)}) copy-start(f32[3,3,128]{2,1,0:T(4,128)} %weight.1) | copy-start | bytes 13828
  23.1 18.5 %copy-start.2 = (f32[128,128]{1,0:T(8,128)S(1)}, f32[128,128]{1,0:T(8,128)}, u32[]{:S(2)}) copy-start(f32[128,128]{1,0:T(8,128)} %w_query.3) | copy-start | bytes 196612
  23.1 18.5 %copy-start.3 = (f32[128,128]{1,0:T(8,128)S(1)}, f32[128,128]{1,0:T(8,128)}, u32[]{:S(2)}) copy-start(f32[128,128]{1,0:T(8,128)} %w_key.3) | copy-start | bytes 196612
  23.1 18.5 %copy-start.4 = (f32[128,128]{1,0:T(8,128)S(1)}, f32[128,128]{1,0:T(8,128)}, u32[]{:S(2)}) copy-start(f32[128,128]{1,0:T(8,128)} %w_value.3) | copy-start | bytes 196612
  23.1 18.5 %copy-start.5 = (f32[128,128]{1,0:T(8,128)S(1)}, f32[128,128]{1,0:T(8,128)}, u32[]{:S(2)}) copy-start(f32[128,128]{1,0:T(8,128)} %w_out.3) | copy-start | bytes 196612
  23.1 33.5 %all-to-all-start = ((f32[256,2,128]{2,1,0:T(2,128)}), f32[256,2,128]{2,1,0:T(2,128)S(1)}, u32[]{:S(2)}, u32[]{:S(2)}) async-start(f32[256,2,128]{2,1,0:T(2,128)} %bitcast.4), calls=%async_computation | async-start | bytes 524288 | tf_op jit(solution)/shard_map/all_to_all | solution.py:528

commit v9 on v8

--- a/solution.py
+++ b/solution.py
@@ -13,7 +13,7 @@
 COL = ("xh", "z", "c")
 CHIP_COL = ("xh", "z")
 ROW_GROUP = ("xl", "y")
-CHIPS = ("z", "xh") + ROW_GROUP
+CHIPS = CHIP_COL + ROW_GROUP
 ROWS, COLS, CHANNELS = 8, 16, 128
 CELLS, WIN_ROWS = 2, 4
 COUNT = ROWS * COLS
@@ -60,14 +60,14 @@
     return jax.ShapeDtypeStruct(shape, jnp.float32)
 
 
-def call(kernel, outs, *args, scratch=(), flops=1 << 20):
+def call(kernel, outs, *args, scratch=(), flops=1 << 20, copied=0, sems=()):
     in_vmem = pl.BlockSpec(memory_space=pltpu.VMEM)
     return pl.pallas_call(
         kernel,
         out_shape=outs,
         in_specs=[in_vmem] * len(args),
-        out_specs=[in_vmem] * len(outs),
-        scratch_shapes=[pltpu.VMEM(shape, jnp.float32) for shape in scratch],
+        out_specs=[pl.BlockSpec(memory_space=pl.ANY)] * copied + [in_vmem] * (len(outs) - copied),
+        scratch_shapes=[pltpu.VMEM(shape, jnp.float32) for shape in scratch] + list(sems),
         compiler_params=pltpu.CompilerParams(vmem_limit_bytes=48 << 20),
         cost_estimate=pl.CostEstimate(flops=flops, bytes_accessed=flops, transcendentals=0),
     )(*args)
@@ -170,7 +170,7 @@
 def mix_kernel(
     last_col, tokens, grad, above, below, beside, beyond, weight,
     message, pooled_out, padded, mixed_out, normed_out, inv_out, grad_out,
-    normed_ext, inv_ext, mixed_ext, before, after, rows,
+    normed_ext, inv_ext, mixed_ext, before, after, rows, tiles, sem,
 ):
     col = here()[1]
     even = col % 2 == 0
@@ -202,8 +202,10 @@
         pooled_out[CELLS + cell : CELLS + cell + 1] = jnp.broadcast_to(pooled_inv, pooled_n.shape)
     for k in range(8):
         rows[k : k + 1] = pooled_out[k % CELLS : k % CELLS + 1]
-    tiles = jnp.broadcast_to(rows[...][None], (message.shape[0] // 8, 8, CHANNELS))
-    message[...] = tiles.reshape(message.shape)
+    filled = jnp.broadcast_to(rows[...][None], (message.shape[0] // 8, 8, CHANNELS))
+    tiles[...] = filled.reshape(message.shape)
+    copy = pltpu.make_async_copy(tiles, message, sem)
+    copy.start()
     mixed_out[...] = mixed_ext[1 : 1 + ROWS, 1 : 1 + COLS]
     for ext, out in ((normed_ext, normed_out), (inv_ext, inv_out)):
         out[0:COUNT] = ext[1 : 1 + ROWS, 1 : 1 + COLS].reshape(COUNT, CHANNELS)
@@ -225,6 +227,7 @@
     grad_out[left : left + ROWS] = before[low + 1 : high]
     grad_out[left + ROWS : left + 2 * ROWS] = after[low + 1 : high]
     grad_out[COUNT + USED :] = jnp.zeros((RING - USED, CHANNELS), jnp.float32)
+    copy.wait()
 
 
 def top_half():
@@ -309,9 +312,9 @@
 
     d_scores = probs * (d_probs - jnp.sum(d_probs * probs, 0, keepdims=True))
     d0, d1 = pieces(d_scores, 2)
-    d_query_keys = by_keys(d0, d1)
     p0, p1 = pieces(probs[:, :wide], 2)
-    att_keys = by_keys(p0, p1)
+    keyed = by_keys(jnp.concatenate([d0, p0], 1), jnp.concatenate([d1, p1], 1))
+    d_query_keys, att_keys = keyed[:, : d0.shape[1]], keyed[:, d0.shape[1] :]
     d0, d1 = d0[:, :wide], d1[:, :wide]
     large = jnp.concatenate([q0[:, :wide], v0[:, :wide]], 1)
     small = jnp.concatenate([q1[:, :wide], v1[:, :wide]], 1)
@@ -469,10 +472,8 @@
         g_conv[k // 3, k % 3 : k % 3 + 1] = conv[k : k + 1]
     blocks = ((g_query, root), (g_key, 1.0 / POOL), (g_value, 1.0 / POOL), (g_out, root))
     for k in range(cores * lines):
-        line = k % lines
-        place_of = k - line + line % (lines // 2) * 2 + line // (lines // 2)
-        out, factor = blocks[place_of * row_count // CHANNELS]
-        at = place_of * row_count % CHANNELS
+        out, factor = blocks[k * row_count // CHANNELS]
+        at = k * row_count % CHANNELS
         out[at : at + row_count] = near[k // lines, k % lines, 0:row_count] * factor
 
 
@@ -512,7 +513,7 @@
     message, pooled, padded, mixed, normed, inv_std, grad = call(
         functools.partial(mix_kernel, col_count - 1),
         [
-            pltpu.VMEM((chips * CELLS, CHANNELS), jnp.float32),
+            f32(chips * CELLS, CHANNELS),
             f32(2 * CELLS, CHANNELS),
             f32(ROWS + 4, 24, CHANNELS),
             f32(*tile),
@@ -521,7 +522,8 @@
             f32(*all_tokens),
         ],
         tokens, cotangent, above, below, beside, beyond, taps,
-        scratch=[(ROWS + 2, 24, CHANNELS)] * 3 + [(SIDE, CHANNELS)] * 2 + [(8, CHANNELS)],
+        scratch=[(ROWS + 2, 24, CHANNELS)] * 3 + [(SIDE, CHANNELS)] * 2 + [(8, CHANNELS), (chips * CELLS, CHANNELS)],
+        copied=1, sems=[pltpu.SemaphoreType.DMA],
     )
 
     message = message.reshape(chips, CELLS, CHANNELS)

time: 124 us -> 124 us (level)
  no operation moved by 1% of the time
where the time goes in v9:
time: 124 us; the launch traced here: 123 us
  blocking collectives  81.6 us (66%)
  starting transfers between devices  18.5 us (15%)
  waiting for transfers between devices  13.9 us (11%)
  Pallas kernels  7.71 us (6%)
    all_to_all x1, blocking collectives, body(): sums = jnp.sum(lax.all_to_all(sums, CHIPS, 0, 0, tiled=True), 0)  26.5 us
    all_gather x4, blocking collectives, pair_gather(): return lax.all_gather(value, axis, axis_index_groups=groups, axis=0)  20.3 us
    all_to_all x1, starting transfers between devices, body(): message = lax.all_to_all(message, CHIPS, 0, 0, tiled=True)  18.5 us
    all_to_all x1, waiting for transfers between devices, body(): message = lax.all_to_all(message, CHIPS, 0, 0, tiled=True)  13.9 us
    all_to_all x1, blocking collectives, body(): message = lax.all_to_all(message, CHIP_COL, 0, 0, tiled=True)  13.2 us
    all_to_all x1, blocking collectives, body(): message = lax.all_to_all(message, ROW_GROUP, 0, 0, tiled=True)  10.1 us
    pallas_call x9, Pallas kernels, call(): pl.pallas_call(kernel, out_shape=outs, in_specs=[in_vmem] * len(args), ou...  6.9 us
    all_gather x1, blocking collectives, body(): near = lax.all_gather(message, 'c', axis=0)  5.69 us
  transfers between devices with their start and end apart: 1, of which 1 were waited for; matrix products, arithmetic and copies ran while one was open for 0% of the time, Pallas kernels for 1%

profile of v9, /device:TPU:1, one launch (start us, length us, event | category | flops | bytes accessed | tf_op | source)
XLA Modules:
  0.0 123.3 jit_solution(17540434951373801366)
XLA Ops:
  0.6 0.8 shard_map.126
  1.4 8.4 %all-gather = f32[6,16,128]{2,1,0:T(8,128)S(1)} all-gather(f32[3,16,128]{2,1,0:T(8,128)S(1)} %get-tuple-element.36), channel_id=2, replica_groups=mesh['y'=8,'xl'=2,'xh'=2,'z'=8,'c'=2] {'c'}, dimensions={0}, use_global_device_ids=true | all-gather | bytes 73728 | tf_op jit(solution)/shard_map/all_gather | solution.py:93
  9.8 0.0 copy-start.1
  9.9 0.0 copy-start.6
  9.9 5.9 %all-gather.1 = f32[4,3,16,128]{3,2,1,0:T(8,128)S(1)} all-gather(f32[2,3,16,128]{3,2,1,0:T(8,128)S(1)} %shard_map.127), channel_id=3, replica_groups={{0,32},{64,96},{128,160},{192,224},{256,288},{320,352},{384,416},{448,4..., dimensions={0}, use_global_device_ids=true | all-gather | bytes 147456 | tf_op jit(solution)/shard_map/all_gather | solution.py:93
  15.8 1.9 %all-gather.2 = f32[240,128]{1,0:T(8,128)S(1)} all-gather(f32[120,128]{1,0:T(8,128)S(1)} %get-tuple-element.37), channel_id=4, replica_groups=mesh['y'=8,'xl'=2,'xh'=2,'z'=8,'c'=2] {'c'}, dimensions={0}, use_global_device_ids=true | all-gather | bytes 184320 | tf_op jit(solution)/shard_map/all_gather | solution.py:93
  17.7 4.2 %all-gather.3 = f32[80,128]{1,0:T(8,128)S(1)} all-gather(f32[40,128]{1,0:T(8,128)S(1)} %get-tuple-element.41), channel_id=5, replica_groups={{1,2},{3,4},{5,6},{7,8},{9,10},{11,12},{13,14},{15,16},{17,18},{19,20},..., dimensions={0}, use_global_device_ids=true | all-gather | bytes 61440 | tf_op jit(solution)/shard_map/all_gather | solution.py:93
  21.9 1.2 shard_map.130
  23.1 0.0 copy-start.3
  23.1 18.5 %all-to-all-start = ((f32[256,2,128]{2,1,0:T(2,128)}), f32[256,2,128]{2,1,0:T(2,128)S(1)}, u32[]{:S(2)}, u32[]{:S(2)}) async-start(f32[256,2,128]{2,1,0:T(2,128)} %bitcast.4), calls=%async_computation | async-start | bytes 524288 | tf_op jit(solution)/shard_map/all_to_all | solution.py:530
  41.7 1.0 shard_map.131
  42.7 13.9 %all-to-all-done = f32[256,2,128]{2,1,0:T(2,128)S(1)} async-done(((f32[256,2,128]{2,1,0:T(2,128)}), f32[256,2,128]{2,1,0:T(2,128)S(1)}, u32[]{:S(2)}, u32[]{:S(2)}) %all-to-all-start) | async-done | bytes 262176 | tf_op jit(solution)/shard_map/all_to_all | solution.py:530
  56.6 3.4 %all_gather.47 = f32[512,2,128]{2,1,0:T(2,128)S(1)} all-gather(f32[256,2,128]{2,1,0:T(2,128)S(1)} %all-to-all-done), channel_id=1, replica_groups=mesh['y'=8,'xl'=2,'xh'=2,'z'=8,'c'=2] {'c'}, dimensions={0}, use_global_device_ids=true | all-gather | bytes 786432 | tf_op jit(solution)/shard_map/all_gather | solution.py:531
  60.0 3.5 %shard_map.132 = (f32[256,384]{1,0:T(8,128)S(1)}, f32[256,384]{1,0:T(8,128)S(1)}, f32[128,128]{1,0:T(8,128)S(1)}, f32[128,128]{1,0:T(8,128)S(1)}, f32[64,128]{1,0:T(8,128)S(1)}) custom-call(f32[1024,128]{1,0:T(8,128)S(1)} %bitcast.10, f32[128,384]{1,0:T(8,128)S(1)} %get-tuple-element.46.to_keys, f32[128,384]{1,0:T(8,128)S(1)} %get-tuple-element.47.to_values, ...), custom_call_target="tpu_custom_call" | custom-call | flops 2147483648 | bytes 2147483648 | tf_op jit(solution)/shard_map/pallas_call | solution.py:65
  63.5 2.4 %all-gather.4 = f32[512,384]{1,0:T(8,128)S(1)} all-gather(f32[256,384]{1,0:T(8,128)S(1)} %get-tuple-element.53), channel_id=6, replica_groups=mesh['y'=8,'xl'=2,'xh'=2,'z'=8,'c'=2] {'c'}, dimensions={0}, use_global_device_ids=true | all-gather | bytes 1179648 | tf_op jit(solution)/shard_map/all_gather | solution.py:553
  65.9 0.1 fusion.1
  66.0 0.4 copy.14
  66.4 26.5 %all_to_all.20 = f32[256,1,384]{2,1,0:T(1,128)S(1)} all-to-all(f32[256,1,384]{2,1,0:T(1,128)S(1)} %copy.14), channel_id=1, replica_groups=mesh['y'=8,'xl'=2,'xh'=2,'z'=8,'c'=2] {'xh','z','xl','y'}, dimensions={0} | all-to-all | bytes 786432 | tf_op jit(solution)/shard_map/all_to_all | solution.py:556
  92.9 0.3 reduce_sum.11
  93.2 0.3 shard_map.133
  93.5 10.1 %all_to_all.21.received = f32[16,16,128]{2,1,0:T(8,128)S(1)} all-to-all(f32[16,16,128]{2,1,0:T(8,128)S(1)} %get-tuple-element.58), channel_id=1, replica_groups=mesh['y'=8,'xl'=2,'xh'=2,'z'=8,'c'=2] {'xl','y'}, dimensions={0} | all-to-all | bytes 262144 | tf_op jit(solution)/shard_map/all_to_all | solution.py:563
  103.6 13.2 %all_to_all.22 = f32[16,32,128]{2,1,0:T(8,128)S(1)} all-to-all(f32[16,32,128]{2,1,0:T(8,128)S(1)} %shard_map.134), channel_id=1, replica_groups=mesh['y'=8,'xl'=2,'xh'=2,'z'=8,'c'=2] {'xh','z'}, dimensions={0} | all-to-all | bytes 524288 | tf_op jit(solution)/shard_map/all_to_all | solution.py:570
  116.8 5.7 %all-gather.5 = f32[32,32,128]{2,1,0:T(8,128)S(1)} all-gather(f32[16,32,128]{2,1,0:T(8,128)S(1)} %all_to_all.22), channel_id=7, replica_groups=mesh['y'=8,'xl'=2,'xh'=2,'z'=8,'c'=2] {'c'}, dimensions={0}, use_global_device_ids=true | all-gather | bytes 786432 | tf_op jit(solution)/shard_map/all_gather | solution.py:571
  122.5 0.8 shard_map.135
  (16 shorter events, 0.1 us)
Async XLA Ops:
  9.8 5.9 %copy-start = (f32[8,16,128]{2,1,0:T(8,128)S(1)}, f32[8,16,128]{2,1,0:T(8,128)}, u32[]{:S(2)}) copy-start(f32[8,16,128]{2,1,0:T(8,128)} %tokens.7) | copy-start | bytes 196612
  9.8 5.9 %copy-start.1 = (f32[8,16,128]{2,1,0:T(8,128)S(1)}, f32[8,16,128]{2,1,0:T(8,128)}, u32[]{:S(2)}) copy-start(f32[8,16,128]{2,1,0:T(8,128)} %grad.7) | copy-start | bytes 196612
  9.9 5.9 %copy-start.6 = (f32[3,3,128]{2,1,0:T(4,128)S(1)}, f32[3,3,128]{2,1,0:T(4,128)}, u32[]{:S(2)}) copy-start(f32[3,3,128]{2,1,0:T(4,128)} %weight.1) | copy-start | bytes 13828
  23.1 18.5 %copy-start.2 = (f32[128,128]{1,0:T(8,128)S(1)}, f32[128,128]{1,0:T(8,128)}, u32[]{:S(2)}) copy-start(f32[128,128]{1,0:T(8,128)} %w_query.3) | copy-start | bytes 196612
  23.1 18.5 %copy-start.3 = (f32[128,128]{1,0:T(8,128)S(1)}, f32[128,128]{1,0:T(8,128)}, u32[]{:S(2)}) copy-start(f32[128,128]{1,0:T(8,128)} %w_key.3) | copy-start | bytes 196612
  23.1 18.5 %copy-start.4 = (f32[128,128]{1,0:T(8,128)S(1)}, f32[128,128]{1,0:T(8,128)}, u32[]{:S(2)}) copy-start(f32[128,128]{1,0:T(8,128)} %w_value.3) | copy-start | bytes 196612
  23.1 18.5 %copy-start.5 = (f32[128,128]{1,0:T(8,128)S(1)}, f32[128,128]{1,0:T(8,128)}, u32[]{:S(2)}) copy-start(f32[128,128]{1,0:T(8,128)} %w_out.3) | copy-start | bytes 196612
  23.1 33.5 %all-to-all-start = ((f32[256,2,128]{2,1,0:T(2,128)}), f32[256,2,128]{2,1,0:T(2,128)S(1)}, u32[]{:S(2)}, u32[]{:S(2)}) async-start(f32[256,2,128]{2,1,0:T(2,128)} %bitcast.4), calls=%async_computation | async-start | bytes 524288 | tf_op jit(solution)/shard_map/all_to_all | solution.py:530
